TPU v7x, 32 devices: a whole 2x2x4 slice. The times are simulated.
32 devices in a mesh: seq: 8 (over y, x, core), grp: 4 (over z).
Axes of the slice: x: 2, y: 2, z: 4, core: 2. Of those that a mesh axis runs over, the one named last changes fastest.
Arguments:
- tokens: bfloat16 [8, 2048, 1024], P('grp', 'seq'), may hold values from -6 to 6
- cotangent: bfloat16 [8, 2048, 1024], P('grp', 'seq'), may hold values from -6 to 6
- norm_gain: float32 [1024], replicated, may hold values from 0.5 to 1.5
- in_weight: bfloat16 [1024, 4096], replicated, may hold values from -0.1875 to 0.1875
- conv_weight: float32 [4, 2048], replicated, may hold values from -3 to 3
- conv_bias: float32 [2048], replicated, may hold values from -3 to 3
- select_weight: bfloat16 [2048, 96], replicated, may hold values from -0.125 to 0.125
- rate_weight: bfloat16 [64, 2048], replicated, may hold values from -0.75 to 0.75
- rate_bias: float32 [2048], replicated, may hold values from -5 to -2
- decay_log: float32 [2048, 16], replicated, may hold values from -9 to 2
- skip_gain: float32 [2048], replicated, may hold values from 0.5 to 1.5
- out_weight: bfloat16 [2048, 1024], replicated, may hold values from -0.375 to 0.375
Outputs:
- block_out: bfloat16 [8, 2048, 1024], P('grp', 'seq')
- tokens_grad: bfloat16 [8, 2048, 1024], P('grp', 'seq')
- norm_gain_grad: float32 [1024], P(('seq', 'grp'))
- in_weight_grad: float32 [1024, 4096], P(('seq', 'grp'))
- conv_weight_grad: float32 [4, 2048], P(None, ('seq', 'grp'))
- conv_bias_grad: float32 [2048], P(('seq', 'grp'))
- select_weight_grad: float32 [2048, 96], P(('seq', 'grp'))
- rate_weight_grad: float32 [64, 2048], P(None, ('seq', 'grp'))
- rate_bias_grad: float32 [2048], P(('seq', 'grp'))
- decay_log_grad: float32 [2048, 16], P(('seq', 'grp'))
- skip_gain_grad: float32 [2048], P(('seq', 'grp'))
- out_weight_grad: float32 [2048, 1024], P(('seq', 'grp'))
All inputs are finite; a program needn't handle non-finite values.
Results may differ from a plain program's by a relative error of at most 0.0083.
Values may be sent and summed in bfloat16 or wider, within the bound.
No kernel may reach another device: no remote copies, remote signals or barrier semaphores. Data moves between devices by JAX's collectives and lax.ppermute only.
A program may use at most 256 MiB of HBM per device.

v0:
```python
import functools
import math

import jax
import jax.numpy as jnp
from jax import lax
from jax.experimental import pallas as pl
from jax.experimental.pallas import tpu as pltpu
from jax.sharding import PartitionSpec as P

f32 = jnp.float32
bf16 = jnp.bfloat16
LOG2E = 1.4426950408889634
N = 16
T = 16
WIDTH = 512
NL = WIDTH // 128
VMEM = 60 * 2**20


def lane(l):
    return slice(l * 128, (l + 1) * 128)


def sigmoid(v):
    return 1.0 / (1.0 + jnp.exp(-v))


def joined(ref, rows):
    return jnp.concatenate([ref[l, rows, :] for l in range(NL)], axis=1)


def steps_of(rows):
    return pl.ds(pl.multiple_of(rows, T), T)


def state_of(t):
    return pl.ds(pl.multiple_of(t * N, N), N)


def rows_dot(left, right):
    return lax.dot_general(left, right, (((1,), (1,)), ((), ())), preferred_element_type=f32)


def state_end_kernel(proj_ref, rw_ref, rb_ref, x_ref, a2_ref, bb_ref, he_ref, w_ref, dl_ref, u_ref, *, nseq, length):
    rows = nseq * length

    def steps(i, _):
        r = pl.multiple_of(i * 64, 64)
        at = pl.ds(r, 64)
        low = proj_ref[at, : rw_ref.shape[0]].astype(bf16)
        pre = jnp.dot(low, rw_ref[...], preferred_element_type=f32) + rb_ref[...]
        d = jnp.maximum(pre, 0.0) + jnp.log(1.0 + jnp.exp(-jnp.abs(pre)))
        for l in range(NL):
            dl_ref[l, at, :] = d[:, lane(l)]
            u_ref[l, at, :] = d[:, lane(l)] * x_ref[l, at, :].astype(f32)
        return 0

    lax.fori_loop(0, rows // 64, steps, 0)
    for s in range(nseq):
        for l in range(NL):
            w_ref[s : s + 1, lane(l)] = jnp.sum(dl_ref[l, s * length : (s + 1) * length, :], axis=0, keepdims=True)

    def step(c, h):
        h = [list(v) for v in h]
        for k in range(T):
            for s in range(nseq):
                t = s * length + c * T + k
                bt = bb_ref[t]
                for l in range(NL):
                    f = jnp.exp2(dl_ref[l, pl.ds(t, 1), :] * a2_ref[:, lane(l)])
                    h[s][l] = f * h[s][l] + u_ref[l, pl.ds(t, 1), :] * bt
        return tuple(tuple(v) for v in h)

    z = jnp.zeros((N, 128), f32)
    h = lax.fori_loop(0, length // T, step, ((z,) * NL,) * nseq)
    for s in range(nseq):
        for l in range(NL):
            he_ref[s, :, lane(l)] = h[s][l]


def adjoint_end_kernel(dl_ref, g_ref, a2_ref, cb_ref, sb_ref, *, nseq, length):
    nch = length // T

    def step(m, lam):
        lam = [list(v) for v in lam]
        c = nch - 1 - m
        for k in reversed(range(T)):
            for s in range(nseq):
                t = s * length + c * T + k
                ct = cb_ref[t]
                for l in range(NL):
                    f = jnp.exp2(dl_ref[l, pl.ds(t, 1), :] * a2_ref[:, lane(l)])
                    lam[s][l] = f * (lam[s][l] + g_ref[l, pl.ds(t, 1), :] * ct)
        return tuple(tuple(v) for v in lam)

    z = jnp.zeros((N, 128), f32)
    lam = lax.fori_loop(0, nch, step, ((z,) * NL,) * nseq)
    for s in range(nseq):
        for l in range(NL):
            sb_ref[s, :, lane(l)] = lam[s][l]


def forward_kernel(
    dl_ref, u_ref, g_ref, ga_ref, gs_ref, x_ref, skip_ref, bb_ref, lc_ref, a2_ref, hin_ref,
    hb_ref, gated_ref, ggr_ref, outg_ref, sk_ref, *, nseq, length, unroll,
):
    nch = length // T
    skip = skip_ref[...]
    ones = jnp.ones((8, 128), bf16)

    @pl.when(pl.program_id(0) == 0)
    def _():
        outg_ref[...] = jnp.zeros_like(outg_ref)

    def chunk(c, h, acc):
        hbv, pov = {}, [[None] * T for _ in range(nseq)]
        for k in range(T):
            for s in range(nseq):
                t = s * length + c * T + k
                bt = bb_ref[t]
                po = None
                for l in range(NL):
                    g = jnp.broadcast_to(g_ref[l, pl.ds(t, 1), :], (N, 128)).astype(bf16)
                    f = jnp.exp2(dl_ref[l, pl.ds(t, 1), :] * a2_ref[:, lane(l)])
                    h[s][l] = f * h[s][l] + u_ref[l, pl.ds(t, 1), :] * bt
                    hb = h[s][l].astype(bf16)
                    hb_ref[state_of(t), lane(l)] = hb
                    hbv[k, s, l] = hb
                    po = hb * g if po is None else po + hb * g
                pov[s][k] = po
        lhs = jnp.concatenate([lc_ref[steps_of(s * length + c * T), :] for s in range(nseq)], axis=0)
        parts = []
        for l in range(0, NL, 2):
            rhs = jnp.concatenate(
                [
                    jnp.concatenate([hbv[k, s, l], hbv[k, s, l + 1]], axis=1)
                    for k in range(T) for s in range(nseq)
                ],
                axis=0,
            )
            parts.append(jnp.dot(lhs, rhs, preferred_element_type=f32))
        sc_all = jnp.concatenate(parts, axis=1)
        for s in range(nseq):
            og = rows_dot(ones, jnp.concatenate(pov[s], axis=0))
            outg_ref[pl.ds(s * nch + c, 1), :] += og[:1]
            at = steps_of(s * length + c * T)
            x = joined(x_ref, at).astype(f32)
            mo = sc_all[s * T : (s + 1) * T] + skip * x
            gated_ref[at, :] = (mo * joined(ga_ref, at)).astype(bf16)
            ggr_ref[at, :] = (mo * joined(gs_ref, at)).astype(bf16)
            acc = acc + joined(g_ref, at) * x
        return acc

    def step(i, carry):
        h, acc = carry
        h = [list(v) for v in h]
        for p in range(unroll):
            acc = chunk(i * unroll + p, h, acc)
        return tuple(tuple(v) for v in h), acc

    h0 = tuple(tuple(hin_ref[s, :, lane(l)] for l in range(NL)) for s in range(nseq))
    _, acc = lax.fori_loop(0, nch // unroll, step, (h0, jnp.zeros((T, WIDTH), f32)))
    sk_ref[...] = jnp.broadcast_to(jnp.sum(acc, axis=0, keepdims=True), sk_ref.shape)


def backward_kernel(
    dl_ref, u_ref, g_ref, x_ref, skip_ref, cb_ref, lb_ref, ls_ref, a_ref, a2_ref, lin_ref, hin_ref, hb_ref,
    rl_ref, cp_ref, ing_ref, dlog_ref, rb_ref, *, nseq, length, unroll,
):
    nch = length // T
    abf = a_ref[...].astype(bf16)
    skip = skip_ref[...]
    ones = jnp.ones((8, 128), bf16)

    @pl.when(pl.program_id(0) == 0)
    def _():
        ing_ref[...] = jnp.zeros_like(ing_ref)

    def chunk(c, lam, dlog, rb):
        pov = [[None] * T for _ in range(nseq)]
        dacc = [None] * NL
        vals = {}
        for k in reversed(range(T)):
            for s in range(nseq):
                t = s * length + c * T + k
                ct = cb_ref[t]
                po = None
                for l in range(NL):
                    d = jnp.broadcast_to(dl_ref[l, pl.ds(t, 1), :], (N, 128))
                    u = jnp.broadcast_to(u_ref[l, pl.ds(t, 1), :], (N, 128)).astype(bf16)
                    a = g_ref[l, pl.ds(t, 1), :] * ct + lam[s][l]
                    lam[s][l] = jnp.exp2(d * a2_ref[:, lane(l)]) * a
                    if k > 0:
                        hp = hb_ref[state_of(t - 1), lane(l)]
                    else:
                        hp = hb_ref[state_of(jnp.maximum(t - 1, 0)), lane(l)]
                        hp = jnp.where(c == 0, hin_ref[s, :, lane(l)].astype(bf16), hp)
                    q = lam[s][l].astype(bf16) * hp * abf[:, lane(l)]
                    ab = a.astype(bf16)
                    qd = q * d.astype(bf16)
                    vals[k, s, l] = (ab, q)
                    dacc[l] = qd if dacc[l] is None else dacc[l] + qd
                    po = ab * u if po is None else po + ab * u
                pov[s][k] = po
            if k % 8 == 0:
                for l in range(NL):
                    dlog[l] = dlog[l] + dacc[l].astype(f32)
                    dacc[l] = None
        lhs = jnp.concatenate(
            [lb_ref[steps_of(s * length + c * T), :] for s in range(nseq)] + [ls_ref[...]], axis=0
        )
        parts = []
        for l in range(0, NL, 2):
            rhs = jnp.concatenate(
                [
                    jnp.concatenate([vals[k, s, l][y], vals[k, s, l + 1][y]], axis=1)
                    for k in reversed(range(T)) for s in range(nseq) for y in range(2)
                ],
                axis=0,
            )
            parts.append(jnp.dot(lhs, rhs, preferred_element_type=f32))
        both = jnp.concatenate(parts, axis=1)
        for s in range(nseq):
            w = both[s * T : (s + 1) * T]
            qs = both[(nseq + s) * T : (nseq + s + 1) * T]
            ig = rows_dot(ones, jnp.concatenate(pov[s], axis=0))
            ing_ref[pl.ds(s * nch + c, 1), :] += ig[:1]
            at = steps_of(s * length + c * T)
            d = joined(dl_ref, at)
            rg = (qs + w * joined(x_ref, at).astype(f32)) * (1.0 - jnp.exp(-d))
            rb = rb + rg
            rl_ref[at, :] = rg.astype(bf16)
            cp_ref[at, :] = w * d + skip * joined(g_ref, at)
        return rb

    def step(m, carry):
        lam, dlog, rb = carry
        lam = [list(v) for v in lam]
        dlog = list(dlog)
        for p in range(unroll):
            rb = chunk(nch - 1 - (m * unroll + p), lam, dlog, rb)
        return tuple(tuple(v) for v in lam), tuple(dlog), rb

    l0 = tuple(tuple(lin_ref[s, :, lane(l)] for l in range(NL)) for s in range(nseq))
    z = jnp.zeros((N, 128), f32)
    _, dlog, rb = lax.fori_loop(0, nch // unroll, step, (l0, (z,) * NL, jnp.zeros((T, WIDTH), f32)))
    for l in range(NL):
        dlog_ref[:, lane(l)] = dlog[l]
    rb_ref[...] = jnp.broadcast_to(jnp.sum(rb, axis=0, keepdims=True), rb_ref.shape)


def block_of(rows):
    return pl.BlockSpec((rows, WIDTH), lambda j: (0, j))


def tiles_of(rows):
    return pl.BlockSpec((NL, rows, 128), lambda j: (j, 0, 0))


def states_of(nseq):
    return pl.BlockSpec((nseq, N, WIDTH), lambda j: (0, 0, j))


def whole(a):
    return pl.BlockSpec(a.shape, lambda j: (0,) * a.ndim, pipeline_mode=pl.Buffered(1))


def kernel_call(body, name, channels, operands, specs, out_specs, outs, flops, scratch=(), **options):
    moved = sum(a.size * a.dtype.itemsize for a in operands) + sum(
        math.prod(o.shape) * o.dtype.itemsize for o in outs
    )
    return pl.pallas_call(
        functools.partial(body, **options),
        grid=(channels // WIDTH,),
        in_specs=specs,
        out_specs=out_specs,
        out_shape=outs,
        scratch_shapes=scratch,
        compiler_params=pltpu.CompilerParams(vmem_limit_bytes=VMEM, dimension_semantics=("arbitrary",)),
        cost_estimate=pl.CostEstimate(flops=flops, bytes_accessed=moved, transcendentals=0),
        name=name,
    )(*operands)


def spread(values, nseq, length, kinds, reverse):
    rows = nseq * length
    width = T * nseq * kinds * N
    column = jnp.arange(width)
    pick = (column[None, :] % N == jnp.arange(N)[:, None]).astype(bf16)
    wide = jnp.dot(values.astype(bf16), pick, preferred_element_type=f32)
    return jnp.where(own_column(rows, length, width, nseq, kinds, 0, reverse), wide, 0.0).astype(bf16)


def own_column(rows, length, width, nseq, kinds, kind, reverse):
    row = lax.broadcasted_iota(jnp.int32, (rows, width), 0)
    column = lax.broadcasted_iota(jnp.int32, (rows, width), 1)
    step = column // (nseq * kinds * N)
    if reverse:
        step = T - 1 - step
    return (
        (step == row % T)
        & ((column // (kinds * N)) % nseq == row // length)
        & ((column // N) % kinds == kind)
    )


def state_end(proj, rate_weight, rate_bias, x, a2, bb, nseq, length):
    tiles, rows, _ = x.shape
    ch = tiles * 128
    o = jax.ShapeDtypeStruct
    return kernel_call(
        state_end_kernel, "state_end", ch,
        (proj, rate_weight, rate_bias, x, a2, bb),
        [whole(proj), block_of(rate_weight.shape[0]), block_of(1), tiles_of(rows), block_of(N), whole(bb)],
        [states_of(nseq), block_of(nseq), tiles_of(rows), tiles_of(rows)],
        (o((nseq, N, ch), f32), o((nseq, ch), f32), o(x.shape, f32), o(x.shape, f32)),
        2 * 10**10, nseq=nseq, length=length,
    )


def adjoint_end(dl, g, a2, cb, nseq, length):
    tiles, rows, _ = dl.shape
    ch = tiles * 128
    return kernel_call(
        adjoint_end_kernel, "adjoint_end", ch,
        (dl, g, a2, cb),
        [tiles_of(rows), tiles_of(rows), block_of(N), whole(cb)],
        [states_of(nseq)],
        (jax.ShapeDtypeStruct((nseq, N, ch), f32),),
        2 * 10**10, nseq=nseq, length=length,
    )[0]


def forward(dl, u, g, ga, gs, x, skip, bb, lc, a2, hin, nseq, length, unroll=1):
    tiles, rows, _ = dl.shape
    ch = tiles * 128
    o = jax.ShapeDtypeStruct
    t = tiles_of(rows)
    return kernel_call(
        forward_kernel, "forward", ch,
        (dl, u, g, ga, gs, x, skip, bb, lc, a2, hin),
        [t, t, t, t, t, t, block_of(1), whole(bb), whole(lc), block_of(N), states_of(nseq)],
        [block_of(rows * N), block_of(rows), block_of(rows), pl.BlockSpec((rows // T, T * N), lambda j: (0, 0)), block_of(8)],
        (o((rows * N, ch), bf16), o((rows, ch), bf16), o((rows, ch), bf16), o((rows // T, T * N), f32), o((8, ch), f32)),
        3 * 10**10, nseq=nseq, length=length, unroll=unroll,
    )


def backward(dl, u, g, x, skip, cb, lb, ls, a, a2, lin, hin, hb, nseq, length, unroll=1):
    tiles, rows, _ = dl.shape
    ch = tiles * 128
    o = jax.ShapeDtypeStruct
    t = tiles_of(rows)
    st = states_of(nseq)
    return kernel_call(
        backward_kernel, "backward", ch,
        (dl, u, g, x, skip, cb, lb, ls, a, a2, lin, hin, hb),
        [t, t, t, t, block_of(1), whole(cb), whole(lb), whole(ls), block_of(N), block_of(N), st, st, block_of(rows * N)],
        [block_of(rows), block_of(rows), pl.BlockSpec((rows // T, T * N), lambda j: (0, 0)), block_of(N), block_of(8)],
        (o((rows, ch), bf16), o((rows, ch), f32), o((rows // T, T * N), f32), o((N, ch), f32), o((8, ch), f32)),
        5 * 10**10, nseq=nseq, length=length, unroll=unroll,
    )


epsilon = 1e-05
ROWS = 64
PAD = 8


def normalized(tokens, gain):
    wide = tokens.astype(f32)
    return (wide * lax.rsqrt(jnp.mean(wide * wide, axis=1, keepdims=True) + epsilon) * gain).astype(bf16)


def gate_kernel(tok_ref, gain_ref, cot_ref, wg_ref, ow_ref, normed_ref, turned_ref, g_ref, ga_ref, gs_ref, gh_ref, gg_ref):
    rows = tok_ref.shape[0]

    @pl.when(pl.program_id(0) == 0)
    def _():
        def norm(i, _):
            at = pl.ds(pl.multiple_of(i * ROWS, ROWS), ROWS)
            normed_ref[at, :] = normalized(tok_ref[at, :], gain_ref[...])
            return 0

        lax.fori_loop(0, rows // ROWS, norm, 0)
        turned_ref[...] = normed_ref[...].T

    gh_ref[...] = jnp.dot(normed_ref[...], wg_ref[...], preferred_element_type=f32)
    gg_ref[...] = rows_dot(cot_ref[...], ow_ref[...])

    def mix(i, _):
        at = pl.ds(pl.multiple_of(i * ROWS, ROWS), ROWS)
        gh = gh_ref[at, :]
        gg = gg_ref[at, :]
        sg = sigmoid(gh)
        ga = gh * sg
        gs = gg * (sg * (1.0 + gh * (1.0 - sg)))
        g = gg * ga
        for l in range(NL):
            g_ref[l, at, :] = g[:, lane(l)]
            ga_ref[l, at, :] = ga[:, lane(l)]
            gs_ref[l, at, :] = gs[:, lane(l)]
        return 0

    lax.fori_loop(0, rows // ROWS, mix, 0)


def gate_side(tokens, gain, cotangent, in_weight, out_weight):
    rows, model = tokens.shape
    inner = out_weight.shape[0]
    first = inner // WIDTH
    tiles = jax.ShapeDtypeStruct((inner // 128, rows, 128), f32)
    return kernel_call(
        gate_kernel, "gate_side", inner,
        (tokens, gain, cotangent, in_weight, out_weight),
        [
            whole(tokens), whole(gain), whole(cotangent),
            pl.BlockSpec((model, WIDTH), lambda j: (0, j + first)),
            pl.BlockSpec((WIDTH, model), lambda j: (j, 0)),
        ],
        [pl.BlockSpec((rows, model), lambda j: (0, 0)), pl.BlockSpec((model, rows), lambda j: (0, 0))]
        + [tiles_of(rows)] * 3,
        (jax.ShapeDtypeStruct((rows, model), bf16), jax.ShapeDtypeStruct((model, rows), bf16), tiles, tiles, tiles),
        4 * rows * model * inner, scratch=[pltpu.VMEM((rows, WIDTH), f32)] * 2,
    )


def taps_of(ext, weight, first, rows):
    taps = weight.shape[0]
    return sum(weight[k : k + 1] * ext[first + k : first + k + rows] for k in range(taps))


def inner_kernel(
    normed_ref, halo_ref, gain_ref, wi_ref, cw_ref, cb_ref, sw_ref, inner_ref, before_ref, x_ref, proj_ref, ext_ref, flat_ref,
    *, nseq, length,
):
    part = jnp.dot(normed_ref[...], wi_ref[...], preferred_element_type=f32).astype(bf16)
    inner_ref[...] = part
    for s in range(nseq):
        ext_ref[s, PAD:, :] = part[s * length : (s + 1) * length].astype(f32)
    before = jnp.dot(
        normalized(halo_ref[...], gain_ref[...]), wi_ref[...], preferred_element_type=f32
    ).astype(bf16)
    before_ref[...] = before
    for s in range(nseq):
        ext_ref[s, :PAD, :] = before[s * PAD : (s + 1) * PAD].astype(f32)

    @pl.when(pl.program_id(0) == 0)
    def _():
        proj_ref[...] = jnp.zeros_like(proj_ref)

    taps = cw_ref.shape[0]
    for s in range(nseq):

        def mix(i, _):
            r = pl.multiple_of(i * ROWS, ROWS)
            at = pl.ds(pl.multiple_of(s * length + r, ROWS), ROWS)
            ext = ext_ref[s, pl.ds(r, ROWS + PAD), :]
            pre = taps_of(ext, cw_ref[...], PAD - taps + 1, ROWS) + cb_ref[...]
            x = (pre * sigmoid(pre)).astype(bf16)
            for l in range(NL):
                x_ref[l, at, :] = x[:, lane(l)]
            flat_ref[at, :] = x
            return 0

        lax.fori_loop(0, length // ROWS, mix, 0)
    proj_ref[...] += jnp.dot(flat_ref[...], sw_ref[...], preferred_element_type=f32)


def inner_side(normed, halo, gain, in_weight, conv_weight, conv_bias, select_weight, nseq, length):
    rows, model = normed.shape
    inner, picks = select_weight.shape
    o = jax.ShapeDtypeStruct
    operands = (normed, halo, gain, in_weight, conv_weight, conv_bias, select_weight)
    specs = [
        whole(normed), whole(halo), whole(gain), block_of(model), block_of(conv_weight.shape[0]), block_of(1),
        pl.BlockSpec((WIDTH, picks), lambda j: (j, 0)),
    ]
    return pl.pallas_call(
        functools.partial(inner_kernel, nseq=nseq, length=length),
        grid=(inner // WIDTH,),
        in_specs=specs,
        out_specs=[block_of(rows), block_of(halo.shape[0]), tiles_of(rows), pl.BlockSpec((rows, picks), lambda j: (0, 0))],
        out_shape=(
            o((rows, inner), bf16), o((halo.shape[0], inner), bf16), o((inner // 128, rows, 128), bf16), o((rows, picks), f32),
        ),
        scratch_shapes=[pltpu.VMEM((nseq, PAD + length, WIDTH), f32), pltpu.VMEM((rows, WIDTH), bf16)],
        compiler_params=pltpu.CompilerParams(vmem_limit_bytes=VMEM, dimension_semantics=("arbitrary",)),
        cost_estimate=pl.CostEstimate(flops=2 * rows * model * inner, bytes_accessed=14 * 2**20, transcendentals=0),
        name="inner_side",
    )(*operands)


def input_grad_kernel(
    place_ref, cp_ref, inner_ref, before_ref, x_ref, pg_ref, sw_ref, cw_ref, cb_ref, turned_ref, halo_ref, gain_ref,
    rl_ref, rank_ref, dlog_ref, rb_ref, sk_ref,
    packed_ref, igr_ref, tail_ref, head_ref, ext_ref, pre_ref, back_ref, vec_ref, *, nseq, length, part,
):
    taps = cw_ref.shape[0]
    j = pl.program_id(0)
    back_ref[...] = cp_ref[...] + rows_dot(pg_ref[...], sw_ref[...])
    vec_ref[...] = jnp.zeros_like(vec_ref)
    for s in range(nseq):
        ext_ref[s, :PAD, :] = before_ref[s * PAD : (s + 1) * PAD, :].astype(f32)
        pre_ref[s, :PAD, :] = jnp.zeros((PAD, WIDTH), f32)
        pre_ref[s, PAD + length :, :] = jnp.zeros((PAD, WIDTH), f32)

        def first(i, _):
            r = pl.multiple_of(i * ROWS, ROWS)
            at = pl.ds(pl.multiple_of(s * length + r, ROWS), ROWS)
            after = pl.ds(pl.multiple_of(r + PAD, PAD), ROWS)
            ext_ref[s, after, :] = inner_ref[at, :].astype(f32)
            ext = ext_ref[s, pl.ds(r, ROWS + PAD), :]
            pre = taps_of(ext, cw_ref[...], PAD - taps + 1, ROWS) + cb_ref[...]
            sg = sigmoid(pre)
            back = back_ref[at, :] * (sg * (1.0 + pre * (1.0 - sg)))
            pre_ref[s, after, :] = back
            for k in range(taps):
                at_k = PAD - taps + 1 + k
                vec_ref[k : k + 1, :] += jnp.sum(back * ext[at_k : at_k + ROWS], axis=0, keepdims=True)
            vec_ref[taps : taps + 1, :] += jnp.sum(back, axis=0, keepdims=True)
            return 0

        lax.fori_loop(0, length // ROWS, first, 0)

        def back_rows(ext, rows):
            return sum(cw_ref[k : k + 1, :] * ext[taps - 1 - k : taps - 1 - k + rows] for k in range(taps))

        def second(i, _):
            r = pl.multiple_of(i * ROWS, ROWS)
            at = pl.ds(pl.multiple_of(s * length + r, ROWS), ROWS)
            ext = pre_ref[s, pl.ds(pl.multiple_of(r + PAD, PAD), ROWS + PAD), :]
            igr_ref[at, :] = back_rows(ext, ROWS).astype(bf16)
            return 0

        lax.fori_loop(0, length // ROWS, second, 0)
        tail_ref[s * PAD : (s + 1) * PAD, :] = back_rows(pre_ref[s, length :, :], PAD)
        lead = pre_ref[s, : 2 * PAD, :]
        kept = lax.broadcasted_iota(jnp.int32, (PAD, WIDTH), 0) < taps - 1
        head = sum(cw_ref[k : k + 1, :] * lead[PAD - k : 2 * PAD - k] for k in range(taps))
        head_ref[s * PAD : (s + 1) * PAD, :] = jnp.where(kept, head, 0.0)

    vec_ref[taps + 1 : taps + 2, :] = rb_ref[0:1, :]
    vec_ref[taps + 2 : taps + 3, :] = sk_ref[0:1, :]
    vec_ref[8:, :] = dlog_ref[...]
    count = place_ref.shape[0]
    wide = packed_ref.shape[2]
    rows_each = turned_ref.shape[0] // count
    rows_pad = padded(rows_each)
    before_normed = normalized(halo_ref[...], gain_ref[...])
    for b in range(WIDTH // wide):
        cols = slice(b * wide, (b + 1) * wide)
        shifted = jnp.concatenate(
            [
                jnp.concatenate(
                    [jnp.zeros((PAD - taps + 1, wide), f32), head_ref[s * PAD : s * PAD + taps - 1, cols]], axis=0
                )
                for s in range(nseq)
            ],
            axis=0,
        )
        product = jnp.dot(turned_ref[...], igr_ref[:, cols], preferred_element_type=f32) + contract_rows(
            before_normed, shifted.astype(bf16)
        )
        at = pl.ds(pl.multiple_of((j * (WIDTH // wide) + b) * rows_pad, rows_pad), rows_pad)
        for q in range(count):
            packed_ref[place_ref[q], at, :] = share_rows(product, q, rows_each)
    eye = (
        lax.broadcasted_iota(jnp.int32, (vec_ref.shape[0], wide), 0) + 160
        == lax.broadcasted_iota(jnp.int32, (vec_ref.shape[0], wide), 1)
    ).astype(bf16)
    small = (
        contract_rows(joined(x_ref, slice(None)), pg_ref[...])
        + contract_rows(rl_ref[...], rank_ref[...])
        + contract_rows(vec_ref[...].astype(bf16), eye)
    )
    base = packed_ref.shape[1] - padded(part)
    for q in range(WIDTH // part):
        packed_ref[place_ref[j * (WIDTH // part) + q], base : base + padded(part), :] = share_rows(small, q, part)


def padded(rows):
    return max(rows, 16)


def share_rows(values, share, rows):
    taken = values[share * rows : (share + 1) * rows]
    if rows < padded(rows):
        taken = jnp.concatenate([taken, jnp.zeros((padded(rows) - rows, values.shape[1]), values.dtype)], axis=0)
    return taken.astype(bf16)


def weight_grad_kernel(place_ref, gated_ref, gate_ref, cot_ref, turned_ref, packed_ref, *, part):
    j = pl.program_id(0)
    count = place_ref.shape[0]
    model = cot_ref.shape[1]
    rows_each = model // count
    rows_pad = padded(rows_each)
    product = contract_rows(gated_ref[...], cot_ref[...])
    for q in range(WIDTH // part):
        packed_ref[place_ref[j * (WIDTH // part) + q], : padded(part), :] = share_rows(product, q, part)
    product = jnp.dot(turned_ref[...], gate_ref[...], preferred_element_type=f32)
    each = model // WIDTH
    at = pl.ds(pl.multiple_of(padded(part) + (j // each) * rows_pad, 16), rows_pad)
    cols = pl.ds(pl.multiple_of((j % each) * WIDTH, WIDTH), WIDTH)
    for q in range(count):
        packed_ref[place_ref[q], at, cols] = share_rows(product, q, rows_each)


def weight_grads(place, gated, gate_grad, cot, turned, part):
    rows, width = gated.shape
    model = cot.shape[1]
    count = place.shape[0]
    packed_rows = padded(part) + (width // model) * padded(model // count)
    col = pl.BlockSpec((rows, WIDTH), lambda j, _: (0, j))
    fixed = lambda a: pl.BlockSpec(a.shape, lambda j, _: (0,) * a.ndim, pipeline_mode=pl.Buffered(1))
    return pl.pallas_call(
        functools.partial(weight_grad_kernel, part=part),
        grid_spec=pltpu.PrefetchScalarGridSpec(
            num_scalar_prefetch=1,
            grid=(width // WIDTH,),
            in_specs=[col, col, fixed(cot), fixed(turned)],
            out_specs=pl.BlockSpec((count, packed_rows, model), lambda j, _: (0, 0, 0)),
        ),
        out_shape=jax.ShapeDtypeStruct((count, packed_rows, model), bf16),
        compiler_params=pltpu.CompilerParams(vmem_limit_bytes=VMEM, dimension_semantics=("arbitrary",)),
        cost_estimate=pl.CostEstimate(flops=4 * rows * width * model, bytes_accessed=14 * 2**20, transcendentals=0),
        name="weight_grads",
    )(place, gated, gate_grad, cot, turned)


def input_grads(
    place, cp, inner, before, x, pg, select_weight, conv_weight, conv_bias, turned, halo, gain, rate_low, rank_part,
    decay_grad, rate_bias_grad, skip_grad, nseq, length, part,
):
    rows, width = cp.shape
    wide = pg.shape[1]
    count = place.shape[0]
    model = turned.shape[0]
    packed_rows = (width // wide) * padded(model // count) + padded(part)
    o = jax.ShapeDtypeStruct

    def drop(spec):
        return pl.BlockSpec(spec.block_shape, lambda j, _, f=spec.index_map: f(j), pipeline_mode=spec.pipeline_mode)

    specs = [
        block_of(rows), block_of(rows), block_of(before.shape[0]), tiles_of(rows), whole(pg),
        pl.BlockSpec((WIDTH, wide), lambda j: (j, 0)), block_of(conv_weight.shape[0]), block_of(1), whole(turned),
        whole(halo), whole(gain), block_of(rows), whole(rank_part), block_of(N), block_of(8), block_of(8),
    ]
    out_specs = [
        pl.BlockSpec((count, packed_rows, wide), lambda j: (0, 0, 0)), block_of(rows), block_of(nseq * PAD),
        block_of(nseq * PAD),
    ]
    return pl.pallas_call(
        functools.partial(input_grad_kernel, nseq=nseq, length=length, part=part),
        grid_spec=pltpu.PrefetchScalarGridSpec(
            num_scalar_prefetch=1,
            grid=(width // WIDTH,),
            in_specs=[drop(s) for s in specs],
            out_specs=[drop(s) for s in out_specs],
            scratch_shapes=[
                pltpu.VMEM((nseq, PAD + length, WIDTH), f32), pltpu.VMEM((nseq, PAD + length + PAD, WIDTH), f32),
                pltpu.VMEM((rows, WIDTH), f32), pltpu.VMEM((8 + N, WIDTH), f32),
            ],
        ),
        out_shape=(
            o((count, packed_rows, wide), bf16), o((rows, width), bf16), o((nseq * PAD, width), f32),
            o((nseq * PAD, width), f32),
        ),
        compiler_params=pltpu.CompilerParams(vmem_limit_bytes=VMEM, dimension_semantics=("arbitrary",)),
        cost_estimate=pl.CostEstimate(flops=4 * rows * width * model, bytes_accessed=24 * 2**20, transcendentals=0),
        name="input_grads",
    )(
        place, cp, inner, before, x, pg, select_weight, conv_weight, conv_bias, turned, halo, gain, rate_low,
        rank_part, decay_grad, rate_bias_grad, skip_grad,
    )


def flip_bit(axis, bit):
    return [(i, i ^ bit) for i in range(lax.axis_size(axis))]


def bits_of(axis):
    size = lax.axis_size(axis)
    return [(axis, 1 << k) for k in range(size.bit_length() - 1)]


def places(order):
    grp = lax.axis_size("grp")
    other = jnp.arange(lax.axis_size("seq") * grp) ^ (lax.axis_index("seq") * grp + lax.axis_index("grp"))
    position = jnp.zeros_like(other)
    for axis, bit in order:
        position = 2 * position + (other // (bit * grp if axis == "seq" else bit)) % 2
    return position.astype(jnp.int32)


def pairs_of(bits):
    return [bits[i : i + 2] for i in range(0, len(bits), 2)]


def sum_packed(packed, order, rounds):
    held = packed
    for bits in rounds:
        count = 1 << len(bits)
        held = held.reshape((count, held.shape[0] // count) + held.shape[1:])
        total = held[0].astype(f32)
        for other in range(1, count):
            flip = sum(bit for i, (axis, bit) in enumerate(bits) if (other >> (len(bits) - 1 - i)) & 1)
            axis = bits[0][0]
            total = total + lax.ppermute(held[other].astype(bf16), axis, flip_bit(axis, flip)).astype(f32)
        held = total
    return held[0]


def ring_place(chips):
    ring = [i ^ (i >> 1) for i in range(chips)]
    return [ring.index(i) for i in range(chips)], ring


def half_places():
    grp, chips = lax.axis_size("grp"), lax.axis_size("seq") // 2
    place = jnp.array(ring_place(chips)[0], jnp.int32)
    share = jnp.arange(2 * chips * grp)
    seq = share // grp
    other = (seq % 2) ^ (lax.axis_index("seq") % 2)
    return ((other * chips + place[seq // 2]) * grp + share % grp).astype(jnp.int32)


def sum_offloaded(packed):
    half = packed.shape[0] // 2
    got = lax.ppermute(packed[half:], "seq", flip_bit("seq", 1))
    held = (packed[:half].astype(f32) + got.astype(f32)).astype(bf16)
    ring = ring_place(lax.axis_size("seq") // 2)[1]
    groups = [[2 * chip + core for chip in ring] for core in range(2)]
    held = lax.psum_scatter(held, "seq", scatter_dimension=0, axis_index_groups=groups, tiled=True)
    return lax.psum_scatter(held, "grp", scatter_dimension=0, tiled=True)[0].astype(f32)


def summary_block(span, summary):
    width = span.shape[-1]
    high = span.astype(bf16)
    low = (span - high.astype(f32)).astype(bf16)
    return jnp.concatenate([summary.astype(bf16).reshape(-1, width), high, low], axis=0)


def carried(block, shape, rates, backward, after=None):
    count, mine = lax.axis_size("seq"), lax.axis_index("seq")
    blocks = lax.all_gather(block, "seq")
    if after is not None:
        blocks, after = lax.optimization_barrier((blocks, after))
    rows = shape[0] * shape[1]
    entering = jnp.zeros(shape, f32)
    for turn in range(count - 1):
        j = count - 1 - turn if backward else turn
        theirs = blocks[j].astype(f32)
        span = theirs[rows : rows + shape[0]] + theirs[rows + shape[0] :]
        longer = jnp.exp(span[:, None, :] * rates) * entering + theirs[:rows].reshape(shape)
        entering = jnp.where(mine < j if backward else j < mine, longer, entering)
    return entering, after


def contract_rows(left, right, kind=f32):
    return lax.dot_general(left, right, (((0,), (0,)), ((), ())), preferred_element_type=f32).astype(kind)


def shards(
    tokens,
    cotangent,
    norm_gain,
    in_weight,
    conv_weight,
    conv_bias,
    select_weight,
    rate_weight,
    rate_bias,
    decay_log,
    skip_gain,
    out_weight,
):
    nseq, length, model = tokens.shape
    inner_width = out_weight.shape[0]
    rank = rate_weight.shape[0]
    taps = conv_weight.shape[0]
    rows = nseq * length
    share_count = lax.axis_size("seq") * lax.axis_size("grp")
    tok = tokens.reshape(rows, model)
    cot = cotangent.reshape(rows, model)
    gain, skip, bias = norm_gain[None], skip_gain[None], conv_bias[None]
    pieces, grp = lax.axis_size("seq"), lax.axis_size("grp")
    halo = lax.ppermute(tokens[:, length - PAD :], "seq", [(i, i + 1) for i in range(pieces - 1)])
    halo = halo.reshape(nseq * PAD, model)
    normed, turned, g, ga, gs = gate_side(tok, gain, cot, in_weight, out_weight)
    inner, before, x, proj = inner_side(
        normed, halo, gain, in_weight, conv_weight, bias, select_weight, nseq, length
    )
    in_gate, out_gate = proj[:, rank : rank + N], proj[:, rank + N :]
    rates = -jnp.exp(decay_log).T
    a2 = rates * LOG2E
    bb = jnp.broadcast_to(in_gate[:, :, None], (rows, N, 128))
    local_end, span, dl, u = state_end(proj, rate_weight, rate_bias[None], x, a2, bb, nseq, length)
    ahead = summary_block(span, local_end)
    ahead, g = lax.optimization_barrier((ahead, g))
    entering, _ = carried(ahead, local_end.shape, rates, False)
    cb = jnp.broadcast_to(out_gate[:, :, None], (rows, N, 128))
    sent_back = adjoint_end(dl, g, a2, cb, nseq, length)
    lc = spread(out_gate, nseq, length, 1, False)
    lb = spread(in_gate, nseq, length, 2, True)
    ls = own_column(nseq * T, T, T * nseq * 2 * N, nseq, 2, 1, True).astype(bf16)
    behind = summary_block(span, sent_back)
    behind, u = lax.optimization_barrier((behind, u))
    states, gated, gate_grad, out_grad, skip_grad = forward(
        dl, u, g, ga, gs, x, skip, bb, lc, a2, entering, nseq, length, 2
    )
    part, part_rows = inner_width // share_count, model // share_count
    weight_packed = weight_grads(half_places(), gated, gate_grad, cot, turned, part)
    leaving, weight_packed = carried(behind, sent_back.shape, rates, True, weight_packed)
    leaving, weight_packed = lax.optimization_barrier((leaving, weight_packed))
    weight_share = sum_offloaded(weight_packed)
    out_share = weight_share[:part]
    gate_share = weight_share[padded(part) :].reshape(-1, padded(part_rows), model)[:, :part_rows]
    gate_share = gate_share.transpose(1, 0, 2).reshape(part_rows, inner_width)
    rate_low, conv_part, in_grad, decay_grad, rate_bias_grad = backward(
        dl, u, g, x, skip, cb, lb, ls, rates, a2, leaving, entering, states, nseq, length, 2
    )
    rank_grad = rows_dot(rate_low, rate_weight)
    wide = 256
    picks = rank + 2 * N
    pg = jnp.concatenate(
        [
            rank_grad.astype(bf16),
            in_grad.reshape(rows, N).astype(bf16),
            out_grad.reshape(rows, N).astype(bf16),
            jnp.zeros((rows, wide - picks), bf16),
        ],
        axis=1,
    )
    rank_part = jnp.pad(proj[:, :rank].astype(bf16), ((0, 0), (picks, wide - picks - rank)))
    seq_bits, grp_bits = bits_of("seq"), bits_of("grp")
    order = seq_bits + grp_bits
    packed, inner_grad, tail, head = input_grads(
        places(order), conv_part, inner, before, x, pg, jnp.pad(select_weight, ((0, 0), (0, wide - picks))),
        conv_weight, bias, turned, halo, gain, rate_low, rank_part, decay_grad, rate_bias_grad, skip_grad,
        nseq, length, part,
    )
    rounds = [seq_bits[:1]] + pairs_of(seq_bits[1:]) + pairs_of(grp_bits)
    held = sum_packed(packed, order, rounds)
    blocks = inner_width // wide
    inner_share = held[: blocks * padded(part_rows)].reshape(blocks, padded(part_rows), wide)[:, :part_rows]
    inner_share = inner_share.transpose(1, 0, 2).reshape(part_rows, inner_width)
    small = held[blocks * padded(part_rows) :][:part]
    sent = head.reshape(nseq, PAD, inner_width)[:, : taps - 1].astype(bf16)
    returned = lax.ppermute(sent, "seq", [(i + 1, i) for i in range(pieces - 1)]).astype(f32)
    fixed = (tail.reshape(nseq, PAD, inner_width)[:, PAD - taps + 1 :] + returned).astype(bf16)
    inner_grad = (
        inner_grad.reshape(nseq, length, inner_width).at[:, length - taps + 1 :].set(fixed).reshape(rows, inner_width)
    )
    wide_tok = tok.astype(f32)
    scale = lax.rsqrt(jnp.mean(wide_tok * wide_tok, axis=1, keepdims=True) + epsilon)
    normed_grad = rows_dot(gate_grad, in_weight[:, inner_width:]) + rows_dot(inner_grad, in_weight[:, :inner_width])
    lifted = normed_grad * norm_gain
    dots = jnp.mean(lifted * wide_tok, axis=1, keepdims=True)
    tokens_grad = cot.astype(f32) + scale * lifted - wide_tok * (scale * scale * scale) * dots
    block_out = wide_tok + jnp.dot(gated, out_weight, preferred_element_type=f32)
    in_share = jnp.concatenate([inner_share, gate_share], axis=1)
    first = (lax.axis_index("seq") * grp + lax.axis_index("grp")) * part_rows
    own_weight = lax.dynamic_slice_in_dim(in_weight, first, part_rows, 0).astype(f32)
    own_gain = lax.dynamic_slice_in_dim(norm_gain, first, part_rows, 0)
    gain_share = jnp.sum(own_weight * in_share, axis=1) / own_gain
    vectors = small[:, picks + rank :].T
    return (
        block_out.astype(bf16).reshape(tokens.shape),
        tokens_grad.astype(bf16).reshape(tokens.shape),
        gain_share,
        in_share,
        vectors[:taps],
        vectors[taps],
        small[:, :picks],
        small[:, picks : picks + rank].T,
        vectors[taps + 1],
        small[:, picks + rank + 8 : picks + rank + 8 + N],
        vectors[taps + 2],
        out_share,
    )


def solution(mesh):
    sharded = P("grp", "seq", None)
    shares = ("seq", "grp")
    return jax.shard_map(
        shards,
        mesh=mesh,
        in_specs=(sharded, sharded) + (P(),) * 10,
        out_specs=(
            sharded,
            sharded,
            P(shares),
            P(shares, None),
            P(None, shares),
            P(shares),
            P(shares, None),
            P(None, shares),
            P(shares),
            P(shares, None),
            P(shares),
            P(shares, None),
        ),
        check_vma=False,
    )
```

profile of v0, /device:TPU:0, one launch (start us, length us, event | category | flops | bytes accessed | tf_op | source)
XLA Modules:
  0.0 327.7 jit_solution(11203463132394852093)
XLA Ops:
  8.0 2.3 collective-permute-start
  10.4 1.6 broadcast_multiply_fusion.a2_ref
  13.0 14.3 %gate_side.1 = (bf16[512,1024]{1,0:T(8,128)(2,1)}, bf16[1024,512]{1,0:T(8,128)(2,1)}, f32[16,512,128]{2,1,0:T(8,128)}, f32[16,512,128]{2,1,0:T(8,128)}, f32[16,512,128]{2,1,0:T(8,128)}) custom-call(bf16[512,1024]{1,0:T(8,128)(2,1)} %bitcast.105, f32[1,1024]{1,0:T(1,128)} %bitcast.140, bf16[512,1024]{1,0:T(8,128)(2,1)} %bitcast.111, ...), custom_call_target="tpu_custom_call" | custom-call | flops 4294967296 | bytes 29364224 | tf_op jit(solution)/shard_map/gate_side/pallas_call | solution.py:273
  27.8 1.0 copy.49.sw_ref
  29.4 12.1 %inner_side.1 = (bf16[512,2048]{1,0:T(8,128)(2,1)}, bf16[16,2048]{1,0:T(8,128)(2,1)}, bf16[16,512,128]{2,1,0:T(8,128)(2,1)}, f32[512,96]{1,0:T(8,128)}) custom-call(bf16[512,1024]{1,0:T(8,128)(2,1)} %get-tuple-element.59.normed_ref, bf16[16,1024]{1,0:T(8,128)(2,1)} %bitcast.133, f32[1,1024]{1,0:T(1,128)} %bitcast.141, bf16[1024,4096]{1,0:T(8,128)(2,1)} %wi_ref.1, ...), custom_call_target="tpu_custom_call" | custom-call | flops 2147483648 | bytes 14680064 | tf_op jit(solution)/shard_map/inner_side/pallas_call | solution.py:480
  41.5 1.2 fusion.97
  42.7 2.6 broadcast_in_dim.23.bb_ref
  45.4 22.0 %state_end.1 = (f32[2,16,2048]{2,1,0:T(8,128)}, f32[2,2048]{1,0:T(2,128)}, f32[16,512,128]{2,1,0:T(8,128)}, f32[16,512,128]{2,1,0:T(8,128)}) custom-call(f32[512,96]{1,0:T(8,128)} %get-tuple-element.60.proj_ref, bf16[64,2048]{1,0:T(8,128)(2,1)} %rw_ref.1, f32[1,2048]{1,0:T(1,128)} %bitcast.145, bf16[16,512,128]{2,1,0:T(8,128)(2,1)} %get-tuple-element.61.x_ref, ...), custom_call_target="tpu_custom_call" | custom-call | flops 20000000000 | bytes 15556608 | tf_op jit(solution)/shard_map/state_end/pallas_call | solution.py:273
  68.2 1.0 convert_element_type.186
  70.0 2.6 broadcast_in_dim.24.cb_ref
  72.6 15.8 %adjoint_end.1 = f32[2,16,2048]{2,1,0:T(8,128)} custom-call(f32[16,512,128]{2,1,0:T(8,128)} %get-tuple-element.62.dl_ref, f32[16,512,128]{2,1,0:T(8,128)} %get-tuple-element.66.g_ref, f32[16,2048]{1,0:T(8,128)} %broadcast_multiply_fusion.a2_ref, f32[512,16,128]{2,1,0:T(8,128)} %broadcast_in_dim.24.cb_ref), custom_call_target="tpu_custom_call" | custom-call | flops 20000000000 | bytes 12976128 | tf_op jit(solution)/shard_map/adjoint_end/pallas_call | solution.py:273
  90.3 1.5 fusion.19.lc_ref
  91.8 5.5 %all-gather.7.cloned.1.call-done = bf16[8,36,2048]{2,1,0:T(8,128)(2,1)} async-done(((bf16[1,36,2048]{2,1,0:T(8,128)(2,1)}), bf16[8,36,2048]{2,1,0:T(8,128)(2,1)}) %all-gather.7.cloned.1.call-update) | async-done | bytes 1179664 | tf_op jit(solution)/shard_map/all_gather | solution.py:750
  97.2 1.6 slice_convert_fusion.1
  99.1 1.1 add_select_fusion.4.hin_ref
  100.2 33.6 %forward.1 = (bf16[8192,2048]{1,0:T(8,128)(2,1)}, bf16[512,2048]{1,0:T(8,128)(2,1)}, bf16[512,2048]{1,0:T(8,128)(2,1)}, f32[32,256]{1,0:T(8,128)}, f32[8,2048]{1,0:T(8,128)}) custom-call(f32[16,512,128]{2,1,0:T(8,128)} %get-tuple-element.62.dl_ref, f32[16,512,128]{2,1,0:T(8,128)} %get-tuple-element.68.u_ref, f32[16,512,128]{2,1,0:T(8,128)} %get-tuple-element.66.g_ref, ...), custom_call_target="tpu_custom_call" | custom-call | flops 30000001024 | bytes 66035712 | tf_op jit(solution)/shard_map/forward/pallas_call | solution.py:273
  133.8 11.0 %weight_grads.1 = bf16[32,128,1024]{2,1,0:T(8,128)(2,1)} custom-call(s32[32]{0:T(128)} %fusion.73.place_ref, bf16[512,2048]{1,0:T(8,128)(2,1)} %get-tuple-element.72.gated_ref, bf16[512,2048]{1,0:T(8,128)(2,1)} %get-tuple-element.73.gate_ref, bf16[512,1024]{1,0:T(8,128)(2,1)} %bitcast.112, bf16[1024,512]{1,0:T(8,128)(2,1)} %get-tuple-element.75.turned_ref), custom_call_target="tpu_custom_call" | custom-call | flops 4294967296 | bytes 14680064 | tf_op jit(solution)/shard_map/weight_grads/pallas_call | solution.py:618
  144.8 1.7 slice_convert_fusion.8
  146.9 1.1 add_select_fusion.3.lin_ref
  148.7 2.4 slice.430
  151.4 1.1 pad.10.sw_ref
  155.2 2.4 select_convert_fusion.lb_ref
  157.7 1.0 collective-permute-done.9
  158.7 7.7 %add_convert_fusion = bf16[16,128,1024]{2,1,0:T(8,128)(2,1)} fusion(bf16[16,128,1024]{2,1,0:T(8,128)(2,1)} %collective-permute-done.9, bf16[32,128,1024]{2,1,0:T(8,128)(2,1)} %weight_grads.1), kind=kLoop, calls=%fused_computation | loop fusion | flops 8388608 | bytes 12582912 | tf_op jit(solution)/shard_map/convert_element_type | solution.py:734
  166.6 41.2 %backward.1 = (bf16[512,2048]{1,0:T(8,128)(2,1)}, f32[512,2048]{1,0:T(8,128)}, f32[32,256]{1,0:T(8,128)}, f32[16,2048]{1,0:T(8,128)}, f32[8,2048]{1,0:T(8,128)}) custom-call(f32[16,512,128]{2,1,0:T(8,128)} %get-tuple-element.62.dl_ref, f32[16,512,128]{2,1,0:T(8,128)} %get-tuple-element.68.u_ref, f32[16,512,128]{2,1,0:T(8,128)} %get-tuple-element.66.g_ref, ...), custom_call_target="tpu_custom_call" | custom-call | flops 49999998976 | bytes 60858368 | tf_op jit(solution)/shard_map/backward/pallas_call | solution.py:273
  208.8 2.4 convolution_convert_fusion
  212.2 24.3 %input_grads.1 = (bf16[32,320,256]{2,1,0:T(8,128)(2,1)}, bf16[512,2048]{1,0:T(8,128)(2,1)}, f32[16,2048]{1,0:T(8,128)}, f32[16,2048]{1,0:T(8,128)}) custom-call(s32[32]{0:T(128)} %fusion.77.place_ref, f32[512,2048]{1,0:T(8,128)} %get-tuple-element.80.cp_ref, bf16[512,2048]{1,0:T(8,128)(2,1)} %get-tuple-element.81.inner_ref, ...), custom_call_target="tpu_custom_call" | custom-call | flops 4294967296 | bytes 25165824 | tf_op jit(solution)/shard_map/input_grads/pallas_call | solution.py:656
  236.5 3.6 %slice.419 = bf16[16,320,256]{2,1,0:T(8,128)(2,1)} slice(bf16[32,320,256]{2,1,0:T(8,128)(2,1)} %get-tuple-element.92), slice={[16:32], [0:320], [0:256]} | slice | bytes 5242880 | tf_op jit(solution)/shard_map/slice | solution.py:712
  240.4 1.4 collective-permute-start.1
  241.8 6.1 %fusion.4 = bf16[512,1024]{1,0:T(8,128)(2,1)} fusion(bf16[512,1024]{1,0:T(8,128)(2,1)S(1)} %bitcast.106, bf16[512,2048]{1,0:T(8,128)(2,1)} %get-tuple-element.72.gated_ref, bf16[2048,1024]{1,0:T(8,128)(2,1)} %ow_ref.1), kind=kOutput, calls=%fused_computation.19 | convolution fusion | flops 2149056512 | bytes 8388608 | tf_op jit(solution)/shard_map/dot_general | solution.py:865
  248.0 1.5 scatter.4
  249.5 5.3 %fusion = f32[512,1024]{1,0:T(8,128)S(1)} fusion(bf16[512,2048]{1,0:T(8,128)(2,1)} %bitcast.144, bf16[1024,4096]{1,0:T(8,128)(2,1)} %wi_ref.1), kind=kOutput, calls=%fused_computation.2 | convolution fusion | flops 2147483648 | bytes 8388608 | tf_op jit(solution)/shard_map/dot_general | solution.py:42
  254.9 5.1 %convert_add_fusion = (f32[16,320,256]{2,1,0:T(8,128)}, bf16[16,320,256]{2,1,0:T(8,128)(2,1)S(1)}) fusion(bf16[16,320,256]{2,1,0:T(8,128)(2,1)} %collective-permute-done.2, bf16[32,320,256]{2,1,0:T(8,128)(2,1)S(1)} %copy-done.1), kind=kLoop, calls=%fused_computation.1 | loop fusion | flops 5242880 | bytes 13107200 | tf_op jit(solution)/shard_map/add | solution.py:712
  260.0 1.3 fusion.95
  261.4 3.0 collective-permute-start.5
  264.4 1.5 collective-permute-start.4
  266.0 3.9 %fusion.8 = (f32[512]{0:T(512)S(1)}, f32[512,1024]{1,0:T(8,128)}) fusion(bf16[2,256,1024]{2,1,0:T(8,128)(2,1)S(1)} %copy-done.3, f32[1024]{0:T(1024)S(1)} %copy-done.16, f32[512,1024]{1,0:T(8,128)S(1)} %fusion, bf16[512,2048]{1,0:T(8,128)(2,1)S(1)} %copy-done.17, bf16[1024,4096]{1,0:T(8,128)(2,1)S(1)} %bitcast.104), kind=kOutput, calls=%fused_computation.23 | convolution fusion | flops 2150104576 | bytes 11540480 | tf_op jit(solution)/shard_map/dot_general | solution.py:42
  269.9 10.3 %collective-permute-done.5 = bf16[4,320,256]{2,1,0:T(8,128)(2,1)S(1)} collective-permute-done((bf16[4,320,256]{2,1,0:T(8,128)(2,1)}, bf16[4,320,256]{2,1,0:T(8,128)(2,1)S(1)}, u32[]{:S(2)}, u32[]{:S(2)}) %collective-permute-start.5) | collective-permute-done | bytes 655392 | tf_op jit(solution)/shard_map/ppermute | solution.py:712
  280.3 13.8 %collective-permute-done.4 = bf16[4,320,256]{2,1,0:T(8,128)(2,1)S(1)} collective-permute-done((bf16[4,320,256]{2,1,0:T(8,128)(2,1)}, bf16[4,320,256]{2,1,0:T(8,128)(2,1)S(1)}, u32[]{:S(2)}, u32[]{:S(2)}) %collective-permute-start.4) | collective-permute-done | bytes 655392 | tf_op jit(solution)/shard_map/ppermute | solution.py:712
  294.3 1.8 fusion.93
  296.1 3.3 collective-permute-start.8
  299.4 1.2 collective-permute-start.6
  300.6 1.6 fusion.7
  302.2 2.9 collective-permute-done.8
  305.1 3.6 %collective-permute-done.7 = bf16[1,320,256]{2,1,0:T(8,128)(2,1)S(1)} collective-permute-done((bf16[1,320,256]{2,1,0:T(8,128)(2,1)S(1)}, bf16[1,320,256]{2,1,0:T(8,128)(2,1)S(1)}, u32[]{:S(2)}, u32[]{:S(2)}) %collective-permute-start.7) | collective-permute-done | bytes 163872 | tf_op jit(solution)/shard_map/ppermute | solution.py:712
  308.7 5.1 %collective-permute-done.6 = bf16[1,320,256]{2,1,0:T(8,128)(2,1)S(1)} collective-permute-done((bf16[1,320,256]{2,1,0:T(8,128)(2,1)S(1)}, bf16[1,320,256]{2,1,0:T(8,128)(2,1)S(1)}, u32[]{:S(2)}, u32[]{:S(2)}) %collective-permute-start.6) | collective-permute-done | bytes 163872 | tf_op jit(solution)/shard_map/ppermute | solution.py:712
  317.4 1.0 slice.524
  318.5 1.3 multiply_reduce_fusion.1
  (146 shorter events, 18.5 us)
Async XLA Ops:
  7.2 90.1 %all-gather.7.cloned.1.call-start = ((), (), s32[]{:S(2)}) async-start(), calls=%async_computation.4 | async-start | bytes 1474560 | tf_op jit(solution)/shard_map/all_gather | solution.py:750
  8.0 20.8 %collective-permute-start = (bf16[2,8,1024]{2,1,0:T(8,128)(2,1)S(1)}, bf16[2,8,1024]{2,1,0:T(8,128)(2,1)S(1)}, u32[]{:S(2)}, u32[]{:S(2)}) collective-permute-start(bf16[2,8,1024]{2,1,0:T(8,128)(2,1)S(1)} %slice.354), channel_id=1, source_target_pairs={{0,4},{4,8},{8,12},{12,16},{16,20},{20,24},{24,28},{1,5},{5,9},{9,... | collective-permute-start | bytes 98312 | tf_op jit(solution)/shard_map/ppermute | solution.py:792
  12.9 133.9 %copy-start.6 = (f32[16,2048]{1,0:T(8,128)}, f32[16,2048]{1,0:T(8,128)S(1)}, u32[]{:S(2)}) copy-start(f32[16,2048]{1,0:T(8,128)S(1)} %negate_bitcast_fusion.a_ref) | copy-start | bytes 393220
  13.0 14.8 %copy-start.10 = (bf16[2048,96]{0,1:T(8,128)(2,1)S(1)}, bf16[2048,96]{0,1:T(8,128)(2,1)}, u32[]{:S(2)}) copy-start(bf16[2048,96]{0,1:T(8,128)(2,1)} %param.21) | copy-start | bytes 1179652
  28.8 0.6 copy-start.13
  69.9 74.9 %all-gather.9.cloned.1.call-start = ((), (), s32[]{:S(2)}) async-start(), calls=%async_computation.5 | async-start | bytes 1474560 | tf_op jit(solution)/shard_map/all_gather | solution.py:750
  72.6 17.7 %copy-start.5 = (f32[512,96]{1,0:T(8,128)S(1)}, f32[512,96]{1,0:T(8,128)}, u32[]{:S(2)}) copy-start(f32[512,96]{1,0:T(8,128)} %get-tuple-element.60.proj_ref) | copy-start | bytes 589828
  90.1 179.8 %reduce-scatter.3.cloned.1.call-start = ((), (), s32[]{:S(2)}) async-start(), calls=%async_computation.2 | async-start | bytes 5242880 | tf_op jit(solution)/shard_map/reduce_scatter | solution.py:737
  144.8 3.9 %copy-start = (bf16[32,128,1024]{2,1,0:T(8,128)(2,1)S(1)}, bf16[32,128,1024]{2,1,0:T(8,128)(2,1)}, u32[]{:S(2)}) copy-start(bf16[32,128,1024]{2,1,0:T(8,128)(2,1)} %weight_grads.1) | copy-start | bytes 25165828
  148.7 2.7 copy-start.2
  151.2 2.1 copy-start.3
  151.2 7.5 %collective-permute-start.9 = (bf16[16,128,1024]{2,1,0:T(8,128)(2,1)}, bf16[16,128,1024]{2,1,0:T(8,128)(2,1)}, u32[]{:S(2)}, u32[]{:S(2)}) collective-permute-start(bf16[16,128,1024]{2,1,0:T(8,128)(2,1)} %slice.430), channel_id=1, source_target_pairs={{0,4},{4,0},{8,12},{12,8},{16,20},{20,16},{24,28},{28,24},{1,5},{5... | collective-permute-start | bytes 12582920 | tf_op jit(solution)/shard_map/ppermute | solution.py:733
  155.2 2.4 copy-start.14
  166.4 151.1 %reduce-scatter.5.cloned.1.call-start = ((), (), s32[]{:S(2)}) async-start(), calls=%async_computation.3 | async-start | bytes 1310720 | tf_op jit(solution)/shard_map/reduce_scatter | solution.py:738
  166.6 42.1 %copy-start.11 = (bf16[64,2048]{1,0:T(8,128)(2,1)S(1)}, bf16[64,2048]{1,0:T(8,128)(2,1)}, u32[]{:S(2)}) copy-start(bf16[64,2048]{1,0:T(8,128)(2,1)} %rw_ref.1) | copy-start | bytes 786436
  236.5 3.8 %copy-start.12 = (f32[16,2048]{1,0:T(8,128)S(1)}, f32[16,2048]{1,0:T(8,128)}, u32[]{:S(2)}) copy-start(f32[16,2048]{1,0:T(8,128)} %get-tuple-element.91) | copy-start | bytes 393220
  240.1 14.8 %collective-permute-start.2 = (bf16[16,320,256]{2,1,0:T(8,128)(2,1)}, bf16[16,320,256]{2,1,0:T(8,128)(2,1)}, u32[]{:S(2)}, u32[]{:S(2)}) collective-permute-start(bf16[16,320,256]{2,1,0:T(8,128)(2,1)} %slice.419), channel_id=1, source_target_pairs={{0,4},{4,0},{8,12},{12,8},{16,20},{20,16},{24,28},{28,24},{1,5},{5... | collective-permute-start | bytes 7864328 | tf_op jit(solution)/shard_map/ppermute | solution.py:712
  240.4 7.6 %copy-start.15 = (f32[16,2048]{1,0:T(8,128)S(1)}, f32[16,2048]{1,0:T(8,128)}, u32[]{:S(2)}) copy-start(f32[16,2048]{1,0:T(8,128)} %get-tuple-element.90) | copy-start | bytes 393220
  240.4 7.6 %collective-permute-start.1 = (bf16[2,3,2048]{2,1,0:T(4,128)(2,1)S(1)}, bf16[2,3,2048]{2,1,0:T(4,128)(2,1)S(1)}, u32[]{:S(2)}, u32[]{:S(2)}) collective-permute-start(bf16[2,3,2048]{2,1,0:T(4,128)(2,1)S(1)} %slice.514), channel_id=1, source_target_pairs={{4,0},{8,4},{12,8},{16,12},{20,16},{24,20},{28,24},{5,1},{9,5},{13... | collective-permute-start | bytes 73736 | tf_op jit(solution)/shard_map/ppermute | solution.py:854
  249.5 5.4 %copy-start.1 = (bf16[32,320,256]{2,1,0:T(8,128)(2,1)S(1)}, bf16[32,320,256]{2,1,0:T(8,128)(2,1)}, u32[]{:S(2)}) copy-start(bf16[32,320,256]{2,1,0:T(8,128)(2,1)} %get-tuple-element.92) | copy-start | bytes 15728644
  249.5 16.4 %slice-start = ((s8[8388608]{0:T(1024)(128)(4,1)}), s8[4194304]{0:T(1024)(128)(4,1)S(1)}, s32[]{:S(2)}) async-start(s8[8388608]{0:T(1024)(128)(4,1)} %bitcast.103), calls=%async_computation.6 | async-start | bytes 8388608
  254.9 11.1 %slice-start.1 = ((s8[8388608]{0:T(1024)(128)(4,1)}), s8[4194304]{0:T(1024)(128)(4,1)S(1)}, s32[]{:S(2)}) async-start(s8[8388608]{0:T(1024)(128)(4,1)} %bitcast.103), calls=%async_computation.7 | async-start | bytes 8388608
  260.0 5.9 %copy-start.16 = (f32[1024]{0:T(1024)S(1)}, f32[1024]{0:T(1024)}, u32[]{:S(2)}) copy-start(f32[1024]{0:T(1024)} %param.17) | copy-start | bytes 12292
  260.0 5.9 %copy-start.17 = (bf16[512,2048]{1,0:T(8,128)(2,1)S(1)}, bf16[512,2048]{1,0:T(8,128)(2,1)}, u32[]{:S(2)}) copy-start(bf16[512,2048]{1,0:T(8,128)(2,1)} %get-tuple-element.73.gate_ref) | copy-start | bytes 6291460
  261.4 18.9 %collective-permute-start.5 = (bf16[4,320,256]{2,1,0:T(8,128)(2,1)}, bf16[4,320,256]{2,1,0:T(8,128)(2,1)S(1)}, u32[]{:S(2)}, u32[]{:S(2)}) collective-permute-start(bf16[4,320,256]{2,1,0:T(8,128)(2,1)} %get-tuple-element.152), channel_id=1, source_target_pairs={{0,24},{4,28},{8,16},{12,20},{16,8},{20,12},{24,0},{28,4},{1,25},{... | collective-permute-start | bytes 1966088 | tf_op jit(solution)/shard_map/ppermute | solution.py:712
  264.4 29.6 %collective-permute-start.4 = (bf16[4,320,256]{2,1,0:T(8,128)(2,1)}, bf16[4,320,256]{2,1,0:T(8,128)(2,1)S(1)}, u32[]{:S(2)}, u32[]{:S(2)}) collective-permute-start(bf16[4,320,256]{2,1,0:T(8,128)(2,1)} %get-tuple-element.153), channel_id=1, source_target_pairs={{0,8},{4,12},{8,0},{12,4},{16,24},{20,28},{24,16},{28,20},{1,9},{5... | collective-permute-start | bytes 1966088 | tf_op jit(solution)/shard_map/ppermute | solution.py:712
  266.0 28.3 %collective-permute-start.3 = (bf16[4,320,256]{2,1,0:T(8,128)(2,1)}, bf16[4,320,256]{2,1,0:T(8,128)(2,1)S(1)}, u32[]{:S(2)}, u32[]{:S(2)}) collective-permute-start(bf16[4,320,256]{2,1,0:T(8,128)(2,1)} %get-tuple-element.151), channel_id=1, source_target_pairs={{0,16},{4,20},{8,24},{12,28},{16,0},{20,4},{24,8},{28,12},{1,17},{... | collective-permute-start | bytes 1966088 | tf_op jit(solution)/shard_map/ppermute | solution.py:712
  294.3 6.3 %copy-start.4 = (f32[512,1024]{1,0:T(8,128)S(1)}, f32[512,1024]{1,0:T(8,128)}, u32[]{:S(2)}) copy-start(f32[512,1024]{1,0:T(8,128)} %get-tuple-element.176) | copy-start | bytes 6291460
  294.3 6.3 %copy-start.9 = (bf16[2,256,1024]{2,1,0:T(8,128)(2,1)S(1)}, bf16[2,256,1024]{2,1,0:T(8,128)(2,1)}, u32[]{:S(2)}) copy-start(bf16[2,256,1024]{2,1,0:T(8,128)(2,1)} %param.16) | copy-start | bytes 3145732
  296.1 9.0 %collective-permute-start.8 = (bf16[1,320,256]{2,1,0:T(8,128)(2,1)S(1)}, bf16[1,320,256]{2,1,0:T(8,128)(2,1)S(1)}, u32[]{:S(2)}, u32[]{:S(2)}) collective-permute-start(bf16[1,320,256]{2,1,0:T(8,128)(2,1)S(1)} %get-tuple-element.169), channel_id=1, source_target_pairs={{0,3},{1,2},{2,1},{3,0},{4,7},{5,6},{6,5},{7,4},{8,11},{9,10},{10,... | collective-permute-start | bytes 491528 | tf_op jit(solution)/shard_map/ppermute | solution.py:712
  299.4 9.3 %collective-permute-start.7 = (bf16[1,320,256]{2,1,0:T(8,128)(2,1)S(1)}, bf16[1,320,256]{2,1,0:T(8,128)(2,1)S(1)}, u32[]{:S(2)}, u32[]{:S(2)}) collective-permute-start(bf16[1,320,256]{2,1,0:T(8,128)(2,1)S(1)} %get-tuple-element.170), channel_id=1, source_target_pairs={{0,1},{1,0},{2,3},{3,2},{4,5},{5,4},{6,7},{7,6},{8,9},{9,8},{10,11... | collective-permute-start | bytes 491528 | tf_op jit(solution)/shard_map/ppermute | solution.py:712
  299.4 14.3 %collective-permute-start.6 = (bf16[1,320,256]{2,1,0:T(8,128)(2,1)S(1)}, bf16[1,320,256]{2,1,0:T(8,128)(2,1)S(1)}, u32[]{:S(2)}, u32[]{:S(2)}) collective-permute-start(bf16[1,320,256]{2,1,0:T(8,128)(2,1)S(1)} %get-tuple-element.168), channel_id=1, source_target_pairs={{0,2},{1,3},{2,0},{3,1},{4,6},{5,7},{6,4},{7,5},{8,10},{9,11},{10,... | collective-permute-start | bytes 491528 | tf_op jit(solution)/shard_map/ppermute | solution.py:712
  317.4 3.0 copy-start.8
  318.5 2.7 copy-start.7
Sparse Core Ops, SparseCore 0:
  70.0 27.1 all-gather.6
  99.1 24.6 all-gather.8
  166.5 43.2 reduce-scatter.2
  270.0 27.6 reduce-scatter.4
where the time goes:
time: 329 us; the launch traced here: 328 us
  Pallas kernels  174 us (53%)
  waiting for transfers between devices  42.4 us (13%)
  other arithmetic  34.4 us (10%)
  local copies, waits for them, and re-layouts  26.7 us (8%)
  matrix products  21.6 us (7%)
  between operations  14.5 us (4%)
  starting transfers between devices  13.9 us (4%)
    pallas_call x5, Pallas kernels, kernel_call(): pl.pallas_call(functools.partial(body, **options), grid=(channels // WIDT...  127 us
    ppermute x7, waiting for transfers between devices, sum_packed(): lax.ppermute(held[other].astype(bf16), axis, flip_bit(axis, flip))  35.9 us
    pallas_call x1, Pallas kernels, input_grads(): pl.pallas_call(functools.partial(input_grad_kernel, nseq=nseq, length=len...  24.3 us
    pallas_call x1, Pallas kernels, inner_side(): pl.pallas_call(functools.partial(inner_kernel, nseq=nseq, length=length),...  12.1 us
    dot_general x3, matrix products, rows_dot(): lax.dot_general(left, right, (((1,), (1,)), ((), ())), preferred_element_...  11.6 us
    pallas_call x1, Pallas kernels, weight_grads(): pl.pallas_call(functools.partial(weight_grad_kernel, part=part), grid_spe...  11 us
    ppermute x7, starting transfers between devices, sum_packed(): lax.ppermute(held[other].astype(bf16), axis, flip_bit(axis, flip))  9.25 us
    convert_element_type x1, other arithmetic, sum_offloaded(): held = (packed[:half].astype(f32) + got.astype(f32)).astype(bf16)  7.67 us
  transfers between devices with their start and end apart: 14, of which 8 were waited for; matrix products, arithmetic and copies ran while one was open for 17% of the time, Pallas kernels for 43%

commit v1 on v0

v1 whole, which is shorter than its diff:
```python
import functools
import math

import jax
import jax.numpy as jnp
import ml_dtypes
import numpy as np
from jax import lax
from jax.experimental import pallas as pl
from jax.experimental.pallas import tpu as pltpu
from jax.sharding import PartitionSpec as P

f32 = jnp.float32
bf16 = jnp.bfloat16
LOG2E = 1.4426950408889634
N = 16
T = 16
WIDTH = 512
NL = WIDTH // 128
VMEM = 60 * 2**20


def lane(l):
    return slice(l * 128, (l + 1) * 128)


def sigmoid(v):
    return pltpu.reciprocal(1.0 + jnp.exp2(v * -LOG2E), approx=True)


def joined(ref, rows):
    return jnp.concatenate([ref[l, rows, :] for l in range(NL)], axis=1)


def steps_of(rows):
    return pl.ds(pl.multiple_of(rows, T), T)


def state_of(t):
    return pl.ds(pl.multiple_of(t * N, N), N)


def rows_dot(left, right):
    return lax.dot_general(left, right, (((1,), (1,)), ((), ())), preferred_element_type=f32)


def rates_of(log_ref):
    return -jnp.exp(log_ref[...])


def state_end_kernel(
    proj_ref, rw_ref, rb_ref, x_ref, log_ref, bb_ref, block_ref, dl_ref, u_ref, a2_ref, pre_ref, *, nseq, length,
):
    rows = nseq * length
    a2_ref[...] = rates_of(log_ref) * LOG2E
    low = proj_ref[:, : rw_ref.shape[0]].astype(bf16)
    pre_ref[...] = jnp.dot(low, rw_ref[...], preferred_element_type=f32) + rb_ref[...]

    def steps(i, _):
        r = pl.multiple_of(i * 64, 64)
        at = pl.ds(r, 64)
        pre = pre_ref[at, :]
        d = jnp.maximum(pre, 0.0) + jnp.log(1.0 + jnp.exp(-jnp.abs(pre)))
        for l in range(NL):
            dl_ref[l, at, :] = d[:, lane(l)]
            u_ref[l, at, :] = d[:, lane(l)] * x_ref[l, at, :].astype(f32)
        return 0

    lax.fori_loop(0, rows // 64, steps, 0)
    for s in range(nseq):
        for l in range(NL):
            span = jnp.sum(dl_ref[l, s * length : (s + 1) * length, :], axis=0, keepdims=True)
            high = span.astype(bf16).astype(f32)
            for i, v in enumerate((high, span - high)):
                at = nseq * (N + i) + s
                block_ref[at : at + 1, lane(l)] = v
    block_ref[nseq * (N + 2) :, :] = jnp.zeros((block_ref.shape[0] - nseq * (N + 2), WIDTH), f32)

    def step(c, h):
        h = [list(v) for v in h]
        for k in range(T):
            for s in range(nseq):
                t = s * length + c * T + k
                bt = bb_ref[t]
                for l in range(NL):
                    f = jnp.exp2(dl_ref[l, pl.ds(t, 1), :] * a2_ref[:, lane(l)])
                    h[s][l] = f * h[s][l] + u_ref[l, pl.ds(t, 1), :] * bt
        return tuple(tuple(v) for v in h)

    z = jnp.zeros((N, 128), f32)
    h = lax.fori_loop(0, length // T, step, ((z,) * NL,) * nseq)
    for s in range(nseq):
        for l in range(NL):
            block_ref[s * N : (s + 1) * N, lane(l)] = h[s][l]


def adjoint_end_kernel(dl_ref, g_ref, log_ref, cb_ref, sb_ref, a2_ref, *, nseq, length):
    a2_ref[...] = rates_of(log_ref) * LOG2E
    nch = length // T

    def step(m, lam):
        lam = [list(v) for v in lam]
        c = nch - 1 - m
        for k in reversed(range(T)):
            for s in range(nseq):
                t = s * length + c * T + k
                ct = cb_ref[t]
                for l in range(NL):
                    f = jnp.exp2(dl_ref[l, pl.ds(t, 1), :] * a2_ref[:, lane(l)])
                    lam[s][l] = f * (lam[s][l] + g_ref[l, pl.ds(t, 1), :] * ct)
        return tuple(tuple(v) for v in lam)

    z = jnp.zeros((N, 128), f32)
    lam = lax.fori_loop(0, nch, step, ((z,) * NL,) * nseq)
    for s in range(nseq):
        for l in range(NL):
            sb_ref[s * N : (s + 1) * N, lane(l)] = lam[s][l].astype(bf16)


def forward_kernel(
    dl_ref, u_ref, g_ref, ga_ref, gs_ref, x_ref, skip_ref, bb_ref, bc_ref, lc_ref, log_ref, hin_ref,
    hb_ref, gated_ref, ggr_ref, outg_ref, gu_ref, sk_ref, a2_ref, *, nseq, length, unroll,
):
    a2_ref[...] = rates_of(log_ref) * LOG2E
    nch = length // T
    skip = skip_ref[...]
    ones = jnp.ones((8, 128), bf16)

    @pl.when(pl.program_id(0) == 0)
    def _():
        outg_ref[...] = jnp.zeros_like(outg_ref)
        gu_ref[...] = jnp.zeros_like(gu_ref)

    def chunk(c, h, acc):
        hbv, pov = {}, [[None] * T for _ in range(nseq)]
        for k in range(T):
            for s in range(nseq):
                t = s * length + c * T + k
                bt = bb_ref[t]
                po = None
                for l in range(NL):
                    g = jnp.broadcast_to(g_ref[l, pl.ds(t, 1), :], (N, 128)).astype(bf16)
                    f = jnp.exp2(dl_ref[l, pl.ds(t, 1), :] * a2_ref[:, lane(l)])
                    held = f * h[s][l]
                    h[s][l] = held + u_ref[l, pl.ds(t, 1), :] * bt
                    hb = held.astype(bf16)
                    hb_ref[state_of(t), lane(l)] = hb
                    hbv[k, s, l] = hb
                    po = hb * g if po is None else po + hb * g
                pov[s][k] = po
        lhs = jnp.concatenate([lc_ref[steps_of(s * length + c * T), :] for s in range(nseq)], axis=0)
        parts = []
        for l in range(0, NL, 2):
            rhs = jnp.concatenate(
                [
                    jnp.concatenate([hbv[k, s, l], hbv[k, s, l + 1]], axis=1)
                    for k in range(T) for s in range(nseq)
                ],
                axis=0,
            )
            parts.append(jnp.dot(lhs, rhs, preferred_element_type=f32))
        sc_all = jnp.concatenate(parts, axis=1)
        for s in range(nseq):
            og = rows_dot(ones, jnp.concatenate(pov[s], axis=0))
            outg_ref[pl.ds(s * nch + c, 1), :] += og[:1]
            at = steps_of(s * length + c * T)
            x = joined(x_ref, at).astype(f32)
            gx = joined(g_ref, at) * x
            d = joined(dl_ref, at)
            bc = jnp.concatenate([bc_ref[at, :]] * NL, axis=1)
            mo = sc_all[s * T : (s + 1) * T] + (d * bc + skip) * x
            gu = gx * d
            gu_ref[at, :] += sum(gu[:, lane(l)] for l in range(NL))
            gated_ref[at, :] = (mo * joined(ga_ref, at)).astype(bf16)
            ggr_ref[at, :] = (mo * joined(gs_ref, at)).astype(bf16)
            acc = acc + gx
        return acc

    def step(i, carry):
        h, acc = carry
        h = [list(v) for v in h]
        for p in range(unroll):
            acc = chunk(i * unroll + p, h, acc)
        return tuple(tuple(v) for v in h), acc

    h0 = tuple(tuple(hin_ref[s, :, lane(l)] for l in range(NL)) for s in range(nseq))
    _, acc = lax.fori_loop(0, nch // unroll, step, (h0, jnp.zeros((T, WIDTH), f32)))
    sk_ref[...] = jnp.broadcast_to(jnp.sum(acc, axis=0, keepdims=True), sk_ref.shape)


def backward_kernel(
    dl_ref, u_ref, g_ref, x_ref, skip_ref, cb_ref, lb_ref, ls_ref, log_ref, lin_ref, hb_ref,
    rl_ref, cp_ref, ing_ref, dlog_ref, rb_ref, a2_ref, *, nseq, length, unroll,
):
    a2_ref[...] = rates_of(log_ref) * LOG2E
    nch = length // T
    abf = rates_of(log_ref).astype(bf16)
    skip = skip_ref[...]
    ones = jnp.ones((8, 128), bf16)

    @pl.when(pl.program_id(0) == 0)
    def _():
        ing_ref[...] = jnp.zeros_like(ing_ref)

    def chunk(c, lam, dlog, rb):
        pov = [[None] * T for _ in range(nseq)]
        dacc = [None] * NL
        vals = {}
        for k in reversed(range(T)):
            for s in range(nseq):
                t = s * length + c * T + k
                ct = cb_ref[t]
                po = None
                for l in range(NL):
                    d = jnp.broadcast_to(dl_ref[l, pl.ds(t, 1), :], (N, 128))
                    u = jnp.broadcast_to(u_ref[l, pl.ds(t, 1), :], (N, 128)).astype(bf16)
                    a = g_ref[l, pl.ds(t, 1), :] * ct + lam[s][l]
                    lam[s][l] = jnp.exp2(d * a2_ref[:, lane(l)]) * a
                    ab = a.astype(bf16)
                    q = ab * hb_ref[state_of(t), lane(l)] * abf[:, lane(l)]
                    qd = q * d.astype(bf16)
                    vals[k, s, l] = (ab, q)
                    dacc[l] = qd if dacc[l] is None else dacc[l] + qd
                    po = ab * u if po is None else po + ab * u
                pov[s][k] = po
            if k % 8 == 0:
                for l in range(NL):
                    dlog[l] = dlog[l] + dacc[l].astype(f32)
                    dacc[l] = None
        lhs = jnp.concatenate(
            [lb_ref[steps_of(s * length + c * T), :] for s in range(nseq)] + [ls_ref[...]], axis=0
        )
        parts = []
        for l in range(0, NL, 2):
            rhs = jnp.concatenate(
                [
                    jnp.concatenate([vals[k, s, l][y], vals[k, s, l + 1][y]], axis=1)
                    for k in reversed(range(T)) for s in range(nseq) for y in range(2)
                ],
                axis=0,
            )
            parts.append(jnp.dot(lhs, rhs, preferred_element_type=f32))
        both = jnp.concatenate(parts, axis=1)
        for s in range(nseq):
            w = both[s * T : (s + 1) * T]
            qs = both[(nseq + s) * T : (nseq + s + 1) * T]
            ig = rows_dot(ones, jnp.concatenate(pov[s], axis=0))
            ing_ref[pl.ds(s * nch + c, 1), :] += ig[:1]
            at = steps_of(s * length + c * T)
            d = joined(dl_ref, at)
            rg = (qs + w * joined(x_ref, at).astype(f32)) * (1.0 - jnp.exp(-d))
            rb = rb + rg
            rl_ref[at, :] = rg.astype(bf16)
            cp_ref[at, :] = w * d + skip * joined(g_ref, at)
        return rb

    def step(m, carry):
        lam, dlog, rb = carry
        lam = [list(v) for v in lam]
        dlog = list(dlog)
        for p in range(unroll):
            rb = chunk(nch - 1 - (m * unroll + p), lam, dlog, rb)
        return tuple(tuple(v) for v in lam), tuple(dlog), rb

    l0 = tuple(tuple(lin_ref[s, :, lane(l)] for l in range(NL)) for s in range(nseq))
    z = jnp.zeros((N, 128), f32)
    _, dlog, rb = lax.fori_loop(0, nch // unroll, step, (l0, (z,) * NL, jnp.zeros((T, WIDTH), f32)))
    for l in range(NL):
        dlog_ref[:, lane(l)] = dlog[l]
    rb_ref[...] = jnp.broadcast_to(jnp.sum(rb, axis=0, keepdims=True), rb_ref.shape)


def block_of(rows):
    return pl.BlockSpec((rows, WIDTH), lambda j: (0, j))


def tiles_of(rows):
    return pl.BlockSpec((NL, rows, 128), lambda j: (j, 0, 0))


def states_of(nseq):
    return pl.BlockSpec((nseq, N, WIDTH), lambda j: (0, 0, j))


def whole(a):
    return pl.BlockSpec(a.shape, lambda j: (0,) * a.ndim, pipeline_mode=pl.Buffered(1))


def kernel_call(body, name, channels, operands, specs, out_specs, outs, flops, scratch=(), **options):
    moved = sum(a.size * a.dtype.itemsize for a in operands) + sum(
        math.prod(o.shape) * o.dtype.itemsize for o in outs
    )
    return pl.pallas_call(
        functools.partial(body, **options),
        grid=(channels // WIDTH,),
        in_specs=specs,
        out_specs=out_specs,
        out_shape=outs,
        scratch_shapes=scratch,
        compiler_params=pltpu.CompilerParams(vmem_limit_bytes=VMEM, dimension_semantics=("arbitrary",)),
        cost_estimate=pl.CostEstimate(flops=flops, bytes_accessed=moved, transcendentals=0),
        name=name,
    )(*operands)


def spread(values, nseq, length, kinds, reverse):
    mask = own_column(nseq * length, length, nseq, kinds, 0, reverse)
    width = mask.shape[1]
    pick = (np.arange(width)[None, :] % N == np.arange(N)[:, None]).astype(ml_dtypes.bfloat16)
    wide = jnp.dot(values.astype(bf16), pick, preferred_element_type=f32)
    return wide.astype(bf16) * mask


def own_column(rows, length, nseq, kinds, kind, reverse):
    column = np.arange(T * nseq * kinds * N)[None, :]
    row = np.arange(rows)[:, None]
    step = column // (nseq * kinds * N)
    if reverse:
        step = T - 1 - step
    own = (step == row % T) & ((column // (kinds * N)) % nseq == row // length) & ((column // N) % kinds == kind)
    return own.astype(ml_dtypes.bfloat16)


def block_rows(nseq):
    return -(-nseq * (N + 2) // 16) * 16


def state_end(proj, rate_weight, rate_bias, x, log, bb, nseq, length):
    tiles, rows, _ = x.shape
    ch = tiles * 128
    o = jax.ShapeDtypeStruct
    return kernel_call(
        state_end_kernel, "state_end", ch,
        (proj, rate_weight, rate_bias, x, log, bb),
        [whole(proj), block_of(rate_weight.shape[0]), block_of(1), tiles_of(rows), block_of(N), whole(bb)],
        [block_of(block_rows(nseq)), tiles_of(rows), tiles_of(rows)],
        (o((block_rows(nseq), ch), f32), o(x.shape, f32), o(x.shape, f32)),
        2 * 10**10, nseq=nseq, length=length,
        scratch=[pltpu.VMEM((N, WIDTH), f32), pltpu.VMEM((rows, WIDTH), f32)],
    )


def adjoint_end(dl, g, log, cb, nseq, length):
    tiles, rows, _ = dl.shape
    ch = tiles * 128
    return kernel_call(
        adjoint_end_kernel, "adjoint_end", ch,
        (dl, g, log, cb),
        [tiles_of(rows), tiles_of(rows), block_of(N), whole(cb)],
        [block_of(nseq * N)],
        (jax.ShapeDtypeStruct((nseq * N, ch), bf16),),
        2 * 10**10, nseq=nseq, length=length, scratch=[pltpu.VMEM((N, WIDTH), f32)],
    )[0]


def forward(dl, u, g, ga, gs, x, skip, bb, bc, lc, log, hin, nseq, length, unroll=1):
    tiles, rows, _ = dl.shape
    ch = tiles * 128
    o = jax.ShapeDtypeStruct
    t = tiles_of(rows)
    return kernel_call(
        forward_kernel, "forward", ch,
        (dl, u, g, ga, gs, x, skip, bb, bc, lc, log, hin),
        [t, t, t, t, t, t, block_of(1), whole(bb), whole(bc), whole(lc), block_of(N), states_of(nseq)],
        [
            block_of(rows * N), block_of(rows), block_of(rows), pl.BlockSpec((rows // T, T * N), lambda j: (0, 0)),
            pl.BlockSpec((rows, 128), lambda j: (0, 0)), block_of(8),
        ],
        (
            o((rows * N, ch), bf16), o((rows, ch), bf16), o((rows, ch), bf16), o((rows // T, T * N), f32),
            o((rows, 128), f32), o((8, ch), f32),
        ),
        3 * 10**10, nseq=nseq, length=length, unroll=unroll, scratch=[pltpu.VMEM((N, WIDTH), f32)],
    )


def backward(dl, u, g, x, skip, cb, lb, ls, log, lin, hb, nseq, length, unroll=1):
    tiles, rows, _ = dl.shape
    ch = tiles * 128
    o = jax.ShapeDtypeStruct
    t = tiles_of(rows)
    st = states_of(nseq)
    return kernel_call(
        backward_kernel, "backward", ch,
        (dl, u, g, x, skip, cb, lb, ls, log, lin, hb),
        [t, t, t, t, block_of(1), whole(cb), whole(lb), whole(ls), block_of(N), st, block_of(rows * N)],
        [block_of(rows), block_of(rows), pl.BlockSpec((rows // T, T * N), lambda j: (0, 0)), block_of(N), block_of(8)],
        (o((rows, ch), bf16), o((rows, ch), f32), o((rows // T, T * N), f32), o((N, ch), f32), o((8, ch), f32)),
        5 * 10**10, nseq=nseq, length=length, unroll=unroll, scratch=[pltpu.VMEM((N, WIDTH), f32)],
    )


epsilon = 1e-05
ROWS = 64
PAD = 8


def normalized(tokens, gain):
    wide = tokens.astype(f32)
    return (wide * lax.rsqrt(jnp.mean(wide * wide, axis=1, keepdims=True) + epsilon) * gain).astype(bf16)


def gate_kernel(tok_ref, gain_ref, cot_ref, wg_ref, ow_ref, normed_ref, turned_ref, scale_ref, g_ref, ga_ref, gs_ref, gh_ref, gg_ref):
    rows = tok_ref.shape[0]

    @pl.when(pl.program_id(0) == 0)
    def _():
        def norm(i, _):
            at = pl.ds(pl.multiple_of(i * ROWS, ROWS), ROWS)
            wide = tok_ref[at, :].astype(f32)
            scale = lax.rsqrt(jnp.mean(wide * wide, axis=1, keepdims=True) + epsilon)
            scale_ref[at, :] = jnp.broadcast_to(scale, (ROWS, 128))
            normed_ref[at, :] = (wide * scale * gain_ref[...]).astype(bf16)
            return 0

        lax.fori_loop(0, rows // ROWS, norm, 0)
        turned_ref[...] = normed_ref[...].T

    gh_ref[...] = jnp.dot(normed_ref[...], wg_ref[...], preferred_element_type=f32)
    gg_ref[...] = rows_dot(cot_ref[...], ow_ref[...])

    def mix(i, _):
        at = pl.ds(pl.multiple_of(i * ROWS, ROWS), ROWS)
        gh = gh_ref[at, :]
        gg = gg_ref[at, :]
        sg = sigmoid(gh)
        ga = gh * sg
        gs = gg * (sg * (1.0 + gh * (1.0 - sg)))
        g = gg * ga
        for l in range(NL):
            g_ref[l, at, :] = g[:, lane(l)]
            ga_ref[l, at, :] = ga[:, lane(l)]
            gs_ref[l, at, :] = gs[:, lane(l)]
        return 0

    lax.fori_loop(0, rows // ROWS, mix, 0)


def gate_side(tokens, gain, cotangent, in_weight, out_weight):
    rows, model = tokens.shape
    inner = out_weight.shape[0]
    first = inner // WIDTH
    tiles = jax.ShapeDtypeStruct((inner // 128, rows, 128), f32)
    return kernel_call(
        gate_kernel, "gate_side", inner,
        (tokens, gain, cotangent, in_weight, out_weight),
        [
            whole(tokens), whole(gain), whole(cotangent),
            pl.BlockSpec((model, WIDTH), lambda j: (0, j + first)),
            pl.BlockSpec((WIDTH, model), lambda j: (j, 0)),
        ],
        [pl.BlockSpec((rows, model), lambda j: (0, 0)), pl.BlockSpec((model, rows), lambda j: (0, 0)), pl.BlockSpec((rows, 128), lambda j: (0, 0))]
        + [tiles_of(rows)] * 3,
        (jax.ShapeDtypeStruct((rows, model), bf16), jax.ShapeDtypeStruct((model, rows), bf16), jax.ShapeDtypeStruct((rows, 128), f32), tiles, tiles, tiles),
        4 * rows * model * inner, scratch=[pltpu.VMEM((rows, WIDTH), f32)] * 2,
    )


def inner_kernel(
    normed_ref, halo_ref, gain_ref, wi_ref, cw_ref, cb_ref, sw_ref, inner_ref, before_ref, x_ref, slope_ref, proj_ref, ext_ref, flat_ref,
    *, nseq, length,
):
    part = jnp.dot(normed_ref[...], wi_ref[...], preferred_element_type=f32).astype(bf16)
    inner_ref[...] = part
    for s in range(nseq):
        for l in range(NL):
            ext_ref[s, l, PAD:, :] = part[s * length : (s + 1) * length, lane(l)].astype(f32)
    before = jnp.dot(
        normalized(halo_ref[...], gain_ref[...]), wi_ref[...], preferred_element_type=f32
    ).astype(bf16)
    before_ref[...] = before
    for s in range(nseq):
        for l in range(NL):
            ext_ref[s, l, :PAD, :] = before[s * PAD : (s + 1) * PAD, lane(l)].astype(f32)

    @pl.when(pl.program_id(0) == 0)
    def _():
        proj_ref[...] = jnp.zeros_like(proj_ref)

    taps = cw_ref.shape[0]
    for s in range(nseq):

        def mix(i, _):
            r = pl.multiple_of(i * ROWS, ROWS)
            at = pl.ds(pl.multiple_of(s * length + r, ROWS), ROWS)
            for l in range(NL):
                pre = cb_ref[:, lane(l)]
                for k in range(taps):
                    pre = pre + cw_ref[k : k + 1, lane(l)] * ext_ref[s, l, pl.ds(r + PAD - taps + 1 + k, ROWS), :]
                sg = sigmoid(pre)
                x = (pre * sg).astype(bf16)
                slope_ref[at, lane(l)] = sg * (1.0 + pre * (1.0 - sg))
                x_ref[l, at, :] = x
                flat_ref[at, lane(l)] = x
            return 0

        lax.fori_loop(0, length // ROWS, mix, 0)
    proj_ref[...] += jnp.dot(flat_ref[...], sw_ref[...], preferred_element_type=f32)


def inner_side(normed, halo, gain, in_weight, conv_weight, conv_bias, select_weight, nseq, length):
    rows, model = normed.shape
    inner, picks = select_weight.shape
    o = jax.ShapeDtypeStruct
    operands = (normed, halo, gain, in_weight, conv_weight, conv_bias, select_weight)
    specs = [
        whole(normed), whole(halo), whole(gain), block_of(model), block_of(conv_weight.shape[0]), block_of(1),
        pl.BlockSpec((WIDTH, picks), lambda j: (j, 0)),
    ]
    return pl.pallas_call(
        functools.partial(inner_kernel, nseq=nseq, length=length),
        grid=(inner // WIDTH,),
        in_specs=specs,
        out_specs=[
            block_of(rows), block_of(halo.shape[0]), tiles_of(rows), block_of(rows),
            pl.BlockSpec((rows, picks), lambda j: (0, 0)),
        ],
        out_shape=(
            o((rows, inner), bf16), o((halo.shape[0], inner), bf16), o((inner // 128, rows, 128), bf16),
            o((rows, inner), f32), o((rows, picks), f32),
        ),
        scratch_shapes=[pltpu.VMEM((nseq, NL, PAD + length, 128), f32), pltpu.VMEM((rows, WIDTH), bf16)],
        compiler_params=pltpu.CompilerParams(vmem_limit_bytes=VMEM, dimension_semantics=("arbitrary",)),
        cost_estimate=pl.CostEstimate(flops=2 * rows * model * inner, bytes_accessed=14 * 2**20, transcendentals=0),
        name="inner_side",
    )(*operands)


def input_grad_kernel(
    place_ref, cp_ref, inner_ref, before_ref, x_ref, slope_ref, pg_ref, sw_ref, cw_ref, turned_ref, halo_ref, gain_ref,
    rl_ref, proj_ref, dlog_ref, rb_ref, sk_ref, *refs, nseq, length, part, rank, grp, last,
):
    if last:
        early_ref, kept_ref, sent_ref, igr_ref, tail_ref, head_ref, pre_ref, back_ref, vec_ref = refs
    else:
        early_ref, (kept_ref, sent_ref, igr_ref, tail_ref, head_ref, small_ref, pre_ref, back_ref, vec_ref) = None, refs
    taps = cw_ref.shape[0]
    j = pl.program_id(0)
    wide = pg_ref.shape[1]
    back_ref[...] = cp_ref[...] + rows_dot(pg_ref[:, wide // 2 :], sw_ref[...])
    vec_ref[...] = jnp.zeros_like(vec_ref)
    small_step = 32
    for s in range(nseq):
        pre_ref[s, :, :PAD, :] = jnp.zeros((NL, PAD, 128), f32)
        pre_ref[s, :, PAD + length :, :] = jnp.zeros((NL, PAD, 128), f32)

        def first(i, total):
            r = pl.multiple_of(i * small_step, small_step)
            at = pl.ds(pl.multiple_of(s * length + r, small_step), small_step)
            back = back_ref[at, :] * slope_ref[at, :]
            for l in range(NL):
                pre_ref[s, l, pl.ds(pl.multiple_of(r + PAD, PAD), small_step), :] = back[:, lane(l)]
            return total + sum(back[q * 8 : (q + 1) * 8] for q in range(small_step // 8))

        total = lax.fori_loop(0, length // small_step, first, jnp.zeros((8, WIDTH), f32))
        vec_ref[taps : taps + 1, :] += jnp.sum(total, axis=0, keepdims=True)

        def second(i, totals):
            r = pl.multiple_of(i * small_step, small_step)
            at = pl.ds(pl.multiple_of(s * length + r, small_step), small_step)
            sums = []
            for l in range(NL):
                inner = inner_ref[at, lane(l)].astype(f32)
                result = jnp.zeros((small_step, 128), f32)
                for k in range(taps):
                    later = pre_ref[s, l, pl.ds(r + PAD + taps - 1 - k, small_step), :]
                    result = result + cw_ref[k : k + 1, lane(l)] * later
                    product = inner * later
                    sums.append(
                        totals[l * taps + k] + sum(product[q * 8 : (q + 1) * 8] for q in range(small_step // 8))
                    )
                igr_ref[at, lane(l)] = result.astype(bf16)
            return tuple(sums)

        totals = lax.fori_loop(0, length // small_step, second, (jnp.zeros((8, 128), f32),) * (taps * NL))
        head_rows = lax.broadcasted_iota(jnp.int32, (PAD, 128), 0) < taps - 1
        for l in range(NL):
            late = pre_ref[s, l, length:, :]
            tail_ref[s * PAD : (s + 1) * PAD, lane(l)] = sum(
                cw_ref[k : k + 1, lane(l)] * late[taps - 1 - k : taps - 1 - k + PAD] for k in range(taps)
            )
            lead = pre_ref[s, l, : 2 * PAD, :]
            before = before_ref[s * PAD : (s + 1) * PAD, lane(l)].astype(f32)
            before = jnp.concatenate([before[PAD - taps + 1 :], jnp.zeros((PAD - taps + 1, 128), f32)], axis=0)
            head = jnp.zeros((PAD, 128), f32)
            for k in range(taps):
                early = jnp.where(head_rows, lead[PAD - k : 2 * PAD - k], 0.0)
                head = head + cw_ref[k : k + 1, lane(l)] * early
                vec_ref[k : k + 1, lane(l)] += jnp.sum(totals[l * taps + k] + before * early, axis=0, keepdims=True)
            head_ref[s * PAD : (s + 1) * PAD, lane(l)] = head

    vec_ref[taps + 1 : taps + 2, :] = rb_ref[0:1, :]
    vec_ref[taps + 2 : taps + 3, :] = sk_ref[0:1, :]
    vec_ref[8:, :] = dlog_ref[...]
    count = place_ref.shape[0] - 1
    rows_each = turned_ref.shape[0] // count
    rows_pad = padded(rows_each)
    before_normed = normalized(halo_ref[...], gain_ref[...])
    products = []
    for b in range(WIDTH // wide):
        cols = slice(b * wide, (b + 1) * wide)
        shifted = jnp.concatenate(
            [
                jnp.concatenate(
                    [jnp.zeros((PAD - taps + 1, wide), f32), head_ref[s * PAD : s * PAD + taps - 1, cols]], axis=0
                )
                for s in range(nseq)
            ],
            axis=0,
        )
        product = jnp.dot(turned_ref[...], igr_ref[:, cols], preferred_element_type=f32) + contract_rows(
            before_normed, shifted.astype(bf16)
        )
        products.append(product.astype(bf16) if rows_each == rows_pad else product)
    eye = (
        lax.broadcasted_iota(jnp.int32, (vec_ref.shape[0], wide), 0) + rank
        == lax.broadcasted_iota(jnp.int32, (vec_ref.shape[0], wide), 1)
    ).astype(bf16)
    low = jnp.concatenate([proj_ref[...], jnp.zeros((proj_ref.shape[0], wide - proj_ref.shape[1]), f32)], axis=1)
    low = jnp.where(lax.broadcasted_iota(jnp.int32, low.shape, 1) < rank, low, 0.0).astype(bf16)
    small = (
        contract_rows(joined(x_ref, slice(None)), pg_ref[...])
        + contract_rows(rl_ref[...], low)
        + contract_rows(vec_ref[...].astype(bf16), eye)
    )
    def store(flag):
        half = count // 2
        for q in range(count):
            ref = kept_ref if (q // grp) % 2 == flag else sent_ref
            spot = lax.rem(place_ref[q], half)
            for b, product in enumerate(products):
                at = pl.ds(pl.multiple_of((j * len(products) + b) * rows_pad, rows_pad), rows_pad)
                ref[spot, at, :] = share_rows(product, q, rows_each)

    core = place_ref[count]
    for flag in range(2):
        pl.when(core == flag)(functools.partial(store, flag))
    if not last:
        small_ref[...] = small.astype(small_ref.dtype)
        return
    base = kept_ref.shape[1] - padded(part)

    def place_small(values, first):
        for q in range(WIDTH // part):
            share = place_ref[first + q]
            rows = share_rows(values, q, part)

            @pl.when(share < count // 2)
            def _():
                kept_ref[share, base : base + padded(part), :] = rows

            @pl.when(share >= count // 2)
            def _():
                sent_ref[share - count // 2, base : base + padded(part), :] = rows

    steps = pl.num_programs(0)
    place_small(early_ref[...], j * (WIDTH // part))
    place_small(small, (steps + j) * (WIDTH // part))


def input_grads(
    place, cp, inner, before, x, slope, pg, select_weight, conv_weight, turned, halo, gain, rate_low, proj,
    decay_grad, rate_bias_grad, skip_grad, early, nseq, length, part, rank, grp,
):
    rows, width = cp.shape
    width = width // 2
    last = early is not None
    first = width // WIDTH if last else 0
    wide = pg.shape[1]
    count = place.shape[0] - 1
    model = turned.shape[0]
    packed_rows = (width // wide) * padded(model // count) + (padded(part) if last else 0)
    o = jax.ShapeDtypeStruct

    def drop(spec, first=0):
        return pl.BlockSpec(
            spec.block_shape, lambda j, _, f=spec.index_map: f(j + first), pipeline_mode=spec.pipeline_mode
        )

    specs = [
        block_of(rows), block_of(rows), block_of(before.shape[0]), tiles_of(rows), block_of(rows), whole(pg),
        pl.BlockSpec((WIDTH, wide // 2), lambda j: (j, 0)), block_of(conv_weight.shape[0]), whole(turned),
        whole(halo), whole(gain), block_of(rows), whole(proj), block_of(N), block_of(8), block_of(8),
    ]
    packed = pl.BlockSpec((count // 2, packed_rows, wide), lambda j: (0, 0, 0))
    out_specs = [packed, packed, block_of(rows), block_of(nseq * PAD), block_of(nseq * PAD)]
    outs = [
        o((count // 2, packed_rows, wide), bf16), o((count // 2, packed_rows, wide), bf16), o((rows, width), bf16),
        o((nseq * PAD, width), f32), o((nseq * PAD, width), f32),
    ]
    operands = [
        place, cp, inner, before, x, slope, pg, select_weight, conv_weight, turned, halo, gain, rate_low, proj,
        decay_grad, rate_bias_grad, skip_grad,
    ]
    in_specs = [drop(s, first) for s in specs]
    block = pl.BlockSpec((WIDTH, wide), lambda j: (j, 0))
    if last:
        operands.append(early)
        in_specs.append(drop(block))
    else:
        out_specs.append(block)
        outs.append(o((width, wide), f32 if part < 16 else bf16))
    return pl.pallas_call(
        functools.partial(input_grad_kernel, nseq=nseq, length=length, part=part, rank=rank, grp=grp, last=last),
        grid_spec=pltpu.PrefetchScalarGridSpec(
            num_scalar_prefetch=1,
            grid=(width // WIDTH,),
            in_specs=in_specs,
            out_specs=[drop(s) for s in out_specs],
            scratch_shapes=[
                pltpu.VMEM((nseq, NL, PAD + length + PAD, 128), f32), pltpu.VMEM((rows, WIDTH), f32),
                pltpu.VMEM((8 + N, WIDTH), f32),
            ],
        ),
        out_shape=outs,
        compiler_params=pltpu.CompilerParams(vmem_limit_bytes=VMEM, dimension_semantics=("arbitrary",)),
        cost_estimate=pl.CostEstimate(flops=24 * rows * width * model, bytes_accessed=16 * 2**20, transcendentals=0),
        name="input_grads",
    )(*operands)


def padded(rows):
    return max(rows, 16)


def share_rows(values, share, rows):
    taken = values[share * rows : (share + 1) * rows]
    if rows < padded(rows):
        taken = jnp.concatenate([taken, jnp.zeros((padded(rows) - rows, values.shape[1]), values.dtype)], axis=0)
    return taken.astype(bf16)


def weight_grad_kernel(gated_ref, gate_ref, cot_ref, turned_ref, packed_ref, *, part):
    j = pl.program_id(0)
    count = packed_ref.shape[0]
    model = cot_ref.shape[1]
    rows_each = model // count
    rows_pad = padded(rows_each)
    product = contract_rows(gated_ref[...], cot_ref[...])
    for q in range(WIDTH // part):
        packed_ref[j * (WIDTH // part) + q, : padded(part), :] = share_rows(product, q, part)
    product = jnp.dot(turned_ref[...], gate_ref[...], preferred_element_type=f32)
    each = model // WIDTH
    at = pl.ds(pl.multiple_of(padded(part) + (j // each) * rows_pad, 16), rows_pad)
    cols = pl.ds(pl.multiple_of((j % each) * WIDTH, WIDTH), WIDTH)
    for q in range(count):
        packed_ref[q, at, cols] = share_rows(product, q, rows_each)


def weight_grads(gated, gate_grad, cot, turned, part):
    rows, width = gated.shape
    model = cot.shape[1]
    count = width // part
    packed_rows = padded(part) + (width // model) * padded(model // count)
    return pl.pallas_call(
        functools.partial(weight_grad_kernel, part=part),
        grid=(width // WIDTH,),
        in_specs=[block_of(rows), block_of(rows), whole(cot), whole(turned)],
        out_specs=pl.BlockSpec((count, packed_rows, model), lambda j: (0, 0, 0)),
        out_shape=jax.ShapeDtypeStruct((count, packed_rows, model), bf16),
        compiler_params=pltpu.CompilerParams(vmem_limit_bytes=VMEM, dimension_semantics=("arbitrary",)),
        cost_estimate=pl.CostEstimate(flops=4 * rows * width * model, bytes_accessed=14 * 2**20, transcendentals=0),
        name="weight_grads",
    )(gated, gate_grad, cot, turned)


def flip_bit(axis, bit):
    return [(i, i ^ bit) for i in range(lax.axis_size(axis))]


def bits_of(axis):
    size = lax.axis_size(axis)
    return [(axis, 1 << k) for k in range(size.bit_length() - 1)]


def places(order):
    grp = lax.axis_size("grp")
    other = jnp.arange(lax.axis_size("seq") * grp) ^ (lax.axis_index("seq") * grp + lax.axis_index("grp"))
    position = jnp.zeros_like(other)
    for axis, bit in order:
        position = 2 * position + (other // (bit * grp if axis == "seq" else bit)) % 2
    return position.astype(jnp.int32)


def pairs_of(bits):
    return [bits[i : i + 2] for i in range(0, len(bits), 2)]


def round_parts(held, bits):
    count = 1 << len(bits)
    size = held[0].shape[0] // count
    parts = [sum(h[i * size : (i + 1) * size].astype(f32) for h in held) for i in range(count)]
    return parts[:1] + [part.astype(bf16) for part in parts[1:]]


def round_trade(parts, bits):
    held = parts[:1]
    for i in range(1, len(parts)):
        flip = sum(bit for at, (axis, bit) in enumerate(bits) if (i >> (len(bits) - 1 - at)) & 1)
        held.append(lax.ppermute(parts[i], bits[0][0], flip_bit(bits[0][0], flip)))
    return held


def sum_packed(kept, sent, rounds, later):
    axis, bit = rounds[0][0]
    held = [kept, lax.ppermute(sent, axis, flip_bit(axis, bit))]
    for bits in rounds[1:]:
        parts = round_parts(held, bits)
        if later is not None:
            *parts, later = lax.optimization_barrier((*parts, later))
        held = round_trade(parts, bits)
    return held, later


def sum_rounds(held, rounds):
    for bits in rounds:
        held = round_trade(round_parts(held, bits), bits)
    return sum(h[0].astype(f32) for h in held)


def carried(block, shape, rates, backward, after=None, spans=None):
    count, mine = lax.axis_size("seq"), lax.axis_index("seq")
    blocks = lax.all_gather(block.astype(bf16), "seq")
    if after is not None:
        blocks, after = lax.optimization_barrier((blocks, after))
    rows = shape[0] * shape[1]
    entering = jnp.zeros(shape, f32)
    for turn in range(count - 1):
        j = count - 1 - turn if backward else turn
        theirs = blocks[j].astype(f32)
        span = (theirs if spans is None else spans[j].astype(f32))[rows : rows + 2 * shape[0]]
        span = span[: shape[0]] + span[shape[0] :]
        longer = jnp.exp(span[:, None, :] * rates) * entering + theirs[:rows].reshape(shape)
        entering = jnp.where(mine < j if backward else j < mine, longer, entering)
    return entering, after, blocks


def contract_rows(left, right, kind=f32):
    return lax.dot_general(left, right, (((0,), (0,)), ((), ())), preferred_element_type=f32).astype(kind)


def shards(
    tokens,
    cotangent,
    norm_gain,
    in_weight,
    conv_weight,
    conv_bias,
    select_weight,
    rate_weight,
    rate_bias,
    decay_log,
    skip_gain,
    out_weight,
):
    nseq, length, model = tokens.shape
    inner_width = out_weight.shape[0]
    rank = rate_weight.shape[0]
    taps = conv_weight.shape[0]
    rows = nseq * length
    share_count = lax.axis_size("seq") * lax.axis_size("grp")
    tok = tokens.reshape(rows, model)
    cot = cotangent.reshape(rows, model)
    gain, skip, bias = norm_gain[None], skip_gain[None], conv_bias[None]
    pieces, grp = lax.axis_size("seq"), lax.axis_size("grp")
    halo = lax.ppermute(tokens[:, length - PAD :], "seq", [(i, i + 1) for i in range(pieces - 1)])
    halo = halo.reshape(nseq * PAD, model)
    normed, turned, scale, g, ga, gs = gate_side(tok, gain, cot, in_weight, out_weight)
    picks, wide = rank + 2 * N, 256
    select_weight = jnp.pad(select_weight, ((0, 0), (0, wide // 2 - picks)))
    inner, before, x, slope, proj = inner_side(
        normed, halo, gain, in_weight, conv_weight, bias, select_weight, nseq, length
    )
    in_gate, out_gate = proj[:, rank : rank + N], proj[:, rank + N : picks]
    log = decay_log.T
    rates = -jnp.exp(log)
    bb = jnp.broadcast_to(in_gate[:, :, None], (rows, N, 128))
    ahead, dl, u = state_end(proj, rate_weight, rate_bias[None], x, log, bb, nseq, length)
    ahead, g = lax.optimization_barrier((ahead.astype(bf16), g))
    state_shape = (nseq, N, inner_width)
    entering, _, spans = carried(ahead, state_shape, rates, False)
    cb = jnp.broadcast_to(out_gate[:, :, None], (rows, N, 128))
    sent_back = adjoint_end(dl, g, log, cb, nseq, length)
    lc = spread(out_gate, nseq, length, 1, False)
    lb = spread(in_gate, nseq, length, 2, True)
    ls = jnp.asarray(own_column(nseq * T, T, nseq, 2, 1, True))
    meet = jnp.sum(in_gate * out_gate, axis=1, keepdims=True)
    bc = jnp.broadcast_to(meet, (rows, 128))
    behind, lb, ls, u = lax.optimization_barrier((sent_back, lb, ls, u))
    states, gated, gate_grad, out_grad, shift, skip_grad = forward(
        dl, u, g, ga, gs, x, skip, bb, bc, lc, log, entering, nseq, length, 4
    )
    part, part_rows = inner_width // share_count, model // share_count
    weight_packed = weight_grads(gated, gate_grad, cot, turned, part)
    leaving, weight_packed, _ = carried(behind, state_shape, rates, True, weight_packed, spans)
    weight_sum = lax.psum_scatter(weight_packed, "seq", scatter_dimension=0, tiled=True)
    rate_low, conv_part, in_grad, decay_grad, rate_bias_grad = backward(
        dl, u, g, x, skip, cb, lb, ls, log, leaving, states, nseq, length, 4
    )
    out_grad = out_grad.reshape(rows, N) + in_gate * jnp.sum(shift, axis=1, keepdims=True)
    rank_grad = rows_dot(rate_low, rate_weight)
    pg = jnp.concatenate(
        [
            jnp.zeros((rows, wide // 2), bf16),
            rank_grad.astype(bf16),
            in_grad.reshape(rows, N).astype(bf16),
            out_grad.astype(bf16),
            jnp.zeros((rows, wide // 2 - picks), bf16),
        ],
        axis=1,
    )
    seq_bits, grp_bits = bits_of("seq"), bits_of("grp")
    order = seq_bits + grp_bits
    place = jnp.concatenate([places(order), (lax.axis_index("seq") % 2)[None].astype(jnp.int32)])
    rounds = [seq_bits[:1]] + pairs_of(seq_bits[1:]) + pairs_of(grp_bits)
    half_width = inner_width // 2

    def half(conv_part, early):
        return input_grads(
            place, conv_part, inner, before, x, slope, pg, select_weight, conv_weight, turned, halo, gain, rate_low,
            proj, decay_grad, rate_bias_grad, skip_grad, early, nseq, length, part, rank, grp,
        )

    wide_tok = tok.astype(f32)
    kept, sent, first_grad, first_tail, first_head, early = half(conv_part, None)
    sent, gated = lax.optimization_barrier((sent, gated))
    block_out = wide_tok + jnp.dot(gated, out_weight, preferred_element_type=f32)
    first_held, (conv_part, block_out) = sum_packed(kept, sent, rounds[:2], (conv_part, block_out))
    kept, sent, second_grad, second_tail, second_head = half(conv_part, early)
    head = jnp.concatenate([first_head, second_head], axis=1)
    *first_held, sent, head = lax.optimization_barrier((*first_held, sent, head))
    head = head.reshape(nseq, PAD, inner_width)[:, : taps - 1].astype(bf16)
    returned = lax.ppermute(head, "seq", [(i + 1, i) for i in range(pieces - 1)]).astype(f32)
    held, (returned, gate_grad, first_grad, weight_sum) = sum_packed(
        kept, sent, rounds[:2], (returned, gate_grad, first_grad, weight_sum)
    )
    first_held = sum_rounds(first_held, rounds[2:])
    held = sum_rounds(held, rounds[2:])
    weight_share = lax.psum_scatter(weight_sum, "grp", scatter_dimension=0, tiled=True)[0].astype(f32)
    out_share = weight_share[:part]
    gate_share = weight_share[padded(part) :].reshape(-1, padded(part_rows), model)[:, :part_rows]
    gate_share = gate_share.transpose(1, 0, 2).reshape(part_rows, inner_width)
    blocks = half_width // wide

    def in_rows(held):
        share = held[: blocks * padded(part_rows)].reshape(blocks, padded(part_rows), wide)[:, :part_rows]
        return share.transpose(1, 0, 2).reshape(part_rows, half_width)

    inner_share = jnp.concatenate([in_rows(first_held), in_rows(held)], axis=1)
    small = held[blocks * padded(part_rows) :][:part]
    inner_grad = jnp.concatenate([first_grad, second_grad], axis=1)
    tail = jnp.concatenate([first_tail, second_tail], axis=1)
    fixed = (tail.reshape(nseq, PAD, inner_width)[:, PAD - taps + 1 :] + returned).astype(bf16)
    inner_grad = (
        inner_grad.reshape(nseq, length, inner_width).at[:, length - taps + 1 :].set(fixed).reshape(rows, inner_width)
    )
    scale = scale[:, :1]
    normed_grad = rows_dot(gate_grad, in_weight[:, inner_width:]) + rows_dot(inner_grad, in_weight[:, :inner_width])
    lifted = normed_grad * norm_gain
    dots = jnp.mean(lifted * wide_tok, axis=1, keepdims=True)
    tokens_grad = cot.astype(f32) + scale * lifted - wide_tok * (scale * scale * scale) * dots
    in_share = jnp.concatenate([inner_share, gate_share], axis=1)
    first = (lax.axis_index("seq") * grp + lax.axis_index("grp")) * part_rows
    own_weight = lax.dynamic_slice_in_dim(in_weight, first, part_rows, 0).astype(f32)
    own_gain = lax.dynamic_slice_in_dim(norm_gain, first, part_rows, 0)
    gain_share = jnp.sum(own_weight * in_share, axis=1) / own_gain
    vectors = small[:, rank : rank + 8].T
    return (
        block_out.astype(bf16).reshape(tokens.shape),
        tokens_grad.astype(bf16).reshape(tokens.shape),
        gain_share,
        in_share,
        vectors[:taps],
        vectors[taps],
        small[:, wide // 2 : wide // 2 + picks],
        small[:, :rank].T,
        vectors[taps + 1],
        small[:, rank + 8 : rank + 8 + N],
        vectors[taps + 2],
        out_share,
    )


def solution(mesh):
    sharded = P("grp", "seq", None)
    shares = ("seq", "grp")
    return jax.shard_map(
        shards,
        mesh=mesh,
        in_specs=(sharded, sharded) + (P(),) * 10,
        out_specs=(
            sharded,
            sharded,
            P(shares),
            P(shares, None),
            P(None, shares),
            P(shares),
            P(shares, None),
            P(None, shares),
            P(shares),
            P(shares, None),
            P(shares),
            P(shares, None),
        ),
        check_vma=False,
    )
```

time: 329 us -> 286 us (0.87)
  waiting for transfers between devices: 42.4 us -> 26.1 us
  other arithmetic: 34.4 us -> 21 us
  local copies, waits for them, and re-layouts: 26.7 us -> 16.1 us
  Pallas kernels: 174 us -> 166 us
  starting transfers between devices: 13.9 us -> 20.9 us
    ppermute x9 -> x15, waiting for transfers between devices: 36.9 us -> 18.9 us  [the longest x12 18.9 us: round_trade(): held.append(lax.ppermute(parts[i], bits[0][0], flip_bit(bits[0][0], flip)))]
    slice x11 -> x5, local copies, waits for them, and re-layouts: 9.38 us -> 0.78 us  [the longest x1 0.62 us: shards(): small[:, wide // 2:wide // 2 + picks]]
    ppermute x9 -> x15, starting transfers between devices: 11 us -> 18.2 us  [the longest x12 16.4 us: round_trade(): held.append(lax.ppermute(parts[i], bits[0][0], flip_bit(bits[0][0], flip)))]
    convert_element_type x9, other arithmetic: 14.5 us -> 8.13 us  [the longest x4 4.38 us: round_parts(): return parts[:1] + [part.astype(bf16) for part in parts[1:]]]
    add x15 -> x6, other arithmetic: 5.89 us -> 1.2 us  [the longest x2 1.12 us: sum_rounds(): return sum((h[0].astype(f32) for h in held))]
    pallas_call x5, Pallas kernels: 127 us -> 122 us  [kernel_call(): pl.pallas_call(functools.partial(body, **options), grid=(channels // WIDT...]
    pallas_call x1 -> x2, Pallas kernels: 24.3 us -> 23.1 us  [input_grads(): pl.pallas_call(functools.partial(input_grad_kernel, nseq=nseq, length=len...]
  transfers between devices with their start and end apart: 14 -> 20, of which waited for: 8 -> 8; matrix products, arithmetic and copies ran while one was open for 17% -> 16% of each run, Pallas kernels for 43% -> 48%
where the time goes in v1:
time: 286 us; the launch traced here: 285 us
  Pallas kernels  166 us (58%)
  waiting for transfers between devices  26.1 us (9%)
  other arithmetic  21 us (7%)
  starting transfers between devices  20.9 us (7%)
  matrix products  20.1 us (7%)
  local copies, waits for them, and re-layouts  16.1 us (6%)
  between operations  14.5 us (5%)
    pallas_call x5, Pallas kernels, kernel_call(): pl.pallas_call(functools.partial(body, **options), grid=(channels // WIDT...  122 us
    pallas_call x2, Pallas kernels, input_grads(): pl.pallas_call(functools.partial(input_grad_kernel, nseq=nseq, length=len...  23.1 us
    ppermute x12, waiting for transfers between devices, round_trade(): held.append(lax.ppermute(parts[i], bits[0][0], flip_bit(bits[0][0], flip)))  18.9 us
    ppermute x12, starting transfers between devices, round_trade(): held.append(lax.ppermute(parts[i], bits[0][0], flip_bit(bits[0][0], flip)))  16.4 us
    dot_general x3, matrix products, rows_dot(): lax.dot_general(left, right, (((1,), (1,)), ((), ())), preferred_element_...  12.1 us
    pallas_call x1, Pallas kernels, inner_side(): pl.pallas_call(functools.partial(inner_kernel, nseq=nseq, length=length),...  10.5 us
    pallas_call x1, Pallas kernels, weight_grads(): pl.pallas_call(functools.partial(weight_grad_kernel, part=part), grid=(wi...  10.4 us
    all_gather x2, waiting for transfers between devices, carried(): blocks = lax.all_gather(block.astype(bf16), 'seq')  7.13 us
  transfers between devices with their start and end apart: 20, of which 8 were waited for; matrix products, arithmetic and copies ran while one was open for 16% of the time, Pallas kernels for 48%

profile of v1, /device:TPU:0, one launch (start us, length us, event | category | flops | bytes accessed | tf_op | source)
XLA Modules:
  0.0 285.2 jit_solution(1021695571161707540)
XLA Ops:
  8.0 2.3 collective-permute-start
  10.4 14.3 %gate_side.1 = (bf16[512,1024]{1,0:T(8,128)(2,1)}, bf16[1024,512]{1,0:T(8,128)(2,1)}, f32[512,128]{1,0:T(8,128)}, f32[16,512,128]{2,1,0:T(8,128)}, f32[16,512,128]{2,1,0:T(8,128)}, /*index=5*/f32[16,512,128]{2,1,0:T(8,128)}) custom-call(bf16[512,1024]{1,0:T(8,128)(2,1)} %bitcast.133, f32[1,1024]{1,0:T(1,128)} %bitcast.173, bf16[512,1024]{1,0:T(8,128)(2,1)} %bitcast.141, ...), custom_call_target="tpu_custom_call" | custom-call | flops 4294967296 | bytes 29626368 | tf_op jit(solution)/shard_map/gate_side/pallas_call | solution.py:293
  26.5 10.5 %inner_side.1 = (bf16[512,2048]{1,0:T(8,128)(2,1)}, bf16[16,2048]{1,0:T(8,128)(2,1)}, bf16[16,512,128]{2,1,0:T(8,128)(2,1)}, f32[512,2048]{1,0:T(8,128)}, f32[512,128]{1,0:T(8,128)}) custom-call(bf16[512,1024]{1,0:T(8,128)(2,1)} %get-tuple-element.90.normed_ref, bf16[16,1024]{1,0:T(8,128)(2,1)} %bitcast.169, f32[1,1024]{1,0:T(1,128)} %bitcast.174, ...), custom_call_target="tpu_custom_call" | custom-call | flops 2147483648 | bytes 14680064 | tf_op jit(solution)/shard_map/inner_side/pallas_call | solution.py:510
  37.0 1.3 multiply_reduce_fusion.1
  38.3 2.6 broadcast_in_dim.24.bb_ref
  41.0 19.4 %state_end.1 = (f32[48,2048]{1,0:T(8,128)}, f32[16,512,128]{2,1,0:T(8,128)}, f32[16,512,128]{2,1,0:T(8,128)}) custom-call(f32[512,128]{1,0:T(8,128)} %get-tuple-element.91.proj_ref, bf16[64,2048]{1,0:T(8,128)(2,1)} %rw_ref.1, f32[1,2048]{1,0:T(1,128)} %bitcast.177, bf16[16,512,128]{2,1,0:T(8,128)(2,1)} %get-tuple-element.92.x_ref, f32[16,2048]{1,0:T(8,128)} %bitcast.165, ...), custom_call_target="tpu_custom_call" | custom-call | flops 20000000000 | bytes 15736832 | tf_op jit(solution)/shard_map/state_end/pallas_call | solution.py:293
  60.3 1.7 convert_element_type.325
  62.2 1.4 fusion.10.lb_ref
  63.6 2.6 broadcast_in_dim.25.cb_ref
  66.2 15.9 %adjoint_end.1 = bf16[32,2048]{1,0:T(8,128)(2,1)} custom-call(f32[16,512,128]{2,1,0:T(8,128)} %get-tuple-element.93.dl_ref, f32[16,512,128]{2,1,0:T(8,128)} %get-tuple-element.96.g_ref, f32[16,2048]{1,0:T(8,128)} %bitcast.166, f32[512,16,128]{2,1,0:T(8,128)} %broadcast_in_dim.25.cb_ref), custom_call_target="tpu_custom_call" | custom-call | flops 20000000000 | bytes 12845056 | tf_op jit(solution)/shard_map/adjoint_end/pallas_call | solution.py:293
  82.1 1.1 fusion.11.lc_ref
  83.3 7.1 %all-gather.5.cloned.1.call-done = bf16[384,2048]{1,0:T(8,128)(2,1)} async-done(((bf16[48,2048]{1,0:T(8,128)(2,1)}), bf16[384,2048]{1,0:T(8,128)(2,1)}) %all-gather.5.cloned.1.call-update) | async-done | bytes 1572880 | tf_op jit(solution)/shard_map/all_gather | solution.py:823
  90.4 1.8 fusion.21
  92.6 1.1 add_select_fusion.hin_ref
  94.5 33.2 %forward.1 = (bf16[8192,2048]{1,0:T(8,128)(2,1)}, bf16[512,2048]{1,0:T(8,128)(2,1)}, bf16[512,2048]{1,0:T(8,128)(2,1)}, f32[32,256]{1,0:T(8,128)}, f32[512,128]{1,0:T(8,128)}, /*index=5*/f32[8,2048]{1,0:T(8,128)}) custom-call(f32[16,512,128]{2,1,0:T(8,128)} %get-tuple-element.93.dl_ref, f32[16,512,128]{2,1,0:T(8,128)} %get-tuple-element.98.u_ref, ...), custom_call_target="tpu_custom_call" | custom-call | flops 30000001024 | bytes 66560000 | tf_op jit(solution)/shard_map/forward/pallas_call | solution.py:293
  127.7 10.4 %weight_grads.1 = bf16[32,128,1024]{2,1,0:T(8,128)(2,1)} custom-call(bf16[512,2048]{1,0:T(8,128)(2,1)} %get-tuple-element.124.gated_ref, bf16[512,2048]{1,0:T(8,128)(2,1)} %get-tuple-element.141.gate_ref, bf16[512,1024]{1,0:T(8,128)(2,1)} %bitcast.142, bf16[1024,512]{1,0:T(8,128)(2,1)} %get-tuple-element.107.turned_ref), custom_call_target="tpu_custom_call" | custom-call | flops 4294967296 | bytes 14680064 | tf_op jit(solution)/shard_map/weight_grads/pallas_call | solution.py:755
  139.3 1.1 fusion.13.lin_ref
  140.5 39.8 %backward.1 = (bf16[512,2048]{1,0:T(8,128)(2,1)}, f32[512,2048]{1,0:T(8,128)}, f32[32,256]{1,0:T(8,128)}, f32[16,2048]{1,0:T(8,128)}, f32[8,2048]{1,0:T(8,128)}) custom-call(f32[16,512,128]{2,1,0:T(8,128)} %get-tuple-element.93.dl_ref, f32[16,512,128]{2,1,0:T(8,128)} %get-tuple-element.98.u_ref, f32[16,512,128]{2,1,0:T(8,128)} %get-tuple-element.96.g_ref, ...), custom_call_target="tpu_custom_call" | custom-call | flops 49999998976 | bytes 60465152 | tf_op jit(solution)/shard_map/backward/pallas_call | solution.py:293
  180.3 2.5 convolution_convert_fusion.2
  183.5 1.0 concatenate.21.pg_ref
  184.4 11.4 %input_grads.2 = (bf16[16,128,256]{2,1,0:T(8,128)(2,1)}, bf16[16,128,256]{2,1,0:T(8,128)(2,1)}, bf16[512,1024]{1,0:T(8,128)(2,1)}, f32[16,1024]{1,0:T(8,128)}, f...) custom-call(s32[33]{0:T(128)} %pad_add_fusion.place_ref, f32[512,2048]{1,0:T(8,128)} %get-tuple-element.127.cp_ref, ...), custom_call_target="tpu_custom_call" | custom-call | flops 12884901888 | bytes 16777216 | tf_op jit(solution)/shard_map/input_grads/pallas_call | solution.py:703
  196.2 5.5 %convert_add_fusion = bf16[512,1024]{1,0:T(8,128)(2,1)} fusion(bf16[512,1024]{1,0:T(8,128)(2,1)S(1)} %bitcast.134, bf16[512,2048]{1,0:T(8,128)(2,1)S(1)} %copy-done.24, bf16[2048,1024]{1,0:T(8,128)(2,1)} %ow_ref.1), kind=kOutput, calls=%fused_computation.6 | convolution fusion | flops 2149056512 | bytes 8388608 | tf_op jit(solution)/shard_map/dot_general | solution.py:927
  202.0 1.4 collective-permute-start.2
  203.8 1.7 collective-permute-start.4
  205.6 11.7 %input_grads.3 = (bf16[16,192,256]{2,1,0:T(8,128)(2,1)}, bf16[16,192,256]{2,1,0:T(8,128)(2,1)}, bf16[512,1024]{1,0:T(8,128)(2,1)}, f32[16,1024]{1,0:T(8,128)}, f32[16,1024]{1,0:T(8,128)}) custom-call(s32[33]{0:T(128)} %pad_add_fusion.place_ref, f32[512,2048]{1,0:T(8,128)} %get-tuple-element.127.cp_ref, bf16[512,2048]{1,0:T(8,128)(2,1)} %get-tuple-element.111.inner_ref, ...), custom_call_target="tpu_custom_call" | custom-call | flops 12884901888 | bytes 16777216 | tf_op jit(solution)/shard_map/input_grads/pallas_call | solution.py:703
  217.3 1.0 pad_maximum_fusion.1
  218.3 1.8 collective-permute-done.4
  220.3 1.5 collective-permute-start.6
  221.9 2.5 collective-permute-start.7
  224.4 1.5 collective-permute-start.8
  227.3 1.9 collective-permute-done.7
  229.7 2.6 collective-permute-done.9
  232.4 2.6 add_convert_fusion
  235.0 2.4 collective-permute-start.10
  238.0 0.9 collective-permute-start.12
  239.0 1.7 pad_maximum_fusion
  241.0 4.8 %fusion = f32[512,1024]{1,0:T(8,128)S(1)} fusion(bf16[512,2048]{1,0:T(8,128)(2,1)S(1)} %bitcast.132, bf16[1024,4096]{1,0:T(8,128)(2,1)} %wi_ref.1), kind=kOutput, calls=%fused_computation | convolution fusion | flops 2147483648 | bytes 8388608 | tf_op jit(solution)/shard_map/dot_general | solution.py:44
  245.9 4.8 %fusion.7 = (f32[512]{0:T(512)S(1)}, f32[512,1024]{1,0:T(8,128)S(1)}) fusion(bf16[2,256,1024]{2,1,0:T(8,128)(2,1)S(1)} %copy-done.3, f32[1024]{0:T(1024)S(1)} %copy-done.22, f32[512,1024]{1,0:T(8,128)S(1)} %fusion, bf16[512,2048]{1,0:T(8,128)(2,1)S(1)} %copy-done.23, bf16[1024,4096]{1,0:T(8,128)(2,1)} %wi_ref.1), kind=kOutput, calls=%fused_computation.10 | convolution fusion | flops 2150104576 | bytes 11540480 | tf_op jit(solution)/shard_map/dot_general | solution.py:44
  250.7 5.1 %collective-permute-done.12 = bf16[4,192,256]{2,1,0:T(8,128)(2,1)} collective-permute-done((bf16[4,192,256]{2,1,0:T(8,128)(2,1)}, bf16[4,192,256]{2,1,0:T(8,128)(2,1)}, u32[]{:S(2)}, u32[]{:S(2)}) %collective-permute-start.12) | collective-permute-done | bytes 393248 | tf_op jit(solution)/shard_map/ppermute | solution.py:800
  255.7 1.4 add_convert_fusion.9
  257.1 2.6 collective-permute-start.13
  259.7 1.9 collective-permute-start.15
  261.6 1.6 fusion.6
  263.2 4.1 %collective-permute-done.13 = bf16[1,192,256]{2,1,0:T(8,128)(2,1)S(1)} collective-permute-done((bf16[1,192,256]{2,1,0:T(8,128)(2,1)S(1)}, bf16[1,192,256]{2,1,0:T(8,128)(2,1)S(1)}, u32[]{:S(2)}, u32[]{:S(2)}) %collective-permute-start.13) | collective-permute-done | bytes 98336 | tf_op jit(solution)/shard_map/ppermute | solution.py:800
  267.3 2.9 %collective-permute-done.15 = bf16[1,192,256]{2,1,0:T(8,128)(2,1)S(1)} collective-permute-done((bf16[1,192,256]{2,1,0:T(8,128)(2,1)S(1)}, bf16[1,192,256]{2,1,0:T(8,128)(2,1)S(1)}, u32[]{:S(2)}, u32[]{:S(2)}) %collective-permute-start.15) | collective-permute-done | bytes 98336 | tf_op jit(solution)/shard_map/ppermute | solution.py:800
  270.2 1.1 convert_add_fusion.10
  274.9 1.0 slice.587
  276.0 1.3 multiply_reduce_fusion
  (132 shorter events, 15.0 us)
Async XLA Ops:
  7.2 83.3 %all-gather.5.cloned.1.call-start = ((), (), s32[]{:S(2)}) async-start(), calls=%async_computation.4 | async-start | bytes 1769472 | tf_op jit(solution)/shard_map/all_gather | solution.py:823
  8.0 17.9 %collective-permute-start = (bf16[2,8,1024]{2,1,0:T(8,128)(2,1)S(1)}, bf16[2,8,1024]{2,1,0:T(8,128)(2,1)S(1)}, u32[]{:S(2)}, u32[]{:S(2)}) collective-permute-start(bf16[2,8,1024]{2,1,0:T(8,128)(2,1)S(1)} %slice.419), channel_id=1, source_target_pairs={{0,4},{4,8},{8,12},{12,16},{16,20},{20,24},{24,28},{1,5},{5,9},{9,... | collective-permute-start | bytes 98312 | tf_op jit(solution)/shard_map/ppermute | solution.py:866
  10.3 14.3 %copy-start.11 = (bf16[2048,96]{0,1:T(8,128)(2,1)S(1)}, bf16[2048,96]{0,1:T(8,128)(2,1)}, u32[]{:S(2)}) copy-start(bf16[2048,96]{0,1:T(8,128)(2,1)} %param.25) | copy-start | bytes 1179652
  25.9 0.6 copy-start.17
  41.0 21.1 %copy-start.15 = (f32[2048,16]{0,1:T(8,128)S(1)}, f32[2048,16]{0,1:T(8,128)}, u32[]{:S(2)}) copy-start(f32[2048,16]{0,1:T(8,128)} %param.28) | copy-start | bytes 393220
  41.0 21.2 %copy-start = (f32[512,128]{1,0:T(8,128)S(1)}, f32[512,128]{1,0:T(8,128)}, u32[]{:S(2)}) copy-start(f32[512,128]{1,0:T(8,128)} %get-tuple-element.91.proj_ref) | copy-start | bytes 786436
  41.0 21.2 %copy-start.4 = (bf16[512,1024]{1,0:T(8,128)(2,1)S(1)}, bf16[512,1024]{1,0:T(8,128)(2,1)}, u32[]{:S(2)}) copy-start(bf16[512,1024]{1,0:T(8,128)(2,1)} %constant.164.clone) | copy-start | bytes 3145732
  41.0 21.2 %copy-start.18 = (bf16[16,1024]{1,0:T(8,128)(2,1)S(1)}, bf16[16,1024]{1,0:T(8,128)(2,1)}, u32[]{:S(2)}) copy-start(bf16[16,1024]{1,0:T(8,128)(2,1)} %constant.163.clone) | copy-start | bytes 98308
  62.0 76.0 %all-gather.7.cloned.1.call-start = ((), (), s32[]{:S(2)}) async-start(), calls=%async_computation.5 | async-start | bytes 1179648 | tf_op jit(solution)/shard_map/all_gather | solution.py:823
  66.2 15.9 %copy-start.10 = (bf16[512,512]{1,0:T(8,128)(2,1)S(1)}, bf16[512,512]{1,0:T(8,128)(2,1)}, u32[]{:S(2)}) copy-start(bf16[512,512]{1,0:T(8,128)(2,1)} %constant.162.clone) | copy-start | bytes 1572868
  66.2 15.9 %copy-start.21 = (bf16[16,512]{1,0:T(8,128)(2,1)S(1)}, bf16[16,512]{1,0:T(8,128)(2,1)}, u32[]{:S(2)}) copy-start(bf16[16,512]{1,0:T(8,128)(2,1)} %constant.161.clone) | copy-start | bytes 49156
  83.3 151.7 %reduce-scatter.3.cloned.1.call-start = ((), (), s32[]{:S(2)}) async-start(), calls=%async_computation.2 | async-start | bytes 9437184 | tf_op jit(solution)/shard_map/reduce_scatter | solution.py:896
  138.0 0.9 copy-start.19
  138.0 1.2 copy-start.9
  138.1 136.8 %reduce-scatter.5.cloned.1.call-start = ((), (), s32[]{:S(2)}) async-start(), calls=%async_computation.3 | async-start | bytes 1310720 | tf_op jit(solution)/shard_map/reduce_scatter | solution.py:939
  140.5 39.8 %copy-start.12 = (bf16[64,2048]{1,0:T(8,128)(2,1)S(1)}, bf16[64,2048]{1,0:T(8,128)(2,1)}, u32[]{:S(2)}) copy-start(bf16[64,2048]{1,0:T(8,128)(2,1)} %rw_ref.1) | copy-start | bytes 786436
  180.2 2.6 copy-start.20
  180.3 2.8 copy-start.14
  184.4 11.8 %copy-start.2 = (bf16[2,256,1024]{2,1,0:T(8,128)(2,1)S(1)}, bf16[2,256,1024]{2,1,0:T(8,128)(2,1)}, u32[]{:S(2)}) copy-start(bf16[2,256,1024]{2,1,0:T(8,128)(2,1)} %param.19) | copy-start | bytes 3145732
  184.4 11.8 %copy-start.24 = (bf16[512,2048]{1,0:T(8,128)(2,1)S(1)}, bf16[512,2048]{1,0:T(8,128)(2,1)}, u32[]{:S(2)}) copy-start(bf16[512,2048]{1,0:T(8,128)(2,1)} %get-tuple-element.124.gated_ref) | copy-start | bytes 6291460
  195.9 5.9 %copy-start.6 = (bf16[16,128,256]{2,1,0:T(8,128)(2,1)S(1)}, bf16[16,128,256]{2,1,0:T(8,128)(2,1)}, u32[]{:S(2)}) copy-start(bf16[16,128,256]{2,1,0:T(8,128)(2,1)} %get-tuple-element.121) | copy-start | bytes 3145732
  195.9 5.8 %collective-permute-start.1 = (bf16[16,128,256]{2,1,0:T(8,128)(2,1)}, bf16[16,128,256]{2,1,0:T(8,128)(2,1)S(1)}, u32[]{:S(2)}, u32[]{:S(2)}) collective-permute-start(bf16[16,128,256]{2,1,0:T(8,128)(2,1)} %get-tuple-element.123), channel_id=1, source_target_pairs={{0,4},{4,0},{8,12},{12,8},{16,20},{20,16},{24,28},{28,24},{1,5},{5... | collective-permute-start | bytes 3145736 | tf_op jit(solution)/shard_map/ppermute | solution.py:806
  202.0 16.2 %collective-permute-start.2 = (bf16[4,128,256]{2,1,0:T(8,128)(2,1)S(1)}, bf16[4,128,256]{2,1,0:T(8,128)(2,1)S(1)}, u32[]{:S(2)}, u32[]{:S(2)}) collective-permute-start(bf16[4,128,256]{2,1,0:T(8,128)(2,1)S(1)} %get-tuple-element.131), channel_id=1, source_target_pairs={{0,16},{4,20},{8,24},{12,28},{16,0},{20,4},{24,8},{28,12},{1,17},{... | collective-permute-start | bytes 786440 | tf_op jit(solution)/shard_map/ppermute | solution.py:800
  203.4 14.8 %collective-permute-start.3 = (bf16[4,128,256]{2,1,0:T(8,128)(2,1)S(1)}, bf16[4,128,256]{2,1,0:T(8,128)(2,1)S(1)}, u32[]{:S(2)}, u32[]{:S(2)}) collective-permute-start(bf16[4,128,256]{2,1,0:T(8,128)(2,1)S(1)} %get-tuple-element.132), channel_id=1, source_target_pairs={{0,8},{4,12},{8,0},{12,4},{16,24},{20,28},{24,16},{28,20},{1,9},{5... | collective-permute-start | bytes 786440 | tf_op jit(solution)/shard_map/ppermute | solution.py:800
  203.8 16.2 %collective-permute-start.4 = (bf16[4,128,256]{2,1,0:T(8,128)(2,1)S(1)}, bf16[4,128,256]{2,1,0:T(8,128)(2,1)S(1)}, u32[]{:S(2)}, u32[]{:S(2)}) collective-permute-start(bf16[4,128,256]{2,1,0:T(8,128)(2,1)S(1)} %get-tuple-element.133), channel_id=1, source_target_pairs={{0,24},{4,28},{8,16},{12,20},{16,8},{20,12},{24,0},{28,4},{1,25},{... | collective-permute-start | bytes 786440 | tf_op jit(solution)/shard_map/ppermute | solution.py:800
  205.6 11.7 %copy-start.16 = (f32[16,1024]{1,0:T(8,128)S(1)}, f32[16,1024]{1,0:T(8,128)}, u32[]{:S(2)}) copy-start(f32[16,1024]{1,0:T(8,128)} %get-tuple-element.135) | copy-start | bytes 196612
  205.6 14.5 %copy-start.13 = (f32[512,128]{1,0:T(8,128)S(1)}, f32[512,128]{1,0:T(8,128)}, u32[]{:S(2)}) copy-start(f32[512,128]{1,0:T(8,128)} %get-tuple-element.126) | copy-start | bytes 786436
  217.3 15.1 %copy-start.1 = (bf16[16,192,256]{2,1,0:T(8,128)(2,1)S(1)}, bf16[16,192,256]{2,1,0:T(8,128)(2,1)}, u32[]{:S(2)}) copy-start(bf16[16,192,256]{2,1,0:T(8,128)(2,1)} %get-tuple-element.129) | copy-start | bytes 4718596
  220.1 12.3 %collective-permute-start.5 = (bf16[16,192,256]{2,1,0:T(8,128)(2,1)}, bf16[16,192,256]{2,1,0:T(8,128)(2,1)}, u32[]{:S(2)}, u32[]{:S(2)}) collective-permute-start(bf16[16,192,256]{2,1,0:T(8,128)(2,1)} %get-tuple-element.137), channel_id=1, source_target_pairs={{0,4},{4,0},{8,12},{12,8},{16,20},{20,16},{24,28},{28,24},{1,5},{5... | collective-permute-start | bytes 4718600 | tf_op jit(solution)/shard_map/ppermute | solution.py:806
  220.3 7.0 %collective-permute-start.6 = (bf16[2,3,2048]{2,1,0:T(4,128)(2,1)S(1)}, bf16[2,3,2048]{2,1,0:T(4,128)(2,1)S(1)}, u32[]{:S(2)}, u32[]{:S(2)}) collective-permute-start(bf16[2,3,2048]{2,1,0:T(4,128)(2,1)S(1)} %slice.572), channel_id=1, source_target_pairs={{4,0},{8,4},{12,8},{16,12},{20,16},{24,20},{28,24},{5,1},{9,5},{13... | collective-permute-start | bytes 73736 | tf_op jit(solution)/shard_map/ppermute | solution.py:933
  221.9 7.3 %collective-permute-start.7 = (bf16[1,128,256]{2,1,0:T(8,128)(2,1)S(1)}, bf16[1,128,256]{2,1,0:T(8,128)(2,1)S(1)}, u32[]{:S(2)}, u32[]{:S(2)}) collective-permute-start(bf16[1,128,256]{2,1,0:T(8,128)(2,1)S(1)} %get-tuple-element.216), channel_id=1, source_target_pairs={{0,2},{1,3},{2,0},{3,1},{4,6},{5,7},{6,4},{7,5},{8,10},{9,11},{10,... | collective-permute-start | bytes 196616 | tf_op jit(solution)/shard_map/ppermute | solution.py:800
  224.4 5.2 %collective-permute-start.8 = (bf16[1,128,256]{2,1,0:T(8,128)(2,1)S(1)}, bf16[1,128,256]{2,1,0:T(8,128)(2,1)S(1)}, u32[]{:S(2)}, u32[]{:S(2)}) collective-permute-start(bf16[1,128,256]{2,1,0:T(8,128)(2,1)S(1)} %get-tuple-element.218), channel_id=1, source_target_pairs={{0,1},{1,0},{2,3},{3,2},{4,5},{5,4},{6,7},{7,6},{8,9},{9,8},{10,11... | collective-permute-start | bytes 196616 | tf_op jit(solution)/shard_map/ppermute | solution.py:800
  225.9 6.4 %collective-permute-start.9 = (bf16[1,128,256]{2,1,0:T(8,128)(2,1)S(1)}, bf16[1,128,256]{2,1,0:T(8,128)(2,1)S(1)}, u32[]{:S(2)}, u32[]{:S(2)}) collective-permute-start(bf16[1,128,256]{2,1,0:T(8,128)(2,1)S(1)} %get-tuple-element.217), channel_id=1, source_target_pairs={{0,3},{1,2},{2,1},{3,0},{4,7},{5,6},{6,5},{7,4},{8,11},{9,10},{10,... | collective-permute-start | bytes 196616 | tf_op jit(solution)/shard_map/ppermute | solution.py:800
  235.0 15.7 %collective-permute-start.10 = (bf16[4,192,256]{2,1,0:T(8,128)(2,1)}, bf16[4,192,256]{2,1,0:T(8,128)(2,1)}, u32[]{:S(2)}, u32[]{:S(2)}) collective-permute-start(bf16[4,192,256]{2,1,0:T(8,128)(2,1)} %get-tuple-element.152), channel_id=1, source_target_pairs={{0,16},{4,20},{8,24},{12,28},{16,0},{20,4},{24,8},{28,12},{1,17},{... | collective-permute-start | bytes 1179656 | tf_op jit(solution)/shard_map/ppermute | solution.py:800
  237.4 13.2 %collective-permute-start.11 = (bf16[4,192,256]{2,1,0:T(8,128)(2,1)}, bf16[4,192,256]{2,1,0:T(8,128)(2,1)}, u32[]{:S(2)}, u32[]{:S(2)}) collective-permute-start(bf16[4,192,256]{2,1,0:T(8,128)(2,1)} %get-tuple-element.153), channel_id=1, source_target_pairs={{0,8},{4,12},{8,0},{12,4},{16,24},{20,28},{24,16},{28,20},{1,9},{5... | collective-permute-start | bytes 1179656 | tf_op jit(solution)/shard_map/ppermute | solution.py:800
  238.0 17.7 %collective-permute-start.12 = (bf16[4,192,256]{2,1,0:T(8,128)(2,1)}, bf16[4,192,256]{2,1,0:T(8,128)(2,1)}, u32[]{:S(2)}, u32[]{:S(2)}) collective-permute-start(bf16[4,192,256]{2,1,0:T(8,128)(2,1)} %get-tuple-element.154), channel_id=1, source_target_pairs={{0,24},{4,28},{8,16},{12,20},{16,8},{20,12},{24,0},{28,4},{1,25},{... | collective-permute-start | bytes 1179656 | tf_op jit(solution)/shard_map/ppermute | solution.py:800
  241.0 4.9 %copy-start.3 = (bf16[2,256,1024]{2,1,0:T(8,128)(2,1)S(1)}, bf16[2,256,1024]{2,1,0:T(8,128)(2,1)}, u32[]{:S(2)}) copy-start(bf16[2,256,1024]{2,1,0:T(8,128)(2,1)} %param.19) | copy-start | bytes 3145732
  241.0 4.9 %copy-start.22 = (f32[1024]{0:T(1024)S(1)}, f32[1024]{0:T(1024)}, u32[]{:S(2)}) copy-start(f32[1024]{0:T(1024)} %param.21) | copy-start | bytes 12292
  241.0 4.9 %copy-start.23 = (bf16[512,2048]{1,0:T(8,128)(2,1)S(1)}, bf16[512,2048]{1,0:T(8,128)(2,1)}, u32[]{:S(2)}) copy-start(bf16[512,2048]{1,0:T(8,128)(2,1)} %get-tuple-element.141.gate_ref) | copy-start | bytes 6291460
  250.6 10.9 %copy-start.7 = (bf16[2,256,1024]{2,1,0:T(8,128)(2,1)S(1)}, bf16[2,256,1024]{2,1,0:T(8,128)(2,1)}, u32[]{:S(2)}) copy-start(bf16[2,256,1024]{2,1,0:T(8,128)(2,1)} %param.20) | copy-start | bytes 3145732
  257.1 10.2 %collective-permute-start.13 = (bf16[1,192,256]{2,1,0:T(8,128)(2,1)S(1)}, bf16[1,192,256]{2,1,0:T(8,128)(2,1)S(1)}, u32[]{:S(2)}, u32[]{:S(2)}) collective-permute-start(bf16[1,192,256]{2,1,0:T(8,128)(2,1)S(1)} %get-tuple-element.205), channel_id=1, source_target_pairs={{0,2},{1,3},{2,0},{3,1},{4,6},{5,7},{6,4},{7,5},{8,10},{9,11},{10,... | collective-permute-start | bytes 294920 | tf_op jit(solution)/shard_map/ppermute | solution.py:800
  259.7 7.6 %collective-permute-start.14 = (bf16[1,192,256]{2,1,0:T(8,128)(2,1)S(1)}, bf16[1,192,256]{2,1,0:T(8,128)(2,1)S(1)}, u32[]{:S(2)}, u32[]{:S(2)}) collective-permute-start(bf16[1,192,256]{2,1,0:T(8,128)(2,1)S(1)} %get-tuple-element.207), channel_id=1, source_target_pairs={{0,1},{1,0},{2,3},{3,2},{4,5},{5,4},{6,7},{7,6},{8,9},{9,8},{10,11... | collective-permute-start | bytes 294920 | tf_op jit(solution)/shard_map/ppermute | solution.py:800
  259.7 10.5 %collective-permute-start.15 = (bf16[1,192,256]{2,1,0:T(8,128)(2,1)S(1)}, bf16[1,192,256]{2,1,0:T(8,128)(2,1)S(1)}, u32[]{:S(2)}, u32[]{:S(2)}) collective-permute-start(bf16[1,192,256]{2,1,0:T(8,128)(2,1)S(1)} %get-tuple-element.206), channel_id=1, source_target_pairs={{0,3},{1,2},{2,1},{3,0},{4,7},{5,6},{6,5},{7,4},{8,11},{9,10},{10,... | collective-permute-start | bytes 294920 | tf_op jit(solution)/shard_map/ppermute | solution.py:800
  274.9 3.0 %copy-start.5 = (bf16[1,128,1024]{2,1,0:T(8,128)(2,1)S(1)}, bf16[1,128,1024]{2,1,0:T(8,128)(2,1)}, u32[]{:S(2)}) copy-start(bf16[1,128,1024]{2,1,0:T(8,128)(2,1)} %reduce-scatter.5.cloned.1.call-done) | copy-start | bytes 786436
  276.0 2.7 copy-start.8
Sparse Core Ops, SparseCore 0:
  62.1 28.2 all-gather.4
  92.3 23.5 all-gather.6
  138.2 74.1 reduce-scatter.2
  239.1 27.8 reduce-scatter.4

commit v2 on v1

--- a/solution.py
+++ b/solution.py
@@ -400,20 +400,11 @@
     return (wide * lax.rsqrt(jnp.mean(wide * wide, axis=1, keepdims=True) + epsilon) * gain).astype(bf16)
 
 
-def gate_kernel(tok_ref, gain_ref, cot_ref, wg_ref, ow_ref, normed_ref, turned_ref, scale_ref, g_ref, ga_ref, gs_ref, gh_ref, gg_ref):
-    rows = tok_ref.shape[0]
+def gate_kernel(normed_ref, cot_ref, wg_ref, ow_ref, turned_ref, g_ref, ga_ref, gs_ref, gh_ref, gg_ref):
+    rows = normed_ref.shape[0]
 
     @pl.when(pl.program_id(0) == 0)
     def _():
-        def norm(i, _):
-            at = pl.ds(pl.multiple_of(i * ROWS, ROWS), ROWS)
-            wide = tok_ref[at, :].astype(f32)
-            scale = lax.rsqrt(jnp.mean(wide * wide, axis=1, keepdims=True) + epsilon)
-            scale_ref[at, :] = jnp.broadcast_to(scale, (ROWS, 128))
-            normed_ref[at, :] = (wide * scale * gain_ref[...]).astype(bf16)
-            return 0
-
-        lax.fori_loop(0, rows // ROWS, norm, 0)
         turned_ref[...] = normed_ref[...].T
 
     gh_ref[...] = jnp.dot(normed_ref[...], wg_ref[...], preferred_element_type=f32)
@@ -436,30 +427,37 @@
     lax.fori_loop(0, rows // ROWS, mix, 0)
 
 
-def gate_side(tokens, gain, cotangent, in_weight, out_weight):
-    rows, model = tokens.shape
+def gate_side(normed, cotangent, in_weight, out_weight):
+    rows, model = normed.shape
     inner = out_weight.shape[0]
     first = inner // WIDTH
     tiles = jax.ShapeDtypeStruct((inner // 128, rows, 128), f32)
     return kernel_call(
         gate_kernel, "gate_side", inner,
-        (tokens, gain, cotangent, in_weight, out_weight),
+        (normed, cotangent, in_weight, out_weight),
         [
-            whole(tokens), whole(gain), whole(cotangent),
-            pl.BlockSpec((model, WIDTH), lambda j: (0, j + first)),
+            whole(normed), whole(cotangent), pl.BlockSpec((model, WIDTH), lambda j: (0, j + first)),
             pl.BlockSpec((WIDTH, model), lambda j: (j, 0)),
         ],
-        [pl.BlockSpec((rows, model), lambda j: (0, 0)), pl.BlockSpec((model, rows), lambda j: (0, 0)), pl.BlockSpec((rows, 128), lambda j: (0, 0))]
-        + [tiles_of(rows)] * 3,
-        (jax.ShapeDtypeStruct((rows, model), bf16), jax.ShapeDtypeStruct((model, rows), bf16), jax.ShapeDtypeStruct((rows, 128), f32), tiles, tiles, tiles),
+        [pl.BlockSpec((model, rows), lambda j: (0, 0))] + [tiles_of(rows)] * 3,
+        (jax.ShapeDtypeStruct((model, rows), bf16), tiles, tiles, tiles),
         4 * rows * model * inner, scratch=[pltpu.VMEM((rows, WIDTH), f32)] * 2,
     )
 
 
 def inner_kernel(
-    normed_ref, halo_ref, gain_ref, wi_ref, cw_ref, cb_ref, sw_ref, inner_ref, before_ref, x_ref, slope_ref, proj_ref, ext_ref, flat_ref,
-    *, nseq, length,
+    tok_ref, halo_ref, gain_ref, wi_ref, cw_ref, cb_ref, sw_ref,
+    normed_ref, inner_ref, before_ref, x_ref, slope_ref, proj_ref, ext_ref, flat_ref, *, nseq, length,
 ):
+    @pl.when(pl.program_id(0) == 0)
+    def _():
+        def norm(i, _):
+            at = pl.ds(pl.multiple_of(i * ROWS, ROWS), ROWS)
+            normed_ref[at, :] = normalized(tok_ref[at, :], gain_ref[...])
+            return 0
+
+        lax.fori_loop(0, nseq * length // ROWS, norm, 0)
+
     part = jnp.dot(normed_ref[...], wi_ref[...], preferred_element_type=f32).astype(bf16)
     inner_ref[...] = part
     for s in range(nseq):
@@ -498,13 +496,13 @@
     proj_ref[...] += jnp.dot(flat_ref[...], sw_ref[...], preferred_element_type=f32)
 
 
-def inner_side(normed, halo, gain, in_weight, conv_weight, conv_bias, select_weight, nseq, length):
-    rows, model = normed.shape
+def inner_side(tokens, halo, gain, in_weight, conv_weight, conv_bias, select_weight, nseq, length):
+    rows, model = tokens.shape
     inner, picks = select_weight.shape
     o = jax.ShapeDtypeStruct
-    operands = (normed, halo, gain, in_weight, conv_weight, conv_bias, select_weight)
+    operands = (tokens, halo, gain, in_weight, conv_weight, conv_bias, select_weight)
     specs = [
-        whole(normed), whole(halo), whole(gain), block_of(model), block_of(conv_weight.shape[0]), block_of(1),
+        whole(tokens), whole(halo), whole(gain), block_of(model), block_of(conv_weight.shape[0]), block_of(1),
         pl.BlockSpec((WIDTH, picks), lambda j: (j, 0)),
     ]
     return pl.pallas_call(
@@ -512,11 +510,11 @@
         grid=(inner // WIDTH,),
         in_specs=specs,
         out_specs=[
-            block_of(rows), block_of(halo.shape[0]), tiles_of(rows), block_of(rows),
+            pl.BlockSpec((rows, model), lambda j: (0, 0)), block_of(rows), block_of(halo.shape[0]), tiles_of(rows), block_of(rows),
             pl.BlockSpec((rows, picks), lambda j: (0, 0)),
         ],
         out_shape=(
-            o((rows, inner), bf16), o((halo.shape[0], inner), bf16), o((inner // 128, rows, 128), bf16),
+            o((rows, model), bf16), o((rows, inner), bf16), o((halo.shape[0], inner), bf16), o((inner // 128, rows, 128), bf16),
             o((rows, inner), f32), o((rows, picks), f32),
         ),
         scratch_shapes=[pltpu.VMEM((nseq, NL, PAD + length, 128), f32), pltpu.VMEM((rows, WIDTH), bf16)],
@@ -764,6 +762,62 @@
     )(gated, gate_grad, cot, turned)
 
 
+def share_kernel(*refs, count, rank, taps, part, part_rows, picks):
+    first, second = refs[:count], refs[count : 2 * count]
+    summed_ref, weight_ref, gain_ref = refs[2 * count : 2 * count + 3]
+    in_ref, out_ref, conv_ref, bias_ref, select_ref, rate_ref, rate_bias_ref, decay_ref, skip_ref, norm_ref = refs[
+        2 * count + 3 :
+    ]
+    pad = padded(part_rows)
+    wide = first[0].shape[2]
+    model = summed_ref.shape[1]
+    each = first[0].shape[1] // pad
+
+    def total(held, at, rows):
+        return sum(h[0, at : at + rows, :].astype(f32) for h in held)
+
+    for half, held in enumerate((first, second)):
+        for b in range(each):
+            at = (half * each + b) * wide
+            in_ref[:, at : at + wide] = total(held, b * pad, pad)[:part_rows]
+    gate_at = 2 * each * wide
+    for b in range((in_ref.shape[1] - gate_at) // model):
+        at = padded(part) + b * pad
+        in_ref[:, gate_at + b * model : gate_at + (b + 1) * model] = summed_ref[at : at + pad, :][:part_rows].astype(f32)
+    out_ref[...] = summed_ref[: padded(part), :][:part].astype(f32)
+    gain = jnp.sum(weight_ref[...].astype(f32) * in_ref[...], axis=1, keepdims=True)
+    gain = jnp.broadcast_to(gain, (part_rows, 128))
+    if part_rows < 8:
+        gain = jnp.concatenate([gain, jnp.zeros((8 - part_rows, 128), f32)], axis=0)
+    norm_ref[...] = gain.T[:1, :part_rows] / gain_ref[...]
+    small = total(second, each * pad, padded(part))[:part]
+    turned = small[:, : wide // 2].T
+    rate_ref[...] = turned[:rank]
+    conv_ref[...] = turned[rank : rank + taps]
+    bias_ref[...] = turned[rank + taps : rank + taps + 1]
+    rate_bias_ref[...] = turned[rank + taps + 1 : rank + taps + 2]
+    skip_ref[...] = turned[rank + taps + 2 : rank + taps + 3]
+    decay_ref[...] = turned[rank + 8 : rank + 8 + N].T
+    select_ref[...] = small[:, wide // 2 : wide // 2 + picks]
+
+
+def shares_of(first, second, summed, own_weight, own_gain, rank, taps, part, picks):
+    part_rows, width = own_weight.shape
+    model = summed.shape[1]
+    o = lambda *shape: jax.ShapeDtypeStruct(shape, f32)
+    return pl.pallas_call(
+        functools.partial(
+            share_kernel, count=len(first), rank=rank, taps=taps, part=part, part_rows=part_rows, picks=picks
+        ),
+        out_shape=(
+            o(part_rows, width), o(part, model), o(taps, part), o(1, part), o(part, picks), o(rank, part), o(1, part),
+            o(part, N), o(1, part), o(1, part_rows),
+        ),
+        compiler_params=pltpu.CompilerParams(vmem_limit_bytes=VMEM),
+        name="shares",
+    )(*first, *second, summed, own_weight, own_gain)
+
+
 def flip_bit(axis, bit):
     return [(i, i ^ bit) for i in range(lax.axis_size(axis))]
 
@@ -812,10 +866,13 @@
     return held, later
 
 
-def sum_rounds(held, rounds):
+def remaining_rounds(held, rounds, later):
     for bits in rounds:
-        held = round_trade(round_parts(held, bits), bits)
-    return sum(h[0].astype(f32) for h in held)
+        parts = round_parts(held, bits)
+        if later is not None and bits is rounds[-1]:
+            *parts, later = lax.optimization_barrier((*parts, later))
+        held = round_trade(parts, bits)
+    return held, later
 
 
 def carried(block, shape, rates, backward, after=None, spans=None):
@@ -865,18 +922,18 @@
     pieces, grp = lax.axis_size("seq"), lax.axis_size("grp")
     halo = lax.ppermute(tokens[:, length - PAD :], "seq", [(i, i + 1) for i in range(pieces - 1)])
     halo = halo.reshape(nseq * PAD, model)
-    normed, turned, scale, g, ga, gs = gate_side(tok, gain, cot, in_weight, out_weight)
     picks, wide = rank + 2 * N, 256
     select_weight = jnp.pad(select_weight, ((0, 0), (0, wide // 2 - picks)))
-    inner, before, x, slope, proj = inner_side(
-        normed, halo, gain, in_weight, conv_weight, bias, select_weight, nseq, length
+    normed, inner, before, x, slope, proj = inner_side(
+        tok, halo, gain, in_weight, conv_weight, bias, select_weight, nseq, length
     )
     in_gate, out_gate = proj[:, rank : rank + N], proj[:, rank + N : picks]
     log = decay_log.T
     rates = -jnp.exp(log)
     bb = jnp.broadcast_to(in_gate[:, :, None], (rows, N, 128))
     ahead, dl, u = state_end(proj, rate_weight, rate_bias[None], x, log, bb, nseq, length)
-    ahead, g = lax.optimization_barrier((ahead.astype(bf16), g))
+    ahead, cot = lax.optimization_barrier((ahead.astype(bf16), cot))
+    turned, g, ga, gs = gate_side(normed, cot, in_weight, out_weight)
     state_shape = (nseq, N, inner_width)
     entering, _, spans = carried(ahead, state_shape, rates, False)
     cb = jnp.broadcast_to(out_gate[:, :, None], (rows, N, 128))
@@ -921,62 +978,59 @@
             proj, decay_grad, rate_bias_grad, skip_grad, early, nseq, length, part, rank, grp,
         )
 
-    wide_tok = tok.astype(f32)
     kept, sent, first_grad, first_tail, first_head, early = half(conv_part, None)
     sent, gated = lax.optimization_barrier((sent, gated))
+    wide_tok = tok.astype(f32)
     block_out = wide_tok + jnp.dot(gated, out_weight, preferred_element_type=f32)
     first_held, (conv_part, block_out) = sum_packed(kept, sent, rounds[:2], (conv_part, block_out))
     kept, sent, second_grad, second_tail, second_head = half(conv_part, early)
     head = jnp.concatenate([first_head, second_head], axis=1)
-    *first_held, sent, head = lax.optimization_barrier((*first_held, sent, head))
+    *first_held, sent, head, weight_sum = lax.optimization_barrier((*first_held, sent, head, weight_sum))
     head = head.reshape(nseq, PAD, inner_width)[:, : taps - 1].astype(bf16)
     returned = lax.ppermute(head, "seq", [(i + 1, i) for i in range(pieces - 1)]).astype(f32)
-    held, (returned, gate_grad, first_grad, weight_sum) = sum_packed(
-        kept, sent, rounds[:2], (returned, gate_grad, first_grad, weight_sum)
-    )
-    first_held = sum_rounds(first_held, rounds[2:])
-    held = sum_rounds(held, rounds[2:])
-    weight_share = lax.psum_scatter(weight_sum, "grp", scatter_dimension=0, tiled=True)[0].astype(f32)
-    out_share = weight_share[:part]
-    gate_share = weight_share[padded(part) :].reshape(-1, padded(part_rows), model)[:, :part_rows]
-    gate_share = gate_share.transpose(1, 0, 2).reshape(part_rows, inner_width)
-    blocks = half_width // wide
-
-    def in_rows(held):
-        share = held[: blocks * padded(part_rows)].reshape(blocks, padded(part_rows), wide)[:, :part_rows]
-        return share.transpose(1, 0, 2).reshape(part_rows, half_width)
-
-    inner_share = jnp.concatenate([in_rows(first_held), in_rows(held)], axis=1)
-    small = held[blocks * padded(part_rows) :][:part]
-    inner_grad = jnp.concatenate([first_grad, second_grad], axis=1)
+    held, (gate_grad, *first_held) = sum_packed(kept, sent, rounds[:2], (gate_grad, *first_held))
+    normed_grad = rows_dot(gate_grad, in_weight[:, inner_width:])
+    *first_held, normed_grad = lax.optimization_barrier((*first_held, normed_grad))
+    first_held, _ = remaining_rounds(first_held, rounds[2:], None)
+    held, (returned, second_grad, normed_grad) = remaining_rounds(
+        held, rounds[2:], (returned, second_grad, normed_grad)
+    )
+    weight_share = lax.psum_scatter(weight_sum, "grp", scatter_dimension=0, tiled=True)[0]
+    first = (lax.axis_index("seq") * grp + lax.axis_index("grp")) * part_rows
+    own_weight = lax.dynamic_slice_in_dim(in_weight, first, part_rows, 0)
+    own_gain = lax.dynamic_slice_in_dim(norm_gain, first, part_rows, 0)[None]
+    in_share, out_share, conv_share, bias_share, select_share, rate_share, rate_bias_share, decay_share, skip_share, (
+        gain_share
+    ) = shares_of(first_held, held, weight_share, own_weight, own_gain, rank, taps, part, picks)
     tail = jnp.concatenate([first_tail, second_tail], axis=1)
     fixed = (tail.reshape(nseq, PAD, inner_width)[:, PAD - taps + 1 :] + returned).astype(bf16)
-    inner_grad = (
-        inner_grad.reshape(nseq, length, inner_width).at[:, length - taps + 1 :].set(fixed).reshape(rows, inner_width)
-    )
-    scale = scale[:, :1]
-    normed_grad = rows_dot(gate_grad, in_weight[:, inner_width:]) + rows_dot(inner_grad, in_weight[:, :inner_width])
+
+    def patched(grad, at):
+        rows_of = grad.reshape(nseq, length, half_width)
+        rows_of = rows_of.at[:, length - taps + 1 :].set(fixed[:, :, at : at + half_width])
+        return rows_of.reshape(rows, half_width)
+
+    normed_grad = (
+        normed_grad
+        + rows_dot(patched(first_grad, 0), in_weight[:, :half_width])
+        + rows_dot(patched(second_grad, half_width), in_weight[:, half_width:inner_width])
+    )
+    scale = lax.rsqrt(jnp.mean(wide_tok * wide_tok, axis=1, keepdims=True) + epsilon)
     lifted = normed_grad * norm_gain
     dots = jnp.mean(lifted * wide_tok, axis=1, keepdims=True)
     tokens_grad = cot.astype(f32) + scale * lifted - wide_tok * (scale * scale * scale) * dots
-    in_share = jnp.concatenate([inner_share, gate_share], axis=1)
-    first = (lax.axis_index("seq") * grp + lax.axis_index("grp")) * part_rows
-    own_weight = lax.dynamic_slice_in_dim(in_weight, first, part_rows, 0).astype(f32)
-    own_gain = lax.dynamic_slice_in_dim(norm_gain, first, part_rows, 0)
-    gain_share = jnp.sum(own_weight * in_share, axis=1) / own_gain
-    vectors = small[:, rank : rank + 8].T
     return (
         block_out.astype(bf16).reshape(tokens.shape),
         tokens_grad.astype(bf16).reshape(tokens.shape),
-        gain_share,
+        gain_share[0],
         in_share,
-        vectors[:taps],
-        vectors[taps],
-        small[:, wide // 2 : wide // 2 + picks],
-        small[:, :rank].T,
-        vectors[taps + 1],
-        small[:, rank + 8 : rank + 8 + N],
-        vectors[taps + 2],
+        conv_share,
+        bias_share[0],
+        select_share,
+        rate_share,
+        rate_bias_share[0],
+        decay_share,
+        skip_share[0],
         out_share,
     )
 

time: 286 us -> 281 us (0.983)
  waiting for transfers between devices: 26.1 us -> 14 us
  starting transfers between devices: 20.9 us -> 25.3 us
    all_gather x2, waiting for transfers between devices: 7.13 us -> 0.02 us  [carried(): blocks = lax.all_gather(block.astype(bf16), 'seq')]
    ppermute x12, waiting for transfers between devices: 18.9 us -> 13.2 us  [round_trade(): held.append(lax.ppermute(parts[i], bits[0][0], flip_bit(bits[0][0], flip)))]
    ppermute x2, starting transfers between devices: 0.34 us -> 4.55 us  [sum_packed(): held = [kept, lax.ppermute(sent, axis, flip_bit(axis, bit))]]
    slice x6 -> x1, local copies, waits for them, and re-layouts: 3.15 us -> 0.01 us  [patched(): fixed[:, :, at:at + half_width]]
    pallas_call x5, Pallas kernels: 122 us -> 119 us  [kernel_call(): pl.pallas_call(functools.partial(body, **options), grid=(channels // WIDT...]
    dot_general x3 -> x4, matrix products: 12.1 us -> 13.2 us  [rows_dot(): lax.dot_general(left, right, (((1,), (1,)), ((), ())), preferred_element_...]
  transfers between devices with their start and end apart: 20 -> 20, of which waited for: 8 -> 4; matrix products, arithmetic and copies ran while one was open for 16% -> 18% of each run, Pallas kernels for 48% -> 48%
where the time goes in v2:
time: 281 us; the launch traced here: 279 us
  Pallas kernels  167 us (59%)
  starting transfers between devices  25.3 us (9%)
  matrix products  21.3 us (8%)
  other arithmetic  19.2 us (7%)
  local copies, waits for them, and re-layouts  18.6 us (7%)
  between operations  14.4 us (5%)
  waiting for transfers between devices  14 us (5%)
    pallas_call x5, Pallas kernels, kernel_call(): pl.pallas_call(functools.partial(body, **options), grid=(channels // WIDT...  119 us
    pallas_call x2, Pallas kernels, input_grads(): pl.pallas_call(functools.partial(input_grad_kernel, nseq=nseq, length=len...  23 us
    ppermute x12, starting transfers between devices, round_trade(): held.append(lax.ppermute(parts[i], bits[0][0], flip_bit(bits[0][0], flip)))  16.5 us
    dot_general x4, matrix products, rows_dot(): lax.dot_general(left, right, (((1,), (1,)), ((), ())), preferred_element_...  13.2 us
    ppermute x12, waiting for transfers between devices, round_trade(): held.append(lax.ppermute(parts[i], bits[0][0], flip_bit(bits[0][0], flip)))  13.2 us
    pallas_call x1, Pallas kernels, inner_side(): pl.pallas_call(functools.partial(inner_kernel, nseq=nseq, length=length),...  11.7 us
    pallas_call x1, Pallas kernels, weight_grads(): pl.pallas_call(functools.partial(weight_grad_kernel, part=part), grid=(wi...  10.3 us
    convert_element_type x4, other arithmetic, round_parts(): return parts[:1] + [part.astype(bf16) for part in parts[1:]]  5.75 us
  transfers between devices with their start and end apart: 20, of which 4 were waited for; matrix products, arithmetic and copies ran while one was open for 18% of the time, Pallas kernels for 48%

profile of v2, /device:TPU:0, one launch (start us, length us, event | category | flops | bytes accessed | tf_op | source)
XLA Modules:
  0.0 279.5 jit_solution(12663954345769159121)
XLA Ops:
  8.0 2.3 collective-permute-start
  11.3 1.3 copy.35
  14.1 11.7 %inner_side.1 = (bf16[512,1024]{1,0:T(8,128)(2,1)}, bf16[512,2048]{1,0:T(8,128)(2,1)}, bf16[16,2048]{1,0:T(8,128)(2,1)}, bf16[16,512,128]{2,1,0:T(8,128)(2,1)}, f32[512,2048]{1,0:T(8,128)}, /*index=5*/f32[512,128]{1,0:T(8,128)}) custom-call(bf16[512,1024]{1,0:T(8,128)(2,1)} %bitcast.120, bf16[16,1024]{1,0:T(8,128)(2,1)} %bitcast.147, f32[1,1024]{1,0:T(1,128)} %bitcast.152, ...), custom_call_target="tpu_custom_call" | custom-call | flops 2147483648 | bytes 14680064 | tf_op jit(solution)/shard_map/inner_side/pallas_call | solution.py:508
  25.8 1.3 multiply_reduce_fusion.1
  27.2 2.6 broadcast_in_dim.26.bb_ref
  29.8 19.3 %state_end.1 = (f32[48,2048]{1,0:T(8,128)}, f32[16,512,128]{2,1,0:T(8,128)}, f32[16,512,128]{2,1,0:T(8,128)}) custom-call(f32[512,128]{1,0:T(8,128)} %get-tuple-element.125.proj_ref, bf16[64,2048]{1,0:T(8,128)(2,1)} %rw_ref.1, f32[1,2048]{1,0:T(1,128)} %bitcast.160, bf16[16,512,128]{2,1,0:T(8,128)(2,1)} %get-tuple-element.126.x_ref, f32[16,2048]{1,0:T(8,128)} %bitcast.143, ...), custom_call_target="tpu_custom_call" | custom-call | flops 20000000000 | bytes 15736832 | tf_op jit(solution)/shard_map/state_end/pallas_call | solution.py:293
  49.1 1.7 convert_element_type.294
  50.9 1.4 fusion.10.lb_ref
  52.3 12.8 %gate_side.1 = (bf16[1024,512]{1,0:T(8,128)(2,1)}, f32[16,512,128]{2,1,0:T(8,128)}, f32[16,512,128]{2,1,0:T(8,128)}, f32[16,512,128]{2,1,0:T(8,128)}) custom-call(bf16[512,1024]{1,0:T(8,128)(2,1)} %get-tuple-element.128.normed_ref, bf16[512,1024]{1,0:T(8,128)(2,1)} %bitcast.122, bf16[1024,4096]{1,0:T(8,128)(2,1)} %wg_ref.1, bf16[2048,1024]{1,0:T(8,128)(2,1)} %ow_ref.1), custom_call_target="tpu_custom_call" | custom-call | flops 4294967296 | bytes 28311552 | tf_op jit(solution)/shard_map/gate_side/pallas_call | solution.py:293
  65.1 2.6 broadcast_in_dim.27.cb_ref
  67.7 15.9 %adjoint_end.1 = bf16[32,2048]{1,0:T(8,128)(2,1)} custom-call(f32[16,512,128]{2,1,0:T(8,128)} %get-tuple-element.127.dl_ref, f32[16,512,128]{2,1,0:T(8,128)} %get-tuple-element.131.g_ref, f32[16,2048]{1,0:T(8,128)} %bitcast.144, f32[512,16,128]{2,1,0:T(8,128)} %broadcast_in_dim.27.cb_ref), custom_call_target="tpu_custom_call" | custom-call | flops 20000000000 | bytes 12845056 | tf_op jit(solution)/shard_map/adjoint_end/pallas_call | solution.py:293
  83.6 1.1 fusion.11.lc_ref
  84.8 1.8 fusion.20
  87.0 1.1 add_select_fusion.hin_ref
  88.9 33.1 %forward.1 = (bf16[8192,2048]{1,0:T(8,128)(2,1)}, bf16[512,2048]{1,0:T(8,128)(2,1)}, bf16[512,2048]{1,0:T(8,128)(2,1)}, f32[32,256]{1,0:T(8,128)}, f32[512,128]{1,0:T(8,128)}, /*index=5*/f32[8,2048]{1,0:T(8,128)}) custom-call(f32[16,512,128]{2,1,0:T(8,128)} %get-tuple-element.127.dl_ref, f32[16,512,128]{2,1,0:T(8,128)} %get-tuple-element.133.u_ref, ...), custom_call_target="tpu_custom_call" | custom-call | flops 30000001024 | bytes 66560000 | tf_op jit(solution)/shard_map/forward/pallas_call | solution.py:293
  122.1 10.3 %weight_grads.1 = bf16[32,128,1024]{2,1,0:T(8,128)(2,1)} custom-call(bf16[512,2048]{1,0:T(8,128)(2,1)} %get-tuple-element.159.gated_ref, bf16[512,2048]{1,0:T(8,128)(2,1)} %get-tuple-element.187.gate_ref, bf16[512,1024]{1,0:T(8,128)(2,1)} %bitcast.123, bf16[1024,512]{1,0:T(8,128)(2,1)} %get-tuple-element.142.turned_ref), custom_call_target="tpu_custom_call" | custom-call | flops 4294967296 | bytes 14680064 | tf_op jit(solution)/shard_map/weight_grads/pallas_call | solution.py:753
  133.7 1.1 fusion.12.lin_ref
  134.9 38.2 %backward.1 = (bf16[512,2048]{1,0:T(8,128)(2,1)}, f32[512,2048]{1,0:T(8,128)}, f32[32,256]{1,0:T(8,128)}, f32[16,2048]{1,0:T(8,128)}, f32[8,2048]{1,0:T(8,128)}) custom-call(f32[16,512,128]{2,1,0:T(8,128)} %get-tuple-element.127.dl_ref, f32[16,512,128]{2,1,0:T(8,128)} %get-tuple-element.133.u_ref, f32[16,512,128]{2,1,0:T(8,128)} %get-tuple-element.131.g_ref, ...), custom_call_target="tpu_custom_call" | custom-call | flops 49999998976 | bytes 60465152 | tf_op jit(solution)/shard_map/backward/pallas_call | solution.py:293
  173.1 2.4 convolution_convert_fusion.2
  177.2 11.5 %input_grads.2 = (bf16[16,128,256]{2,1,0:T(8,128)(2,1)}, bf16[16,128,256]{2,1,0:T(8,128)(2,1)}, bf16[512,1024]{1,0:T(8,128)(2,1)}, f32[16,1024]{1,0:T(8,128)}, f...) custom-call(s32[33]{0:T(128)} %pad_add_fusion.place_ref, f32[512,2048]{1,0:T(8,128)} %get-tuple-element.161.cp_ref, ...), custom_call_target="tpu_custom_call" | custom-call | flops 12884901888 | bytes 16777216 | tf_op jit(solution)/shard_map/input_grads/pallas_call | solution.py:701
  188.7 4.5 %collective-permute-start.1 = (bf16[16,128,256]{2,1,0:T(8,128)(2,1)}, bf16[16,128,256]{2,1,0:T(8,128)(2,1)S(1)}, u32[]{:S(2)}, u32[]{:S(2)}) collective-permute-start(bf16[16,128,256]{2,1,0:T(8,128)(2,1)} %get-tuple-element.158), channel_id=1, source_target_pairs={{0,4},{4,0},{8,12},{12,8},{16,20},{20,16},{24,28},{28,24},{1,5},{5... | collective-permute-start | bytes 3145736 | tf_op jit(solution)/shard_map/ppermute | solution.py:860
  193.2 5.5 %convert_add_fusion = bf16[512,1024]{1,0:T(8,128)(2,1)} fusion(bf16[512,1024]{1,0:T(8,128)(2,1)S(1)} %bitcast.121, bf16[512,2048]{1,0:T(8,128)(2,1)S(1)} %copy-done.23, bf16[2048,1024]{1,0:T(8,128)(2,1)} %ow_ref.1), kind=kOutput, calls=%fused_computation.4 | convolution fusion | flops 2149056512 | bytes 8388608 | tf_op jit(solution)/shard_map/dot_general | solution.py:984
  198.7 1.1 add_convert_fusion.3
  199.8 1.3 collective-permute-start.2
  201.1 2.2 collective-permute-start.4
  203.3 11.5 %input_grads.3 = (bf16[16,192,256]{2,1,0:T(8,128)(2,1)}, bf16[16,192,256]{2,1,0:T(8,128)(2,1)}, bf16[512,1024]{1,0:T(8,128)(2,1)}, f32[16,1024]{1,0:T(8,128)}, f32[16,1024]{1,0:T(8,128)}) custom-call(s32[33]{0:T(128)} %pad_add_fusion.place_ref, f32[512,2048]{1,0:T(8,128)} %get-tuple-element.161.cp_ref, bf16[512,2048]{1,0:T(8,128)(2,1)} %get-tuple-element.146.inner_ref, ...), custom_call_target="tpu_custom_call" | custom-call | flops 12884901888 | bytes 16777216 | tf_op jit(solution)/shard_map/input_grads/pallas_call | solution.py:701
  214.8 1.0 pad_maximum_fusion
  215.8 1.7 collective-permute-done.4
  218.4 1.6 constant_dynamic-slice_fusion.refs_9_
  220.1 1.5 collective-permute-start.9
  223.3 1.9 add_convert_fusion
  225.2 2.6 collective-permute-start.6
  228.3 1.0 collective-permute-start.8
  229.3 4.6 %fusion = f32[512,1024]{1,0:T(8,128)S(1)} fusion(bf16[512,2048]{1,0:T(8,128)(2,1)S(1)} %copy-done.22, bf16[1024,4096]{1,0:T(8,128)(2,1)} %wg_ref.1), kind=kOutput, calls=%fused_computation | convolution fusion | flops 2147483648 | bytes 8388608 | tf_op jit(solution)/shard_map/dot_general | solution.py:44
  234.0 1.9 add_convert_fusion.10
  235.8 2.5 collective-permute-start.10
  238.3 1.5 collective-permute-start.11
  240.3 6.6 %collective-permute-done.8 = bf16[4,192,256]{2,1,0:T(8,128)(2,1)S(1)} collective-permute-done((bf16[4,192,256]{2,1,0:T(8,128)(2,1)S(1)}, bf16[4,192,256]{2,1,0:T(8,128)(2,1)S(1)}, u32[]{:S(2)}, u32[]{:S(2)}) %collective-permute-start.8) | collective-permute-done | bytes 393248 | tf_op jit(solution)/shard_map/ppermute | solution.py:854
  247.8 2.4 collective-permute-start.13
  250.2 1.5 collective-permute-start.14
  251.7 1.4 scatter.6
  253.1 1.4 scatter.9
  254.5 3.3 %fusion.8 = f32[512,1024]{1,0:T(8,128)S(1)} fusion(bf16[512,1024]{1,0:T(8,128)(2,1)} %bitcast.157, bf16[1024,4096]{1,0:T(8,128)(2,1)} %wg_ref.1), kind=kOutput, calls=%fused_computation.12 | convolution fusion | flops 1073741824 | bytes 5242880 | tf_op jit(solution)/shard_map/dot_general | solution.py:44
  257.8 2.9 %fusion.6 = f32[512,1024]{1,0:T(8,128)S(1)} fusion(bf16[512,1024]{1,0:T(8,128)(2,1)S(1)} %bitcast.159, bf16[1024,4096]{1,0:T(8,128)(2,1)} %wg_ref.1), kind=kOutput, calls=%fused_computation.10 | convolution fusion | flops 1073741824 | bytes 5242880 | tf_op jit(solution)/shard_map/dot_general | solution.py:44
  261.9 1.6 fusion.4
  263.6 4.8 %collective-permute-done.15.refs_7_ = bf16[1,192,256]{2,1,0:T(8,128)(2,1)S(1)} collective-permute-done((bf16[1,192,256]{2,1,0:T(8,128)(2,1)S(1)}, bf16[1,192,256]{2,1,0:T(8,128)(2,1)S(1)}, u32[]{:S(2)}, u32[]{:S(2)}) %collective-permute-start.15) | collective-permute-done | bytes 98336 | tf_op jit(solution)/shard_map/ppermute | solution.py:854
  269.1 2.5 shares.1
  271.5 1.4 copy.37
  (118 shorter events, 13.7 us)
Async XLA Ops:
  7.2 77.7 %all-gather.5.cloned.1.call-start = ((), (), s32[]{:S(2)}) async-start(), calls=%async_computation.4 | async-start | bytes 1769472 | tf_op jit(solution)/shard_map/all_gather | solution.py:880
  8.0 5.5 %collective-permute-start = (bf16[2,8,1024]{2,1,0:T(8,128)(2,1)S(1)}, bf16[2,8,1024]{2,1,0:T(8,128)(2,1)S(1)}, u32[]{:S(2)}, u32[]{:S(2)}) collective-permute-start(bf16[2,8,1024]{2,1,0:T(8,128)(2,1)S(1)} %slice.404), channel_id=1, source_target_pairs={{0,4},{4,8},{8,12},{12,16},{16,20},{20,24},{24,28},{1,5},{5,9},{9,... | collective-permute-start | bytes 98312 | tf_op jit(solution)/shard_map/ppermute | solution.py:923
  13.5 0.6 copy-start.15
  29.8 21.0 %copy-start.1 = (f32[512,128]{1,0:T(8,128)S(1)}, f32[512,128]{1,0:T(8,128)}, u32[]{:S(2)}) copy-start(f32[512,128]{1,0:T(8,128)} %get-tuple-element.125.proj_ref) | copy-start | bytes 786436
  29.8 21.0 %copy-start.4 = (bf16[512,1024]{1,0:T(8,128)(2,1)S(1)}, bf16[512,1024]{1,0:T(8,128)(2,1)}, u32[]{:S(2)}) copy-start(bf16[512,1024]{1,0:T(8,128)(2,1)} %constant.187.clone) | copy-start | bytes 3145732
  29.8 21.0 %copy-start.16 = (bf16[16,1024]{1,0:T(8,128)(2,1)S(1)}, bf16[16,1024]{1,0:T(8,128)(2,1)}, u32[]{:S(2)}) copy-start(bf16[16,1024]{1,0:T(8,128)(2,1)} %constant.186.clone) | copy-start | bytes 98308
  50.8 81.6 %all-gather.7.cloned.1.call-start = ((), (), s32[]{:S(2)}) async-start(), calls=%async_computation.5 | async-start | bytes 1179648 | tf_op jit(solution)/shard_map/all_gather | solution.py:880
  67.7 15.9 %copy-start.8 = (bf16[512,512]{1,0:T(8,128)(2,1)S(1)}, bf16[512,512]{1,0:T(8,128)(2,1)}, u32[]{:S(2)}) copy-start(bf16[512,512]{1,0:T(8,128)(2,1)} %constant.185.clone) | copy-start | bytes 1572868
  67.7 15.9 %copy-start.20 = (bf16[16,512]{1,0:T(8,128)(2,1)S(1)}, bf16[16,512]{1,0:T(8,128)(2,1)}, u32[]{:S(2)}) copy-start(bf16[16,512]{1,0:T(8,128)(2,1)} %constant.184.clone) | copy-start | bytes 49156
  84.8 132.8 %reduce-scatter.3.cloned.1.call-start = ((), (), s32[]{:S(2)}) async-start(), calls=%async_computation.2 | async-start | bytes 9437184 | tf_op jit(solution)/shard_map/reduce_scatter | solution.py:953
  132.4 0.9 copy-start.17
  132.4 1.2 copy-start.7
  132.4 136.0 %reduce-scatter.5.cloned.1.call-start = ((), (), s32[]{:S(2)}) async-start(), calls=%async_computation.3 | async-start | bytes 1310720 | tf_op jit(solution)/shard_map/reduce_scatter | solution.py:998
  134.9 38.3 %copy-start.9 = (bf16[64,2048]{1,0:T(8,128)(2,1)S(1)}, bf16[64,2048]{1,0:T(8,128)(2,1)}, u32[]{:S(2)}) copy-start(bf16[64,2048]{1,0:T(8,128)(2,1)} %rw_ref.1) | copy-start | bytes 786436
  173.1 2.6 copy-start.18
  173.1 2.7 copy-start.10
  177.2 16.0 %copy-start = (bf16[2,256,1024]{2,1,0:T(8,128)(2,1)S(1)}, bf16[2,256,1024]{2,1,0:T(8,128)(2,1)}, u32[]{:S(2)}) copy-start(bf16[2,256,1024]{2,1,0:T(8,128)(2,1)} %param.21) | copy-start | bytes 3145732
  177.2 16.0 %copy-start.23 = (bf16[512,2048]{1,0:T(8,128)(2,1)S(1)}, bf16[512,2048]{1,0:T(8,128)(2,1)}, u32[]{:S(2)}) copy-start(bf16[512,2048]{1,0:T(8,128)(2,1)} %get-tuple-element.159.gated_ref) | copy-start | bytes 6291460
  188.6 10.1 %copy-start.5 = (bf16[16,128,256]{2,1,0:T(8,128)(2,1)S(1)}, bf16[16,128,256]{2,1,0:T(8,128)(2,1)}, u32[]{:S(2)}) copy-start(bf16[16,128,256]{2,1,0:T(8,128)(2,1)} %get-tuple-element.156) | copy-start | bytes 3145732
  188.7 10.0 %collective-permute-start.1 = (bf16[16,128,256]{2,1,0:T(8,128)(2,1)}, bf16[16,128,256]{2,1,0:T(8,128)(2,1)S(1)}, u32[]{:S(2)}, u32[]{:S(2)}) collective-permute-start(bf16[16,128,256]{2,1,0:T(8,128)(2,1)} %get-tuple-element.158), channel_id=1, source_target_pairs={{0,4},{4,0},{8,12},{12,8},{16,20},{20,16},{24,28},{28,24},{1,5},{5... | collective-permute-start | bytes 3145736 | tf_op jit(solution)/shard_map/ppermute | solution.py:860
  199.8 16.0 %collective-permute-start.2 = (bf16[4,128,256]{2,1,0:T(8,128)(2,1)S(1)}, bf16[4,128,256]{2,1,0:T(8,128)(2,1)S(1)}, u32[]{:S(2)}, u32[]{:S(2)}) collective-permute-start(bf16[4,128,256]{2,1,0:T(8,128)(2,1)S(1)} %get-tuple-element.165), channel_id=1, source_target_pairs={{0,16},{4,20},{8,24},{12,28},{16,0},{20,4},{24,8},{28,12},{1,17},{... | collective-permute-start | bytes 786440 | tf_op jit(solution)/shard_map/ppermute | solution.py:854
  201.1 14.7 %collective-permute-start.3 = (bf16[4,128,256]{2,1,0:T(8,128)(2,1)S(1)}, bf16[4,128,256]{2,1,0:T(8,128)(2,1)}, u32[]{:S(2)}, u32[]{:S(2)}) collective-permute-start(bf16[4,128,256]{2,1,0:T(8,128)(2,1)S(1)} %get-tuple-element.166), channel_id=1, source_target_pairs={{0,8},{4,12},{8,0},{12,4},{16,24},{20,28},{24,16},{28,20},{1,9},{5... | collective-permute-start | bytes 786440 | tf_op jit(solution)/shard_map/ppermute | solution.py:854
  201.1 16.4 %collective-permute-start.4 = (bf16[4,128,256]{2,1,0:T(8,128)(2,1)S(1)}, bf16[4,128,256]{2,1,0:T(8,128)(2,1)}, u32[]{:S(2)}, u32[]{:S(2)}) collective-permute-start(bf16[4,128,256]{2,1,0:T(8,128)(2,1)S(1)} %get-tuple-element.167), channel_id=1, source_target_pairs={{0,24},{4,28},{8,16},{12,20},{16,8},{20,12},{24,0},{28,4},{1,25},{... | collective-permute-start | bytes 786440 | tf_op jit(solution)/shard_map/ppermute | solution.py:854
  203.3 11.6 %copy-start.13 = (f32[16,1024]{1,0:T(8,128)S(1)}, f32[16,1024]{1,0:T(8,128)}, u32[]{:S(2)}) copy-start(f32[16,1024]{1,0:T(8,128)} %get-tuple-element.169) | copy-start | bytes 196612
  203.3 14.6 %copy-start.19 = (f32[1024]{0:T(1024)S(1)}, f32[1024]{0:T(1024)}, u32[]{:S(2)}) copy-start(f32[1024]{0:T(1024)} %param.23) | copy-start | bytes 12292
  203.3 18.3 %copy-start.14 = (f32[16,1024]{1,0:T(8,128)S(1)}, f32[16,1024]{1,0:T(8,128)}, u32[]{:S(2)}) copy-start(f32[16,1024]{1,0:T(8,128)} %get-tuple-element.191) | copy-start | bytes 196612
  214.8 8.4 %copy-start.3 = (bf16[16,192,256]{2,1,0:T(8,128)(2,1)S(1)}, bf16[16,192,256]{2,1,0:T(8,128)(2,1)}, u32[]{:S(2)}) copy-start(bf16[16,192,256]{2,1,0:T(8,128)(2,1)} %get-tuple-element.163) | copy-start | bytes 4718596
  217.5 5.7 %collective-permute-start.5 = (bf16[16,192,256]{2,1,0:T(8,128)(2,1)}, bf16[16,192,256]{2,1,0:T(8,128)(2,1)}, u32[]{:S(2)}, u32[]{:S(2)}) collective-permute-start(bf16[16,192,256]{2,1,0:T(8,128)(2,1)} %get-tuple-element.172), channel_id=1, source_target_pairs={{0,4},{4,0},{8,12},{12,8},{16,20},{20,16},{24,28},{28,24},{1,5},{5... | collective-permute-start | bytes 4718600 | tf_op jit(solution)/shard_map/ppermute | solution.py:860
  220.1 3.1 %collective-permute-start.9 = (bf16[2,3,2048]{2,1,0:T(4,128)(2,1)S(1)}, bf16[2,3,2048]{2,1,0:T(4,128)(2,1)S(1)}, u32[]{:S(2)}, u32[]{:S(2)}) collective-permute-start(bf16[2,3,2048]{2,1,0:T(4,128)(2,1)S(1)} %slice.559), channel_id=1, source_target_pairs={{4,0},{8,4},{12,8},{16,12},{20,16},{24,20},{28,24},{5,1},{9,5},{13... | collective-permute-start | bytes 73736 | tf_op jit(solution)/shard_map/ppermute | solution.py:990
  223.2 6.1 %copy-start.22 = (bf16[512,2048]{1,0:T(8,128)(2,1)S(1)}, bf16[512,2048]{1,0:T(8,128)(2,1)}, u32[]{:S(2)}) copy-start(bf16[512,2048]{1,0:T(8,128)(2,1)} %get-tuple-element.187.gate_ref) | copy-start | bytes 6291460
  225.2 8.8 %copy-start.2 = (f32[4,128,256]{2,1,0:T(8,128)S(1)}, f32[4,128,256]{2,1,0:T(8,128)}, u32[]{:S(2)}) copy-start(f32[4,128,256]{2,1,0:T(8,128)} %get-tuple-element.195) | copy-start | bytes 1572868
  225.2 14.6 %collective-permute-start.6 = (bf16[4,192,256]{2,1,0:T(8,128)(2,1)S(1)}, bf16[4,192,256]{2,1,0:T(8,128)(2,1)S(1)}, u32[]{:S(2)}, u32[]{:S(2)}) collective-permute-start(bf16[4,192,256]{2,1,0:T(8,128)(2,1)S(1)} %get-tuple-element.178), channel_id=1, source_target_pairs={{0,16},{4,20},{8,24},{12,28},{16,0},{20,4},{24,8},{28,12},{1,17},{... | collective-permute-start | bytes 1179656 | tf_op jit(solution)/shard_map/ppermute | solution.py:854
  227.8 12.5 %collective-permute-start.7 = (bf16[4,192,256]{2,1,0:T(8,128)(2,1)S(1)}, bf16[4,192,256]{2,1,0:T(8,128)(2,1)S(1)}, u32[]{:S(2)}, u32[]{:S(2)}) collective-permute-start(bf16[4,192,256]{2,1,0:T(8,128)(2,1)S(1)} %get-tuple-element.179), channel_id=1, source_target_pairs={{0,8},{4,12},{8,0},{12,4},{16,24},{20,28},{24,16},{28,20},{1,9},{5... | collective-permute-start | bytes 1179656 | tf_op jit(solution)/shard_map/ppermute | solution.py:854
  228.3 18.6 %collective-permute-start.8 = (bf16[4,192,256]{2,1,0:T(8,128)(2,1)S(1)}, bf16[4,192,256]{2,1,0:T(8,128)(2,1)S(1)}, u32[]{:S(2)}, u32[]{:S(2)}) collective-permute-start(bf16[4,192,256]{2,1,0:T(8,128)(2,1)S(1)} %get-tuple-element.180), channel_id=1, source_target_pairs={{0,24},{4,28},{8,16},{12,20},{16,8},{20,12},{24,0},{28,4},{1,25},{... | collective-permute-start | bytes 1179656 | tf_op jit(solution)/shard_map/ppermute | solution.py:854
  235.8 25.5 %collective-permute-start.10 = (bf16[1,128,256]{2,1,0:T(8,128)(2,1)}, bf16[1,128,256]{2,1,0:T(8,128)(2,1)S(1)}, u32[]{:S(2)}, u32[]{:S(2)}) collective-permute-start(bf16[1,128,256]{2,1,0:T(8,128)(2,1)} %get-tuple-element.274), channel_id=1, source_target_pairs={{0,2},{1,3},{2,0},{3,1},{4,6},{5,7},{6,4},{7,5},{8,10},{9,11},{10,... | collective-permute-start | bytes 196616 | tf_op jit(solution)/shard_map/ppermute | solution.py:854
  238.3 25.2 %collective-permute-start.11 = (bf16[1,128,256]{2,1,0:T(8,128)(2,1)}, bf16[1,128,256]{2,1,0:T(8,128)(2,1)}, u32[]{:S(2)}, u32[]{:S(2)}) collective-permute-start(bf16[1,128,256]{2,1,0:T(8,128)(2,1)} %get-tuple-element.273), channel_id=1, source_target_pairs={{0,1},{1,0},{2,3},{3,2},{4,5},{5,4},{6,7},{7,6},{8,9},{9,8},{10,11... | collective-permute-start | bytes 196616 | tf_op jit(solution)/shard_map/ppermute | solution.py:854
  239.8 23.7 %collective-permute-start.12 = (bf16[1,128,256]{2,1,0:T(8,128)(2,1)}, bf16[1,128,256]{2,1,0:T(8,128)(2,1)}, u32[]{:S(2)}, u32[]{:S(2)}) collective-permute-start(bf16[1,128,256]{2,1,0:T(8,128)(2,1)} %get-tuple-element.272), channel_id=1, source_target_pairs={{0,3},{1,2},{2,1},{3,0},{4,7},{5,6},{6,5},{7,4},{8,11},{9,10},{10,... | collective-permute-start | bytes 196616 | tf_op jit(solution)/shard_map/ppermute | solution.py:854
  247.8 15.8 %collective-permute-start.13 = (bf16[1,192,256]{2,1,0:T(8,128)(2,1)}, bf16[1,192,256]{2,1,0:T(8,128)(2,1)}, u32[]{:S(2)}, u32[]{:S(2)}) collective-permute-start(bf16[1,192,256]{2,1,0:T(8,128)(2,1)} %get-tuple-element.200), channel_id=1, source_target_pairs={{0,2},{1,3},{2,0},{3,1},{4,6},{5,7},{6,4},{7,5},{8,10},{9,11},{10,... | collective-permute-start | bytes 294920 | tf_op jit(solution)/shard_map/ppermute | solution.py:854
  250.2 13.4 %collective-permute-start.14 = (bf16[1,192,256]{2,1,0:T(8,128)(2,1)S(1)}, bf16[1,192,256]{2,1,0:T(8,128)(2,1)}, u32[]{:S(2)}, u32[]{:S(2)}) collective-permute-start(bf16[1,192,256]{2,1,0:T(8,128)(2,1)S(1)} %get-tuple-element.201), channel_id=1, source_target_pairs={{0,1},{1,0},{2,3},{3,2},{4,5},{5,4},{6,7},{7,6},{8,9},{9,8},{10,11... | collective-permute-start | bytes 294920 | tf_op jit(solution)/shard_map/ppermute | solution.py:854
  254.5 3.3 %copy-start.21 = (bf16[2,256,1024]{2,1,0:T(8,128)(2,1)S(1)}, bf16[2,256,1024]{2,1,0:T(8,128)(2,1)}, u32[]{:S(2)}) copy-start(bf16[2,256,1024]{2,1,0:T(8,128)(2,1)} %scatter.9) | copy-start | bytes 3145732
  260.7 1.2 copy-start.6
  261.4 2.2 copy-start.12
  261.4 7.0 %collective-permute-start.15 = (bf16[1,192,256]{2,1,0:T(8,128)(2,1)S(1)}, bf16[1,192,256]{2,1,0:T(8,128)(2,1)S(1)}, u32[]{:S(2)}, u32[]{:S(2)}) collective-permute-start(bf16[1,192,256]{2,1,0:T(8,128)(2,1)S(1)} %get-tuple-element.202), channel_id=1, source_target_pairs={{0,3},{1,2},{2,1},{3,0},{4,7},{5,6},{6,5},{7,4},{8,11},{9,10},{10,... | collective-permute-start | bytes 294920 | tf_op jit(solution)/shard_map/ppermute | solution.py:854
  268.4 0.6 copy-start.11
Sparse Core Ops, SparseCore 0:
  50.9 28.2 all-gather.4
  84.9 26.3 all-gather.6
  132.6 76.9 reduce-scatter.2
  222.6 33.6 reduce-scatter.4

commit v3 on v2

--- a/solution.py
+++ b/solution.py
@@ -67,14 +67,15 @@
         return 0
 
     lax.fori_loop(0, rows // 64, steps, 0)
-    for s in range(nseq):
-        for l in range(NL):
-            span = jnp.sum(dl_ref[l, s * length : (s + 1) * length, :], axis=0, keepdims=True)
-            high = span.astype(bf16).astype(f32)
-            for i, v in enumerate((high, span - high)):
-                at = nseq * (N + i) + s
-                block_ref[at : at + 1, lane(l)] = v
-    block_ref[nseq * (N + 2) :, :] = jnp.zeros((block_ref.shape[0] - nseq * (N + 2), WIDTH), f32)
+    fill = block_ref.shape[0] - nseq * (N + 2)
+    for l in range(NL):
+        spans = [
+            jnp.sum(dl_ref[l, s * length : (s + 1) * length, :], axis=0, keepdims=True) for s in range(nseq)
+        ]
+        highs = [span.astype(bf16).astype(f32) for span in spans]
+        lows = [span - high for span, high in zip(spans, highs)]
+        rows_of = jnp.concatenate(highs + lows + [jnp.zeros((fill, 128), f32)], axis=0)
+        block_ref[nseq * N :, lane(l)] = rows_of.astype(bf16)
 
     def step(c, h):
         h = [list(v) for v in h]
@@ -91,7 +92,7 @@
     h = lax.fori_loop(0, length // T, step, ((z,) * NL,) * nseq)
     for s in range(nseq):
         for l in range(NL):
-            block_ref[s * N : (s + 1) * N, lane(l)] = h[s][l]
+            block_ref[s * N : (s + 1) * N, lane(l)] = h[s][l].astype(bf16)
 
 
 def adjoint_end_kernel(dl_ref, g_ref, log_ref, cb_ref, sb_ref, a2_ref, *, nseq, length):
@@ -334,7 +335,7 @@
         (proj, rate_weight, rate_bias, x, log, bb),
         [whole(proj), block_of(rate_weight.shape[0]), block_of(1), tiles_of(rows), block_of(N), whole(bb)],
         [block_of(block_rows(nseq)), tiles_of(rows), tiles_of(rows)],
-        (o((block_rows(nseq), ch), f32), o(x.shape, f32), o(x.shape, f32)),
+        (o((block_rows(nseq), ch), bf16), o(x.shape, f32), o(x.shape, f32)),
         2 * 10**10, nseq=nseq, length=length,
         scratch=[pltpu.VMEM((N, WIDTH), f32), pltpu.VMEM((rows, WIDTH), f32)],
     )
@@ -445,9 +446,13 @@
     )
 
 
+def filled(weight):
+    return jnp.concatenate([weight, jnp.zeros((128 - weight.shape[0], weight.shape[1]), weight.dtype)], axis=0)
+
+
 def inner_kernel(
     tok_ref, halo_ref, gain_ref, wi_ref, cw_ref, cb_ref, sw_ref,
-    normed_ref, inner_ref, before_ref, x_ref, slope_ref, proj_ref, ext_ref, flat_ref, *, nseq, length,
+    normed_ref, inner_ref, before_ref, x_ref, slope_ref, proj_ref, meet_ref, ext_ref, flat_ref, *, nseq, length, rank,
 ):
     @pl.when(pl.program_id(0) == 0)
     def _():
@@ -493,29 +498,39 @@
             return 0
 
         lax.fori_loop(0, length // ROWS, mix, 0)
-    proj_ref[...] += jnp.dot(flat_ref[...], sw_ref[...], preferred_element_type=f32)
-
-
-def inner_side(tokens, halo, gain, in_weight, conv_weight, conv_bias, select_weight, nseq, length):
+    proj_ref[...] += rows_dot(flat_ref[...], filled(sw_ref[...]))
+
+    @pl.when(pl.program_id(0) == pl.num_programs(0) - 1)
+    def _():
+        values = proj_ref[...]
+        lanes = lax.broadcasted_iota(jnp.int32, values.shape, 1)
+        products = values * pltpu.roll(values, 128 - N, 1)
+        own = (lanes >= rank) & (lanes < rank + N)
+        total = jnp.sum(jnp.where(own, products, 0.0), axis=1, keepdims=True)
+        meet_ref[...] = jnp.broadcast_to(total, meet_ref.shape)
+
+
+def inner_side(tokens, halo, gain, in_weight, conv_weight, conv_bias, select_weight, nseq, length, rank):
     rows, model = tokens.shape
-    inner, picks = select_weight.shape
+    picks, inner = select_weight.shape
     o = jax.ShapeDtypeStruct
     operands = (tokens, halo, gain, in_weight, conv_weight, conv_bias, select_weight)
     specs = [
         whole(tokens), whole(halo), whole(gain), block_of(model), block_of(conv_weight.shape[0]), block_of(1),
-        pl.BlockSpec((WIDTH, picks), lambda j: (j, 0)),
+        block_of(picks),
     ]
+    square = pl.BlockSpec((rows, 128), lambda j: (0, 0))
     return pl.pallas_call(
-        functools.partial(inner_kernel, nseq=nseq, length=length),
+        functools.partial(inner_kernel, nseq=nseq, length=length, rank=rank),
         grid=(inner // WIDTH,),
         in_specs=specs,
         out_specs=[
             pl.BlockSpec((rows, model), lambda j: (0, 0)), block_of(rows), block_of(halo.shape[0]), tiles_of(rows), block_of(rows),
-            pl.BlockSpec((rows, picks), lambda j: (0, 0)),
+            square, square,
         ],
         out_shape=(
             o((rows, model), bf16), o((rows, inner), bf16), o((halo.shape[0], inner), bf16), o((inner // 128, rows, 128), bf16),
-            o((rows, inner), f32), o((rows, picks), f32),
+            o((rows, inner), f32), o((rows, 128), f32), o((rows, 128), f32),
         ),
         scratch_shapes=[pltpu.VMEM((nseq, NL, PAD + length, 128), f32), pltpu.VMEM((rows, WIDTH), bf16)],
         compiler_params=pltpu.CompilerParams(vmem_limit_bytes=VMEM, dimension_semantics=("arbitrary",)),
@@ -535,7 +550,9 @@
     taps = cw_ref.shape[0]
     j = pl.program_id(0)
     wide = pg_ref.shape[1]
-    back_ref[...] = cp_ref[...] + rows_dot(pg_ref[:, wide // 2 :], sw_ref[...])
+    back_ref[...] = cp_ref[...] + jnp.dot(
+        pg_ref[:, wide // 2 :], filled(sw_ref[...]), preferred_element_type=f32
+    )
     vec_ref[...] = jnp.zeros_like(vec_ref)
     small_step = 32
     for s in range(nseq):
@@ -677,7 +694,7 @@
 
     specs = [
         block_of(rows), block_of(rows), block_of(before.shape[0]), tiles_of(rows), block_of(rows), whole(pg),
-        pl.BlockSpec((WIDTH, wide // 2), lambda j: (j, 0)), block_of(conv_weight.shape[0]), whole(turned),
+        block_of(select_weight.shape[0]), block_of(conv_weight.shape[0]), whole(turned),
         whole(halo), whole(gain), block_of(rows), whole(proj), block_of(N), block_of(8), block_of(8),
     ]
     packed = pl.BlockSpec((count // 2, packed_rows, wide), lambda j: (0, 0, 0))
@@ -762,7 +779,7 @@
     )(gated, gate_grad, cot, turned)
 
 
-def share_kernel(*refs, count, rank, taps, part, part_rows, picks):
+def share_kernel(place_ref, *refs, count, rank, taps, part, part_rows, picks):
     first, second = refs[:count], refs[count : 2 * count]
     summed_ref, weight_ref, gain_ref = refs[2 * count : 2 * count + 3]
     in_ref, out_ref, conv_ref, bias_ref, select_ref, rate_ref, rate_bias_ref, decay_ref, skip_ref, norm_ref = refs[
@@ -789,7 +806,9 @@
     gain = jnp.broadcast_to(gain, (part_rows, 128))
     if part_rows < 8:
         gain = jnp.concatenate([gain, jnp.zeros((8 - part_rows, 128), f32)], axis=0)
-    norm_ref[...] = gain.T[:1, :part_rows] / gain_ref[...]
+    gains = gain_ref[...]
+    gains = pltpu.roll(gains, gains.shape[1] - place_ref[0] * part_rows, 1)
+    norm_ref[...] = gain.T[:1, :part_rows] / gains[:, :part_rows]
     small = total(second, each * pad, padded(part))[:part]
     turned = small[:, : wide // 2].T
     rate_ref[...] = turned[:rank]
@@ -797,25 +816,37 @@
     bias_ref[...] = turned[rank + taps : rank + taps + 1]
     rate_bias_ref[...] = turned[rank + taps + 1 : rank + taps + 2]
     skip_ref[...] = turned[rank + taps + 2 : rank + taps + 3]
-    decay_ref[...] = turned[rank + 8 : rank + 8 + N].T
+    decay_ref[...] = turned[rank + 8 : rank + 8 + N]
     select_ref[...] = small[:, wide // 2 : wide // 2 + picks]
 
 
-def shares_of(first, second, summed, own_weight, own_gain, rank, taps, part, picks):
-    part_rows, width = own_weight.shape
+def shares_of(first, second, summed, in_weight, gain, place, rank, taps, part, part_rows, picks):
+    width = in_weight.shape[1]
     model = summed.shape[1]
     o = lambda *shape: jax.ShapeDtypeStruct(shape, f32)
+    own = pl.BlockSpec((part_rows, width), lambda i, s: (s[0], 0))
+    if part_rows % 16:
+        in_weight = lax.dynamic_slice_in_dim(in_weight, place * part_rows, part_rows, 0)
+        own = pl.BlockSpec((part_rows, width), lambda i, s: (0, 0))
+    fixed = lambda shape: pl.BlockSpec(shape, lambda i, s: (0,) * len(shape))
+    arrays = (*first, *second, summed, in_weight, gain)
+    specs = [fixed(a.shape) for a in arrays]
+    specs[-2] = own
+    outs = (
+        o(part_rows, width), o(part, model), o(taps, part), o(1, part), o(part, picks), o(rank, part), o(1, part),
+        o(N, part), o(1, part), o(1, part_rows),
+    )
     return pl.pallas_call(
         functools.partial(
             share_kernel, count=len(first), rank=rank, taps=taps, part=part, part_rows=part_rows, picks=picks
         ),
-        out_shape=(
-            o(part_rows, width), o(part, model), o(taps, part), o(1, part), o(part, picks), o(rank, part), o(1, part),
-            o(part, N), o(1, part), o(1, part_rows),
+        grid_spec=pltpu.PrefetchScalarGridSpec(
+            num_scalar_prefetch=1, grid=(1,), in_specs=specs, out_specs=[fixed(out.shape) for out in outs],
         ),
-        compiler_params=pltpu.CompilerParams(vmem_limit_bytes=VMEM),
+        out_shape=outs,
+        compiler_params=pltpu.CompilerParams(vmem_limit_bytes=VMEM, dimension_semantics=("arbitrary",)),
         name="shares",
-    )(*first, *second, summed, own_weight, own_gain)
+    )(place[None].astype(jnp.int32), *arrays)
 
 
 def flip_bit(axis, bit):
@@ -877,7 +908,7 @@
 
 def carried(block, shape, rates, backward, after=None, spans=None):
     count, mine = lax.axis_size("seq"), lax.axis_index("seq")
-    blocks = lax.all_gather(block.astype(bf16), "seq")
+    blocks = lax.all_gather(block, "seq")
     if after is not None:
         blocks, after = lax.optimization_barrier((blocks, after))
     rows = shape[0] * shape[1]
@@ -923,16 +954,16 @@
     halo = lax.ppermute(tokens[:, length - PAD :], "seq", [(i, i + 1) for i in range(pieces - 1)])
     halo = halo.reshape(nseq * PAD, model)
     picks, wide = rank + 2 * N, 256
-    select_weight = jnp.pad(select_weight, ((0, 0), (0, wide // 2 - picks)))
-    normed, inner, before, x, slope, proj = inner_side(
-        tok, halo, gain, in_weight, conv_weight, bias, select_weight, nseq, length
+    select_weight = select_weight.T
+    normed, inner, before, x, slope, proj, bc = inner_side(
+        tok, halo, gain, in_weight, conv_weight, bias, select_weight, nseq, length, rank
     )
     in_gate, out_gate = proj[:, rank : rank + N], proj[:, rank + N : picks]
     log = decay_log.T
     rates = -jnp.exp(log)
     bb = jnp.broadcast_to(in_gate[:, :, None], (rows, N, 128))
     ahead, dl, u = state_end(proj, rate_weight, rate_bias[None], x, log, bb, nseq, length)
-    ahead, cot = lax.optimization_barrier((ahead.astype(bf16), cot))
+    ahead, cot = lax.optimization_barrier((ahead, cot))
     turned, g, ga, gs = gate_side(normed, cot, in_weight, out_weight)
     state_shape = (nseq, N, inner_width)
     entering, _, spans = carried(ahead, state_shape, rates, False)
@@ -941,8 +972,6 @@
     lc = spread(out_gate, nseq, length, 1, False)
     lb = spread(in_gate, nseq, length, 2, True)
     ls = jnp.asarray(own_column(nseq * T, T, nseq, 2, 1, True))
-    meet = jnp.sum(in_gate * out_gate, axis=1, keepdims=True)
-    bc = jnp.broadcast_to(meet, (rows, 128))
     behind, lb, ls, u = lax.optimization_barrier((sent_back, lb, ls, u))
     states, gated, gate_grad, out_grad, shift, skip_grad = forward(
         dl, u, g, ga, gs, x, skip, bb, bc, lc, log, entering, nseq, length, 4
@@ -992,16 +1021,16 @@
     normed_grad = rows_dot(gate_grad, in_weight[:, inner_width:])
     *first_held, normed_grad = lax.optimization_barrier((*first_held, normed_grad))
     first_held, _ = remaining_rounds(first_held, rounds[2:], None)
-    held, (returned, second_grad, normed_grad) = remaining_rounds(
-        held, rounds[2:], (returned, second_grad, normed_grad)
+    held, (returned, second_grad, normed_grad, second_tail) = remaining_rounds(
+        held, rounds[2:], (returned, second_grad, normed_grad, second_tail)
     )
     weight_share = lax.psum_scatter(weight_sum, "grp", scatter_dimension=0, tiled=True)[0]
-    first = (lax.axis_index("seq") * grp + lax.axis_index("grp")) * part_rows
-    own_weight = lax.dynamic_slice_in_dim(in_weight, first, part_rows, 0)
-    own_gain = lax.dynamic_slice_in_dim(norm_gain, first, part_rows, 0)[None]
     in_share, out_share, conv_share, bias_share, select_share, rate_share, rate_bias_share, decay_share, skip_share, (
         gain_share
-    ) = shares_of(first_held, held, weight_share, own_weight, own_gain, rank, taps, part, picks)
+    ) = shares_of(
+        first_held, held, weight_share, in_weight, gain, lax.axis_index("seq") * grp + lax.axis_index("grp"), rank,
+        taps, part, part_rows, picks,
+    )
     tail = jnp.concatenate([first_tail, second_tail], axis=1)
     fixed = (tail.reshape(nseq, PAD, inner_width)[:, PAD - taps + 1 :] + returned).astype(bf16)
 
@@ -1029,7 +1058,7 @@
         select_share,
         rate_share,
         rate_bias_share[0],
-        decay_share,
+        decay_share.T,
         skip_share[0],
         out_share,
     )

time: 281 us -> 275 us (0.979)
  local copies, waits for them, and re-layouts: 18.6 us -> 13.8 us
  other arithmetic: 19.2 us -> 14.9 us
    ppermute x12, starting transfers between devices: 16.5 us -> 19.6 us  [round_trade(): held.append(lax.ppermute(parts[i], bits[0][0], flip_bit(bits[0][0], flip)))]
  transfers between devices with their start and end apart: 20 -> 20, of which waited for: 4 -> 5; matrix products, arithmetic and copies ran while one was open for 18% -> 16% of each run, Pallas kernels for 48% -> 49%
where the time goes in v3:
time: 275 us; the launch traced here: 274 us
  Pallas kernels  167 us (61%)
  starting transfers between devices  27.2 us (10%)
  matrix products  21.2 us (8%)
  waiting for transfers between devices  15.4 us (6%)
  other arithmetic  14.9 us (5%)
  between operations  14.5 us (5%)
  local copies, waits for them, and re-layouts  13.8 us (5%)
    pallas_call x5, Pallas kernels, kernel_call(): pl.pallas_call(functools.partial(body, **options), grid=(channels // WIDT...  119 us
    pallas_call x2, Pallas kernels, input_grads(): pl.pallas_call(functools.partial(input_grad_kernel, nseq=nseq, length=len...  23.2 us
    ppermute x12, starting transfers between devices, round_trade(): held.append(lax.ppermute(parts[i], bits[0][0], flip_bit(bits[0][0], flip)))  19.6 us
    ppermute x12, waiting for transfers between devices, round_trade(): held.append(lax.ppermute(parts[i], bits[0][0], flip_bit(bits[0][0], flip)))  14 us
    dot_general x4, matrix products, rows_dot(): lax.dot_general(left, right, (((1,), (1,)), ((), ())), preferred_element_...  13.1 us
    pallas_call x1, Pallas kernels, inner_side(): pl.pallas_call(functools.partial(inner_kernel, nseq=nseq, length=length,...  12.4 us
    pallas_call x1, Pallas kernels, weight_grads(): pl.pallas_call(functools.partial(weight_grad_kernel, part=part), grid=(wi...  10.4 us
    dot_general x1, matrix products, shards(): jnp.dot(gated, out_weight, preferred_element_type=f32)  5.51 us
  transfers between devices with their start and end apart: 20, of which 5 were waited for; matrix products, arithmetic and copies ran while one was open for 16% of the time, Pallas kernels for 49%

profile of v3, /device:TPU:0, one launch (start us, length us, event | category | flops | bytes accessed | tf_op | source)
XLA Modules:
  0.0 274.0 jit_solution(7689818992771753252)
XLA Ops:
  8.0 2.3 collective-permute-start
  10.3 0.9 exponential_negate_fusion
  11.9 12.4 %inner_side.1 = (bf16[512,1024]{1,0:T(8,128)(2,1)}, bf16[512,2048]{1,0:T(8,128)(2,1)}, bf16[16,2048]{1,0:T(8,128)(2,1)}, bf16[16,512,128]{2,1,0:T(8,128)(2,1)}, ...) custom-call(bf16[512,1024]{1,0:T(8,128)(2,1)} %bitcast.121, bf16[16,1024]{1,0:T(8,128)(2,1)} %bitcast.155, ...), custom_call_target="tpu_custom_call" | custom-call | flops 2147483648 | bytes 14680064 | tf_op jit(solution)/shard_map/inner_side/pallas_call | solution.py:523
  24.3 1.2 fusion.51
  25.6 2.6 broadcast_in_dim.24.bb_ref
  28.2 19.2 %state_end.1 = (bf16[48,2048]{1,0:T(8,128)(2,1)}, f32[16,512,128]{2,1,0:T(8,128)}, f32[16,512,128]{2,1,0:T(8,128)}) custom-call(f32[512,128]{1,0:T(8,128)} %get-tuple-element.127.proj_ref, bf16[64,2048]{1,0:T(8,128)(2,1)} %rw_ref.1, f32[1,2048]{1,0:T(1,128)} %bitcast.165, bf16[16,512,128]{2,1,0:T(8,128)(2,1)} %get-tuple-element.128.x_ref, ...), custom_call_target="tpu_custom_call" | custom-call | flops 20000000000 | bytes 15540224 | tf_op jit(solution)/shard_map/state_end/pallas_call | solution.py:294
  47.5 1.4 fusion.10.lb_ref
  48.9 12.8 %gate_side.1 = (bf16[1024,512]{1,0:T(8,128)(2,1)}, f32[16,512,128]{2,1,0:T(8,128)}, f32[16,512,128]{2,1,0:T(8,128)}, f32[16,512,128]{2,1,0:T(8,128)}) custom-call(bf16[512,1024]{1,0:T(8,128)(2,1)} %get-tuple-element.130.normed_ref, bf16[512,1024]{1,0:T(8,128)(2,1)} %bitcast.123, bf16[1024,4096]{1,0:T(8,128)(2,1)} %refs_9_.1, bf16[2048,1024]{1,0:T(8,128)(2,1)} %ow_ref.1), custom_call_target="tpu_custom_call" | custom-call | flops 4294967296 | bytes 28311552 | tf_op jit(solution)/shard_map/gate_side/pallas_call | solution.py:294
  61.7 2.6 broadcast_in_dim.25.cb_ref
  64.3 15.9 %adjoint_end.1 = bf16[32,2048]{1,0:T(8,128)(2,1)} custom-call(f32[16,512,128]{2,1,0:T(8,128)} %get-tuple-element.129.dl_ref, f32[16,512,128]{2,1,0:T(8,128)} %get-tuple-element.133.g_ref, f32[16,2048]{1,0:T(8,128)} %bitcast.148, f32[512,16,128]{2,1,0:T(8,128)} %broadcast_in_dim.25.cb_ref), custom_call_target="tpu_custom_call" | custom-call | flops 20000000000 | bytes 12845056 | tf_op jit(solution)/shard_map/adjoint_end/pallas_call | solution.py:294
  80.2 1.1 fusion.11.lc_ref
  81.4 1.8 fusion.20
  83.5 1.1 add_select_fusion.hin_ref
  84.6 33.1 %forward.1 = (bf16[8192,2048]{1,0:T(8,128)(2,1)}, bf16[512,2048]{1,0:T(8,128)(2,1)}, bf16[512,2048]{1,0:T(8,128)(2,1)}, f32[32,256]{1,0:T(8,128)}, f32[512,128]{1,0:T(8,128)}, /*index=5*/f32[8,2048]{1,0:T(8,128)}) custom-call(f32[16,512,128]{2,1,0:T(8,128)} %get-tuple-element.129.dl_ref, f32[16,512,128]{2,1,0:T(8,128)} %get-tuple-element.135.u_ref, ...), custom_call_target="tpu_custom_call" | custom-call | flops 30000001024 | bytes 66560000 | tf_op jit(solution)/shard_map/forward/pallas_call | solution.py:294
  117.7 10.4 %weight_grads.1 = bf16[32,128,1024]{2,1,0:T(8,128)(2,1)} custom-call(bf16[512,2048]{1,0:T(8,128)(2,1)} %get-tuple-element.162.gated_ref, bf16[512,2048]{1,0:T(8,128)(2,1)} %get-tuple-element.190.gate_ref, bf16[512,1024]{1,0:T(8,128)(2,1)} %bitcast.124, bf16[1024,512]{1,0:T(8,128)(2,1)} %get-tuple-element.145.turned_ref), custom_call_target="tpu_custom_call" | custom-call | flops 4294967296 | bytes 14680064 | tf_op jit(solution)/shard_map/weight_grads/pallas_call | solution.py:770
  129.4 1.1 fusion.12.lin_ref
  130.5 37.8 %backward.1 = (bf16[512,2048]{1,0:T(8,128)(2,1)}, f32[512,2048]{1,0:T(8,128)}, f32[32,256]{1,0:T(8,128)}, f32[16,2048]{1,0:T(8,128)}, f32[8,2048]{1,0:T(8,128)}) custom-call(f32[16,512,128]{2,1,0:T(8,128)} %get-tuple-element.129.dl_ref, f32[16,512,128]{2,1,0:T(8,128)} %get-tuple-element.135.u_ref, f32[16,512,128]{2,1,0:T(8,128)} %get-tuple-element.133.g_ref, ...), custom_call_target="tpu_custom_call" | custom-call | flops 49999998976 | bytes 60465152 | tf_op jit(solution)/shard_map/backward/pallas_call | solution.py:294
  168.3 2.4 convolution_convert_fusion.2
  171.4 0.9 concatenate.17.pg_ref
  172.4 11.6 %input_grads.2 = (bf16[16,128,256]{2,1,0:T(8,128)(2,1)}, bf16[16,128,256]{2,1,0:T(8,128)(2,1)}, bf16[512,1024]{1,0:T(8,128)(2,1)}, f32[16,1024]{1,0:T(8,128)}, f...) custom-call(s32[33]{0:T(128)} %pad_add_fusion.place_ref, f32[512,2048]{1,0:T(8,128)} %get-tuple-element.164.cp_ref, ...), custom_call_target="tpu_custom_call" | custom-call | flops 12884901888 | bytes 16777216 | tf_op jit(solution)/shard_map/input_grads/pallas_call | solution.py:718
  184.0 3.4 %collective-permute-start.1 = (bf16[16,128,256]{2,1,0:T(8,128)(2,1)}, bf16[16,128,256]{2,1,0:T(8,128)(2,1)S(1)}, u32[]{:S(2)}, u32[]{:S(2)}) collective-permute-start(bf16[16,128,256]{2,1,0:T(8,128)(2,1)} %get-tuple-element.161), channel_id=1, source_target_pairs={{0,4},{4,0},{8,12},{12,8},{16,20},{20,16},{24,28},{28,24},{1,5},{5... | collective-permute-start | bytes 3145736 | tf_op jit(solution)/shard_map/ppermute | solution.py:891
  187.4 5.5 %convert_add_fusion = bf16[512,1024]{1,0:T(8,128)(2,1)} fusion(bf16[512,1024]{1,0:T(8,128)(2,1)S(1)} %bitcast.122, bf16[512,2048]{1,0:T(8,128)(2,1)S(1)} %copy-done.32, bf16[2048,1024]{1,0:T(8,128)(2,1)} %ow_ref.1), kind=kOutput, calls=%fused_computation.4 | convolution fusion | flops 2149056512 | bytes 8388608 | tf_op jit(solution)/shard_map/dot_general | solution.py:1013
  192.9 1.2 add_convert_fusion.3
  194.1 4.3 %collective-permute-start.2 = (bf16[4,128,256]{2,1,0:T(8,128)(2,1)}, bf16[4,128,256]{2,1,0:T(8,128)(2,1)S(1)}, u32[]{:S(2)}, u32[]{:S(2)}) collective-permute-start(bf16[4,128,256]{2,1,0:T(8,128)(2,1)} %get-tuple-element.168), channel_id=1, source_target_pairs={{0,16},{4,20},{8,24},{12,28},{16,0},{20,4},{24,8},{28,12},{1,17},{... | collective-permute-start | bytes 786440 | tf_op jit(solution)/shard_map/ppermute | solution.py:885
  198.9 1.0 collective-permute-start.4
  199.9 11.6 %input_grads.3 = (bf16[16,192,256]{2,1,0:T(8,128)(2,1)}, bf16[16,192,256]{2,1,0:T(8,128)(2,1)}, bf16[512,1024]{1,0:T(8,128)(2,1)}, f32[16,1024]{1,0:T(8,128)}, f32[16,1024]{1,0:T(8,128)}) custom-call(s32[33]{0:T(128)} %pad_add_fusion.place_ref, f32[512,2048]{1,0:T(8,128)} %get-tuple-element.164.cp_ref, bf16[512,2048]{1,0:T(8,128)(2,1)} %get-tuple-element.149.inner_ref, ...), custom_call_target="tpu_custom_call" | custom-call | flops 12884901888 | bytes 16777216 | tf_op jit(solution)/shard_map/input_grads/pallas_call | solution.py:718
  211.5 1.0 pad_maximum_fusion
  212.5 2.6 collective-permute-done.4
  215.4 1.5 collective-permute-start.9
  217.6 1.0 collective-permute-done.9
  218.8 1.9 add_convert_fusion
  220.8 2.3 collective-permute-start.6
  223.7 1.0 collective-permute-start.8
  224.7 4.6 %fusion = f32[512,1024]{1,0:T(8,128)S(1)} fusion(bf16[512,2048]{1,0:T(8,128)(2,1)S(1)} %copy-done.31, bf16[1024,4096]{1,0:T(8,128)(2,1)} %refs_9_.1), kind=kOutput, calls=%fused_computation | convolution fusion | flops 2147483648 | bytes 8388608 | tf_op jit(solution)/shard_map/dot_general | solution.py:44
  230.1 2.5 collective-permute-start.10
  232.6 1.5 collective-permute-start.11
  234.1 1.6 collective-permute-start.12
  235.7 6.6 %collective-permute-done.8 = bf16[4,192,256]{2,1,0:T(8,128)(2,1)S(1)} collective-permute-done((bf16[4,192,256]{2,1,0:T(8,128)(2,1)S(1)}, bf16[4,192,256]{2,1,0:T(8,128)(2,1)S(1)}, u32[]{:S(2)}, u32[]{:S(2)}) %collective-permute-start.8) | collective-permute-done | bytes 393248 | tf_op jit(solution)/shard_map/ppermute | solution.py:885
  242.3 0.9 add_convert_fusion.7
  243.1 2.4 collective-permute-start.13
  245.5 1.5 collective-permute-start.14
  247.7 1.4 scatter.6
  249.1 1.4 scatter.9
  250.5 3.3 %fusion.8 = f32[512,1024]{1,0:T(8,128)S(1)} fusion(bf16[512,1024]{1,0:T(8,128)(2,1)} %bitcast.162, bf16[1024,4096]{1,0:T(8,128)(2,1)} %refs_9_.1), kind=kOutput, calls=%fused_computation.12 | convolution fusion | flops 1073741824 | bytes 5242880 | tf_op jit(solution)/shard_map/dot_general | solution.py:44
  253.8 2.9 %fusion.6 = f32[512,1024]{1,0:T(8,128)S(1)} fusion(bf16[512,1024]{1,0:T(8,128)(2,1)S(1)} %bitcast.164, bf16[1024,4096]{1,0:T(8,128)(2,1)} %refs_9_.1), kind=kOutput, calls=%fused_computation.10 | convolution fusion | flops 1073741824 | bytes 5242880 | tf_op jit(solution)/shard_map/dot_general | solution.py:44
  258.0 1.6 fusion.4
  259.6 4.8 %collective-permute-done.15.refs_7_ = bf16[1,192,256]{2,1,0:T(8,128)(2,1)S(1)} collective-permute-done((bf16[1,192,256]{2,1,0:T(8,128)(2,1)S(1)}, bf16[1,192,256]{2,1,0:T(8,128)(2,1)S(1)}, u32[]{:S(2)}, u32[]{:S(2)}) %collective-permute-start.15) | collective-permute-done | bytes 98336 | tf_op jit(solution)/shard_map/ppermute | solution.py:885
  265.1 2.4 shares.1
  (129 shorter events, 9.3 us)
Async XLA Ops:
  7.2 74.2 %all-gather.5.cloned.1.call-start = ((), (), s32[]{:S(2)}) async-start(), calls=%async_computation.4 | async-start | bytes 1769472 | tf_op jit(solution)/shard_map/all_gather | solution.py:911
  8.0 3.3 %collective-permute-start = (bf16[2,8,1024]{2,1,0:T(8,128)(2,1)S(1)}, bf16[2,8,1024]{2,1,0:T(8,128)(2,1)S(1)}, u32[]{:S(2)}, u32[]{:S(2)}) collective-permute-start(bf16[2,8,1024]{2,1,0:T(8,128)(2,1)S(1)} %slice.404), channel_id=1, source_target_pairs={{0,4},{4,8},{8,12},{12,16},{16,20},{20,24},{24,28},{1,5},{5,9},{9,... | collective-permute-start | bytes 98312 | tf_op jit(solution)/shard_map/ppermute | solution.py:954
  28.2 19.3 %copy-start.1 = (f32[512,128]{1,0:T(8,128)S(1)}, f32[512,128]{1,0:T(8,128)}, u32[]{:S(2)}) copy-start(f32[512,128]{1,0:T(8,128)} %get-tuple-element.127.proj_ref) | copy-start | bytes 786436
  28.2 19.3 %copy-start.4 = (bf16[512,1024]{1,0:T(8,128)(2,1)S(1)}, bf16[512,1024]{1,0:T(8,128)(2,1)}, u32[]{:S(2)}) copy-start(bf16[512,1024]{1,0:T(8,128)(2,1)} %constant.182.clone) | copy-start | bytes 3145732
  28.2 19.3 %copy-start.23 = (bf16[16,1024]{1,0:T(8,128)(2,1)S(1)}, bf16[16,1024]{1,0:T(8,128)(2,1)}, u32[]{:S(2)}) copy-start(bf16[16,1024]{1,0:T(8,128)(2,1)} %constant.181.clone) | copy-start | bytes 98308
  47.4 80.7 %all-gather.7.cloned.1.call-start = ((), (), s32[]{:S(2)}) async-start(), calls=%async_computation.5 | async-start | bytes 1179648 | tf_op jit(solution)/shard_map/all_gather | solution.py:911
  64.3 15.9 %copy-start.8 = (bf16[512,512]{1,0:T(8,128)(2,1)S(1)}, bf16[512,512]{1,0:T(8,128)(2,1)}, u32[]{:S(2)}) copy-start(bf16[512,512]{1,0:T(8,128)(2,1)} %constant.180.clone) | copy-start | bytes 1572868
  64.3 15.9 %copy-start.28 = (bf16[16,512]{1,0:T(8,128)(2,1)S(1)}, bf16[16,512]{1,0:T(8,128)(2,1)}, u32[]{:S(2)}) copy-start(bf16[16,512]{1,0:T(8,128)(2,1)} %constant.179.clone) | copy-start | bytes 49156
  81.3 133.8 %reduce-scatter.3.cloned.1.call-start = ((), (), s32[]{:S(2)}) async-start(), calls=%async_computation.2 | async-start | bytes 9437184 | tf_op jit(solution)/shard_map/reduce_scatter | solution.py:982
  128.1 1.2 copy-start.7
  128.1 136.3 %reduce-scatter.5.cloned.1.call-start = ((), (), s32[]{:S(2)}) async-start(), calls=%async_computation.3 | async-start | bytes 1310720 | tf_op jit(solution)/shard_map/reduce_scatter | solution.py:1027
  130.5 37.8 %copy-start.9 = (bf16[64,2048]{1,0:T(8,128)(2,1)S(1)}, bf16[64,2048]{1,0:T(8,128)(2,1)}, u32[]{:S(2)}) copy-start(bf16[64,2048]{1,0:T(8,128)(2,1)} %rw_ref.1) | copy-start | bytes 786436
  168.3 2.6 copy-start.25
  168.3 2.7 copy-start.14
  172.4 15.0 %copy-start = (bf16[2,256,1024]{2,1,0:T(8,128)(2,1)S(1)}, bf16[2,256,1024]{2,1,0:T(8,128)(2,1)}, u32[]{:S(2)}) copy-start(bf16[2,256,1024]{2,1,0:T(8,128)(2,1)} %param.21) | copy-start | bytes 3145732
  172.4 15.0 %copy-start.32 = (bf16[512,2048]{1,0:T(8,128)(2,1)S(1)}, bf16[512,2048]{1,0:T(8,128)(2,1)}, u32[]{:S(2)}) copy-start(bf16[512,2048]{1,0:T(8,128)(2,1)} %get-tuple-element.162.gated_ref) | copy-start | bytes 6291460
  184.0 8.9 %copy-start.5 = (bf16[16,128,256]{2,1,0:T(8,128)(2,1)S(1)}, bf16[16,128,256]{2,1,0:T(8,128)(2,1)}, u32[]{:S(2)}) copy-start(bf16[16,128,256]{2,1,0:T(8,128)(2,1)} %get-tuple-element.159) | copy-start | bytes 3145732
  184.0 8.9 %collective-permute-start.1 = (bf16[16,128,256]{2,1,0:T(8,128)(2,1)}, bf16[16,128,256]{2,1,0:T(8,128)(2,1)S(1)}, u32[]{:S(2)}, u32[]{:S(2)}) collective-permute-start(bf16[16,128,256]{2,1,0:T(8,128)(2,1)} %get-tuple-element.161), channel_id=1, source_target_pairs={{0,4},{4,0},{8,12},{12,8},{16,20},{20,16},{24,28},{28,24},{1,5},{5... | collective-permute-start | bytes 3145736 | tf_op jit(solution)/shard_map/ppermute | solution.py:891
  194.1 18.4 %collective-permute-start.2 = (bf16[4,128,256]{2,1,0:T(8,128)(2,1)}, bf16[4,128,256]{2,1,0:T(8,128)(2,1)S(1)}, u32[]{:S(2)}, u32[]{:S(2)}) collective-permute-start(bf16[4,128,256]{2,1,0:T(8,128)(2,1)} %get-tuple-element.168), channel_id=1, source_target_pairs={{0,16},{4,20},{8,24},{12,28},{16,0},{20,4},{24,8},{28,12},{1,17},{... | collective-permute-start | bytes 786440 | tf_op jit(solution)/shard_map/ppermute | solution.py:885
  198.5 14.0 %collective-permute-start.3 = (bf16[4,128,256]{2,1,0:T(8,128)(2,1)S(1)}, bf16[4,128,256]{2,1,0:T(8,128)(2,1)S(1)}, u32[]{:S(2)}, u32[]{:S(2)}) collective-permute-start(bf16[4,128,256]{2,1,0:T(8,128)(2,1)S(1)} %get-tuple-element.169), channel_id=1, source_target_pairs={{0,8},{4,12},{8,0},{12,4},{16,24},{20,28},{24,16},{28,20},{1,9},{5... | collective-permute-start | bytes 786440 | tf_op jit(solution)/shard_map/ppermute | solution.py:885
  198.9 16.2 %collective-permute-start.4 = (bf16[4,128,256]{2,1,0:T(8,128)(2,1)S(1)}, bf16[4,128,256]{2,1,0:T(8,128)(2,1)S(1)}, u32[]{:S(2)}, u32[]{:S(2)}) collective-permute-start(bf16[4,128,256]{2,1,0:T(8,128)(2,1)S(1)} %get-tuple-element.170), channel_id=1, source_target_pairs={{0,24},{4,28},{8,16},{12,20},{16,8},{20,12},{24,0},{28,4},{1,25},{... | collective-permute-start | bytes 786440 | tf_op jit(solution)/shard_map/ppermute | solution.py:885
  199.9 11.6 %copy-start.18 = (f32[16,1024]{1,0:T(8,128)S(1)}, f32[16,1024]{1,0:T(8,128)}, u32[]{:S(2)}) copy-start(f32[16,1024]{1,0:T(8,128)} %get-tuple-element.172) | copy-start | bytes 196612
  211.5 7.4 %copy-start.3 = (bf16[16,192,256]{2,1,0:T(8,128)(2,1)S(1)}, bf16[16,192,256]{2,1,0:T(8,128)(2,1)}, u32[]{:S(2)}) copy-start(bf16[16,192,256]{2,1,0:T(8,128)(2,1)} %get-tuple-element.166) | copy-start | bytes 4718596
  212.5 8.3 %copy-start.10 = (bf16[4,128,256]{2,1,0:T(8,128)(2,1)}, bf16[4,128,256]{2,1,0:T(8,128)(2,1)S(1)}, u32[]{:S(2)}) copy-start(bf16[4,128,256]{2,1,0:T(8,128)(2,1)S(1)} %collective-permute-done.3) | copy-start | bytes 786436
  215.1 5.7 %copy-start.12 = (bf16[4,128,256]{2,1,0:T(8,128)(2,1)}, bf16[4,128,256]{2,1,0:T(8,128)(2,1)S(1)}, u32[]{:S(2)}) copy-start(bf16[4,128,256]{2,1,0:T(8,128)(2,1)S(1)} %collective-permute-done.4) | copy-start | bytes 786436
  215.1 3.8 %collective-permute-start.5 = (bf16[16,192,256]{2,1,0:T(8,128)(2,1)}, bf16[16,192,256]{2,1,0:T(8,128)(2,1)}, u32[]{:S(2)}, u32[]{:S(2)}) collective-permute-start(bf16[16,192,256]{2,1,0:T(8,128)(2,1)} %get-tuple-element.175), channel_id=1, source_target_pairs={{0,4},{4,0},{8,12},{12,8},{16,20},{20,16},{24,28},{28,24},{1,5},{5... | collective-permute-start | bytes 4718600 | tf_op jit(solution)/shard_map/ppermute | solution.py:891
  215.4 1.6 copy-start.26
  215.4 3.1 %collective-permute-start.9 = (bf16[2,3,2048]{2,1,0:T(4,128)(2,1)S(1)}, bf16[2,3,2048]{2,1,0:T(4,128)(2,1)S(1)}, u32[]{:S(2)}, u32[]{:S(2)}) collective-permute-start(bf16[2,3,2048]{2,1,0:T(4,128)(2,1)S(1)} %slice.559), channel_id=1, source_target_pairs={{4,0},{8,4},{12,8},{16,12},{20,16},{24,20},{28,24},{5,1},{9,5},{13... | collective-permute-start | bytes 73736 | tf_op jit(solution)/shard_map/ppermute | solution.py:1019
  218.8 5.8 %copy-start.31 = (bf16[512,2048]{1,0:T(8,128)(2,1)S(1)}, bf16[512,2048]{1,0:T(8,128)(2,1)}, u32[]{:S(2)}) copy-start(bf16[512,2048]{1,0:T(8,128)(2,1)} %get-tuple-element.190.gate_ref) | copy-start | bytes 6291460
  220.8 8.5 %copy-start.2 = (f32[4,128,256]{2,1,0:T(8,128)S(1)}, f32[4,128,256]{2,1,0:T(8,128)}, u32[]{:S(2)}) copy-start(f32[4,128,256]{2,1,0:T(8,128)} %get-tuple-element.199) | copy-start | bytes 1572868
  220.8 8.5 %copy-start.11 = (bf16[4,128,256]{2,1,0:T(8,128)(2,1)S(1)}, bf16[4,128,256]{2,1,0:T(8,128)(2,1)}, u32[]{:S(2)}) copy-start(bf16[4,128,256]{2,1,0:T(8,128)(2,1)} %copy-done.10) | copy-start | bytes 786436
  220.8 8.5 %copy-start.13 = (bf16[4,128,256]{2,1,0:T(8,128)(2,1)S(1)}, bf16[4,128,256]{2,1,0:T(8,128)(2,1)}, u32[]{:S(2)}) copy-start(bf16[4,128,256]{2,1,0:T(8,128)(2,1)} %copy-done.12) | copy-start | bytes 786436
  220.8 13.3 %collective-permute-start.6 = (bf16[4,192,256]{2,1,0:T(8,128)(2,1)S(1)}, bf16[4,192,256]{2,1,0:T(8,128)(2,1)S(1)}, u32[]{:S(2)}, u32[]{:S(2)}) collective-permute-start(bf16[4,192,256]{2,1,0:T(8,128)(2,1)S(1)} %get-tuple-element.181), channel_id=1, source_target_pairs={{0,16},{4,20},{8,24},{12,28},{16,0},{20,4},{24,8},{28,12},{1,17},{... | collective-permute-start | bytes 1179656 | tf_op jit(solution)/shard_map/ppermute | solution.py:885
  223.1 12.5 %collective-permute-start.7 = (bf16[4,192,256]{2,1,0:T(8,128)(2,1)S(1)}, bf16[4,192,256]{2,1,0:T(8,128)(2,1)S(1)}, u32[]{:S(2)}, u32[]{:S(2)}) collective-permute-start(bf16[4,192,256]{2,1,0:T(8,128)(2,1)S(1)} %get-tuple-element.182), channel_id=1, source_target_pairs={{0,8},{4,12},{8,0},{12,4},{16,24},{20,28},{24,16},{28,20},{1,9},{5... | collective-permute-start | bytes 1179656 | tf_op jit(solution)/shard_map/ppermute | solution.py:885
  223.7 18.6 %collective-permute-start.8 = (bf16[4,192,256]{2,1,0:T(8,128)(2,1)S(1)}, bf16[4,192,256]{2,1,0:T(8,128)(2,1)S(1)}, u32[]{:S(2)}, u32[]{:S(2)}) collective-permute-start(bf16[4,192,256]{2,1,0:T(8,128)(2,1)S(1)} %get-tuple-element.183), channel_id=1, source_target_pairs={{0,24},{4,28},{8,16},{12,20},{16,8},{20,12},{24,0},{28,4},{1,25},{... | collective-permute-start | bytes 1179656 | tf_op jit(solution)/shard_map/ppermute | solution.py:885
  229.3 17.7 %copy-start.19 = (f32[16,1024]{1,0:T(8,128)S(1)}, f32[16,1024]{1,0:T(8,128)}, u32[]{:S(2)}) copy-start(f32[16,1024]{1,0:T(8,128)} %get-tuple-element.195) | copy-start | bytes 196612
  229.3 17.7 %copy-start.20 = (f32[16,1024]{1,0:T(8,128)S(1)}, f32[16,1024]{1,0:T(8,128)}, u32[]{:S(2)}) copy-start(f32[16,1024]{1,0:T(8,128)} %get-tuple-element.196) | copy-start | bytes 196612
  230.1 27.3 %collective-permute-start.10 = (bf16[1,128,256]{2,1,0:T(8,128)(2,1)}, bf16[1,128,256]{2,1,0:T(8,128)(2,1)}, u32[]{:S(2)}, u32[]{:S(2)}) collective-permute-start(bf16[1,128,256]{2,1,0:T(8,128)(2,1)} %get-tuple-element.242), channel_id=1, source_target_pairs={{0,2},{1,3},{2,0},{3,1},{4,6},{5,7},{6,4},{7,5},{8,10},{9,11},{10,... | collective-permute-start | bytes 196616 | tf_op jit(solution)/shard_map/ppermute | solution.py:885
  232.6 27.0 %collective-permute-start.11 = (bf16[1,128,256]{2,1,0:T(8,128)(2,1)}, bf16[1,128,256]{2,1,0:T(8,128)(2,1)}, u32[]{:S(2)}, u32[]{:S(2)}) collective-permute-start(bf16[1,128,256]{2,1,0:T(8,128)(2,1)} %get-tuple-element.241), channel_id=1, source_target_pairs={{0,1},{1,0},{2,3},{3,2},{4,5},{5,4},{6,7},{7,6},{8,9},{9,8},{10,11... | collective-permute-start | bytes 196616 | tf_op jit(solution)/shard_map/ppermute | solution.py:885
  234.1 25.5 %collective-permute-start.12 = (bf16[1,128,256]{2,1,0:T(8,128)(2,1)}, bf16[1,128,256]{2,1,0:T(8,128)(2,1)}, u32[]{:S(2)}, u32[]{:S(2)}) collective-permute-start(bf16[1,128,256]{2,1,0:T(8,128)(2,1)} %get-tuple-element.240), channel_id=1, source_target_pairs={{0,3},{1,2},{2,1},{3,0},{4,7},{5,6},{6,5},{7,4},{8,11},{9,10},{10,... | collective-permute-start | bytes 196616 | tf_op jit(solution)/shard_map/ppermute | solution.py:885
  243.1 16.4 %collective-permute-start.13 = (bf16[1,192,256]{2,1,0:T(8,128)(2,1)}, bf16[1,192,256]{2,1,0:T(8,128)(2,1)S(1)}, u32[]{:S(2)}, u32[]{:S(2)}) collective-permute-start(bf16[1,192,256]{2,1,0:T(8,128)(2,1)} %get-tuple-element.204), channel_id=1, source_target_pairs={{0,2},{1,3},{2,0},{3,1},{4,6},{5,7},{6,4},{7,5},{8,10},{9,11},{10,... | collective-permute-start | bytes 294920 | tf_op jit(solution)/shard_map/ppermute | solution.py:885
  245.5 14.0 %collective-permute-start.14 = (bf16[1,192,256]{2,1,0:T(8,128)(2,1)S(1)}, bf16[1,192,256]{2,1,0:T(8,128)(2,1)S(1)}, u32[]{:S(2)}, u32[]{:S(2)}) collective-permute-start(bf16[1,192,256]{2,1,0:T(8,128)(2,1)S(1)} %get-tuple-element.205), channel_id=1, source_target_pairs={{0,1},{1,0},{2,3},{3,2},{4,5},{5,4},{6,7},{7,6},{8,9},{9,8},{10,11... | collective-permute-start | bytes 294920 | tf_op jit(solution)/shard_map/ppermute | solution.py:885
  250.5 3.3 %copy-start.30 = (bf16[2,256,1024]{2,1,0:T(8,128)(2,1)S(1)}, bf16[2,256,1024]{2,1,0:T(8,128)(2,1)}, u32[]{:S(2)}) copy-start(bf16[2,256,1024]{2,1,0:T(8,128)(2,1)} %scatter.9) | copy-start | bytes 3145732
  253.8 2.9 %copy-start.21 = (f32[1024]{0:T(1024)S(1)}, f32[1024]{0:T(1024)}, u32[]{:S(2)}) copy-start(f32[1024]{0:T(1024)} %param.23) | copy-start | bytes 12292
  256.7 1.2 copy-start.6
  257.4 7.1 %collective-permute-start.15 = (bf16[1,192,256]{2,1,0:T(8,128)(2,1)S(1)}, bf16[1,192,256]{2,1,0:T(8,128)(2,1)S(1)}, u32[]{:S(2)}, u32[]{:S(2)}) collective-permute-start(bf16[1,192,256]{2,1,0:T(8,128)(2,1)S(1)} %get-tuple-element.206), channel_id=1, source_target_pairs={{0,3},{1,2},{2,1},{3,0},{4,7},{5,6},{6,5},{7,4},{8,11},{9,10},{10,... | collective-permute-start | bytes 294920 | tf_op jit(solution)/shard_map/ppermute | solution.py:885
  259.6 4.9 %copy-start.15 = (bf16[1,192,256]{2,1,0:T(8,128)(2,1)}, bf16[1,192,256]{2,1,0:T(8,128)(2,1)S(1)}, u32[]{:S(2)}) copy-start(bf16[1,192,256]{2,1,0:T(8,128)(2,1)S(1)} %collective-permute-done.13.refs_5_) | copy-start | bytes 294916
  259.6 4.9 %copy-start.16 = (bf16[1,192,256]{2,1,0:T(8,128)(2,1)}, bf16[1,192,256]{2,1,0:T(8,128)(2,1)S(1)}, u32[]{:S(2)}) copy-start(bf16[1,192,256]{2,1,0:T(8,128)(2,1)S(1)} %collective-permute-done.14.refs_6_) | copy-start | bytes 294916
  (5 other events, 4.6 us)
Sparse Core Ops, SparseCore 0:
  47.5 30.2 all-gather.4
  81.4 28.3 all-gather.6
  128.2 79.3 reduce-scatter.2
  217.7 33.3 reduce-scatter.4

commit v4 on v3

--- a/solution.py
+++ b/solution.py
@@ -34,10 +34,6 @@
 
 def steps_of(rows):
     return pl.ds(pl.multiple_of(rows, T), T)
-
-
-def state_of(t):
-    return pl.ds(pl.multiple_of(t * N, N), N)
 
 
 def rows_dot(left, right):
@@ -118,9 +114,25 @@
             sb_ref[s * N : (s + 1) * N, lane(l)] = lam[s][l].astype(bf16)
 
 
+def state_copy(states_ref, held_ref, sems, at, q, s, length, unroll, out):
+    size = unroll * T * N
+    rows = pl.ds(pl.multiple_of(s * length * N + q * size, size), size)
+    far = states_ref.at[rows, pl.ds(pl.multiple_of(at * WIDTH, WIDTH), WIDTH)]
+    near = held_ref.at[s, q]
+    return pltpu.make_async_copy(near, far, sems.at[s, q]) if out else pltpu.make_async_copy(far, near, sems.at[s, q])
+
+
+def state_scratch(nseq, length, unroll):
+    groups = length // (T * unroll)
+    return [
+        pltpu.VMEM((N, WIDTH), f32), pltpu.VMEM((nseq, groups, unroll * T * N, WIDTH), bf16),
+        pltpu.SemaphoreType.DMA((nseq, groups)),
+    ]
+
+
 def forward_kernel(
     dl_ref, u_ref, g_ref, ga_ref, gs_ref, x_ref, skip_ref, bb_ref, bc_ref, lc_ref, log_ref, hin_ref,
-    hb_ref, gated_ref, ggr_ref, outg_ref, gu_ref, sk_ref, a2_ref, *, nseq, length, unroll,
+    hb_ref, gated_ref, ggr_ref, outg_ref, gu_ref, sk_ref, a2_ref, held_ref, sems, *, nseq, length, unroll,
 ):
     a2_ref[...] = rates_of(log_ref) * LOG2E
     nch = length // T
@@ -132,7 +144,12 @@
         outg_ref[...] = jnp.zeros_like(outg_ref)
         gu_ref[...] = jnp.zeros_like(gu_ref)
 
-    def chunk(c, h, acc):
+    step_at, last_step = pl.program_id(0), pl.num_programs(0) - 1
+
+    def leaving(at, q, s):
+        return state_copy(hb_ref, held_ref, sems, at, q, s, length, unroll, True)
+
+    def chunk(c, p, q, h, acc):
         hbv, pov = {}, [[None] * T for _ in range(nseq)]
         for k in range(T):
             for s in range(nseq):
@@ -145,7 +162,7 @@
                     held = f * h[s][l]
                     h[s][l] = held + u_ref[l, pl.ds(t, 1), :] * bt
                     hb = held.astype(bf16)
-                    hb_ref[state_of(t), lane(l)] = hb
+                    held_ref[s, q, (p * T + k) * N : (p * T + k + 1) * N, lane(l)] = hb
                     hbv[k, s, l] = hb
                     po = hb * g if po is None else po + hb * g
                 pov[s][k] = po
@@ -180,18 +197,31 @@
     def step(i, carry):
         h, acc = carry
         h = [list(v) for v in h]
+        @pl.when(step_at > 0)
+        def _():
+            for s in range(nseq):
+                leaving(step_at - 1, i, s).wait()
+
         for p in range(unroll):
-            acc = chunk(i * unroll + p, h, acc)
+            acc = chunk(i * unroll + p, p, i, h, acc)
+        for s in range(nseq):
+            leaving(step_at, i, s).start()
         return tuple(tuple(v) for v in h), acc
 
     h0 = tuple(tuple(hin_ref[s, :, lane(l)] for l in range(NL)) for s in range(nseq))
     _, acc = lax.fori_loop(0, nch // unroll, step, (h0, jnp.zeros((T, WIDTH), f32)))
     sk_ref[...] = jnp.broadcast_to(jnp.sum(acc, axis=0, keepdims=True), sk_ref.shape)
 
+    @pl.when(step_at == last_step)
+    def _():
+        for q in range(nch // unroll):
+            for s in range(nseq):
+                leaving(step_at, q, s).wait()
+
 
 def backward_kernel(
     dl_ref, u_ref, g_ref, x_ref, skip_ref, cb_ref, lb_ref, ls_ref, log_ref, lin_ref, hb_ref,
-    rl_ref, cp_ref, ing_ref, dlog_ref, rb_ref, a2_ref, *, nseq, length, unroll,
+    rl_ref, cp_ref, ing_ref, dlog_ref, rb_ref, a2_ref, held_ref, sems, *, nseq, length, unroll,
 ):
     a2_ref[...] = rates_of(log_ref) * LOG2E
     nch = length // T
@@ -203,7 +233,19 @@
     def _():
         ing_ref[...] = jnp.zeros_like(ing_ref)
 
-    def chunk(c, lam, dlog, rb):
+    step_at, last_step = pl.program_id(0), pl.num_programs(0) - 1
+    groups = nch // unroll
+
+    def arriving(at, q, s):
+        return state_copy(hb_ref, held_ref, sems, at, q, s, length, unroll, False)
+
+    @pl.when(step_at == 0)
+    def _():
+        for q in reversed(range(groups)):
+            for s in range(nseq):
+                arriving(0, q, s).start()
+
+    def chunk(c, p, group, lam, dlog, rb):
         pov = [[None] * T for _ in range(nseq)]
         dacc = [None] * NL
         vals = {}
@@ -218,7 +260,7 @@
                     a = g_ref[l, pl.ds(t, 1), :] * ct + lam[s][l]
                     lam[s][l] = jnp.exp2(d * a2_ref[:, lane(l)]) * a
                     ab = a.astype(bf16)
-                    q = ab * hb_ref[state_of(t), lane(l)] * abf[:, lane(l)]
+                    q = ab * held_ref[s, group, (p * T + k) * N : (p * T + k + 1) * N, lane(l)] * abf[:, lane(l)]
                     qd = q * d.astype(bf16)
                     vals[k, s, l] = (ab, q)
                     dacc[l] = qd if dacc[l] is None else dacc[l] + qd
@@ -259,8 +301,17 @@
         lam, dlog, rb = carry
         lam = [list(v) for v in lam]
         dlog = list(dlog)
-        for p in range(unroll):
-            rb = chunk(nch - 1 - (m * unroll + p), lam, dlog, rb)
+        q = groups - 1 - m
+        for s in range(nseq):
+            arriving(step_at, q, s).wait()
+        for p in reversed(range(unroll)):
+            rb = chunk(q * unroll + p, p, q, lam, dlog, rb)
+
+        @pl.when(step_at < last_step)
+        def _():
+            for s in range(nseq):
+                arriving(step_at + 1, q, s).start()
+
         return tuple(tuple(v) for v in lam), tuple(dlog), rb
 
     l0 = tuple(tuple(lin_ref[s, :, lane(l)] for l in range(NL)) for s in range(nseq))
@@ -364,14 +415,14 @@
         (dl, u, g, ga, gs, x, skip, bb, bc, lc, log, hin),
         [t, t, t, t, t, t, block_of(1), whole(bb), whole(bc), whole(lc), block_of(N), states_of(nseq)],
         [
-            block_of(rows * N), block_of(rows), block_of(rows), pl.BlockSpec((rows // T, T * N), lambda j: (0, 0)),
+            pl.BlockSpec(memory_space=pl.ANY), block_of(rows), block_of(rows), pl.BlockSpec((rows // T, T * N), lambda j: (0, 0)),
             pl.BlockSpec((rows, 128), lambda j: (0, 0)), block_of(8),
         ],
         (
             o((rows * N, ch), bf16), o((rows, ch), bf16), o((rows, ch), bf16), o((rows // T, T * N), f32),
             o((rows, 128), f32), o((8, ch), f32),
         ),
-        3 * 10**10, nseq=nseq, length=length, unroll=unroll, scratch=[pltpu.VMEM((N, WIDTH), f32)],
+        3 * 10**10, nseq=nseq, length=length, unroll=unroll, scratch=state_scratch(nseq, length, unroll),
     )
 
 
@@ -384,10 +435,10 @@
     return kernel_call(
         backward_kernel, "backward", ch,
         (dl, u, g, x, skip, cb, lb, ls, log, lin, hb),
-        [t, t, t, t, block_of(1), whole(cb), whole(lb), whole(ls), block_of(N), st, block_of(rows * N)],
+        [t, t, t, t, block_of(1), whole(cb), whole(lb), whole(ls), block_of(N), st, pl.BlockSpec(memory_space=pl.ANY)],
         [block_of(rows), block_of(rows), pl.BlockSpec((rows // T, T * N), lambda j: (0, 0)), block_of(N), block_of(8)],
         (o((rows, ch), bf16), o((rows, ch), f32), o((rows // T, T * N), f32), o((N, ch), f32), o((8, ch), f32)),
-        5 * 10**10, nseq=nseq, length=length, unroll=unroll, scratch=[pltpu.VMEM((N, WIDTH), f32)],
+        5 * 10**10, nseq=nseq, length=length, unroll=unroll, scratch=state_scratch(nseq, length, unroll),
     )
 
 

time: 275 us -> 273 us (level)
  Pallas kernels: 167 us -> 162 us
  waiting for transfers between devices: 15.4 us -> 19.6 us
    pallas_call x5, Pallas kernels: 119 us -> 114 us  [kernel_call(): pl.pallas_call(functools.partial(body, **options), grid=(channels // WIDT...]
    ppermute x12, waiting for transfers between devices: 14 us -> 18.2 us  [round_trade(): held.append(lax.ppermute(parts[i], bits[0][0], flip_bit(bits[0][0], flip)))]
  transfers between devices with their start and end apart: 20 -> 20, of which waited for: 5 -> 6; matrix products, arithmetic and copies ran while one was open for 16% -> 16% of each run, Pallas kernels for 49% -> 47%
where the time goes in v4:
time: 273 us; the launch traced here: 272 us
  Pallas kernels  162 us (59%)
  starting transfers between devices  25.9 us (9%)
  matrix products  21.2 us (8%)
  waiting for transfers between devices  19.6 us (7%)
  other arithmetic  14.9 us (5%)
  between operations  14.5 us (5%)
  local copies, waits for them, and re-layouts  13.8 us (5%)
    pallas_call x5, Pallas kernels, kernel_call(): pl.pallas_call(functools.partial(body, **options), grid=(channels // WIDT...  114 us
    pallas_call x2, Pallas kernels, input_grads(): pl.pallas_call(functools.partial(input_grad_kernel, nseq=nseq, length=len...  23.3 us
    ppermute x12, starting transfers between devices, round_trade(): held.append(lax.ppermute(parts[i], bits[0][0], flip_bit(bits[0][0], flip)))  19 us
    ppermute x12, waiting for transfers between devices, round_trade(): held.append(lax.ppermute(parts[i], bits[0][0], flip_bit(bits[0][0], flip)))  18.2 us
    dot_general x4, matrix products, rows_dot(): lax.dot_general(left, right, (((1,), (1,)), ((), ())), preferred_element_...  13.1 us
    pallas_call x1, Pallas kernels, inner_side(): pl.pallas_call(functools.partial(inner_kernel, nseq=nseq, length=length,...  12.4 us
    pallas_call x1, Pallas kernels, weight_grads(): pl.pallas_call(functools.partial(weight_grad_kernel, part=part), grid=(wi...  10.4 us
    dot_general x1, matrix products, shards(): jnp.dot(gated, out_weight, preferred_element_type=f32)  5.51 us
  transfers between devices with their start and end apart: 20, of which 6 were waited for; matrix products, arithmetic and copies ran while one was open for 16% of the time, Pallas kernels for 47%

profile of v4, /device:TPU:0, one launch (start us, length us, event | category | flops | bytes accessed | tf_op | source)
XLA Modules:
  0.0 271.8 jit_solution(13414474582604778525)
XLA Ops:
  8.0 2.3 collective-permute-start
  10.3 0.9 exponential_negate_fusion
  11.9 12.4 %inner_side.1 = (bf16[512,1024]{1,0:T(8,128)(2,1)}, bf16[512,2048]{1,0:T(8,128)(2,1)}, bf16[16,2048]{1,0:T(8,128)(2,1)}, bf16[16,512,128]{2,1,0:T(8,128)(2,1)}, ...) custom-call(bf16[512,1024]{1,0:T(8,128)(2,1)} %bitcast.121, bf16[16,1024]{1,0:T(8,128)(2,1)} %bitcast.155, ...), custom_call_target="tpu_custom_call" | custom-call | flops 2147483648 | bytes 14680064 | tf_op jit(solution)/shard_map/inner_side/pallas_call | solution.py:574
  24.3 1.2 fusion.51
  25.6 2.6 broadcast_in_dim.24.bb_ref
  28.2 19.2 %state_end.1 = (bf16[48,2048]{1,0:T(8,128)(2,1)}, f32[16,512,128]{2,1,0:T(8,128)}, f32[16,512,128]{2,1,0:T(8,128)}) custom-call(f32[512,128]{1,0:T(8,128)} %get-tuple-element.127.proj_ref, bf16[64,2048]{1,0:T(8,128)(2,1)} %rw_ref.1, f32[1,2048]{1,0:T(1,128)} %bitcast.165, bf16[16,512,128]{2,1,0:T(8,128)(2,1)} %get-tuple-element.128.x_ref, ...), custom_call_target="tpu_custom_call" | custom-call | flops 20000000000 | bytes 15540224 | tf_op jit(solution)/shard_map/state_end/pallas_call | solution.py:345
  47.5 1.4 fusion.10.lb_ref
  48.9 12.8 %gate_side.1 = (bf16[1024,512]{1,0:T(8,128)(2,1)}, f32[16,512,128]{2,1,0:T(8,128)}, f32[16,512,128]{2,1,0:T(8,128)}, f32[16,512,128]{2,1,0:T(8,128)}) custom-call(bf16[512,1024]{1,0:T(8,128)(2,1)} %get-tuple-element.130.normed_ref, bf16[512,1024]{1,0:T(8,128)(2,1)} %bitcast.123, bf16[1024,4096]{1,0:T(8,128)(2,1)} %refs_9_.1, bf16[2048,1024]{1,0:T(8,128)(2,1)} %ow_ref.1), custom_call_target="tpu_custom_call" | custom-call | flops 4294967296 | bytes 28311552 | tf_op jit(solution)/shard_map/gate_side/pallas_call | solution.py:345
  61.7 2.6 broadcast_in_dim.25.cb_ref
  64.3 15.9 %adjoint_end.1 = bf16[32,2048]{1,0:T(8,128)(2,1)} custom-call(f32[16,512,128]{2,1,0:T(8,128)} %get-tuple-element.129.dl_ref, f32[16,512,128]{2,1,0:T(8,128)} %get-tuple-element.133.g_ref, f32[16,2048]{1,0:T(8,128)} %bitcast.148, f32[512,16,128]{2,1,0:T(8,128)} %broadcast_in_dim.25.cb_ref), custom_call_target="tpu_custom_call" | custom-call | flops 20000000000 | bytes 12845056 | tf_op jit(solution)/shard_map/adjoint_end/pallas_call | solution.py:345
  80.2 1.1 fusion.11.lc_ref
  81.4 1.8 fusion.20
  83.5 1.1 add_select_fusion.hin_ref
  84.6 31.0 %forward.1 = (bf16[8192,2048]{1,0:T(8,128)(2,1)}, bf16[512,2048]{1,0:T(8,128)(2,1)}, bf16[512,2048]{1,0:T(8,128)(2,1)}, f32[32,256]{1,0:T(8,128)}, f32[512,128]{1,0:T(8,128)}, /*index=5*/f32[8,2048]{1,0:T(8,128)}) custom-call(f32[16,512,128]{2,1,0:T(8,128)} %get-tuple-element.129.dl_ref, f32[16,512,128]{2,1,0:T(8,128)} %get-tuple-element.135.u_ref, ...), custom_call_target="tpu_custom_call" | custom-call | flops 30000001024 | bytes 66560000 | tf_op jit(solution)/shard_map/forward/pallas_call | solution.py:345
  115.6 10.4 %weight_grads.1 = bf16[32,128,1024]{2,1,0:T(8,128)(2,1)} custom-call(bf16[512,2048]{1,0:T(8,128)(2,1)} %get-tuple-element.162.gated_ref, bf16[512,2048]{1,0:T(8,128)(2,1)} %get-tuple-element.190.gate_ref, bf16[512,1024]{1,0:T(8,128)(2,1)} %bitcast.124, bf16[1024,512]{1,0:T(8,128)(2,1)} %get-tuple-element.145.turned_ref), custom_call_target="tpu_custom_call" | custom-call | flops 4294967296 | bytes 14680064 | tf_op jit(solution)/shard_map/weight_grads/pallas_call | solution.py:821
  127.2 1.1 fusion.12.lin_ref
  128.4 34.9 %backward.1 = (bf16[512,2048]{1,0:T(8,128)(2,1)}, f32[512,2048]{1,0:T(8,128)}, f32[32,256]{1,0:T(8,128)}, f32[16,2048]{1,0:T(8,128)}, f32[8,2048]{1,0:T(8,128)}) custom-call(f32[16,512,128]{2,1,0:T(8,128)} %get-tuple-element.129.dl_ref, f32[16,512,128]{2,1,0:T(8,128)} %get-tuple-element.135.u_ref, f32[16,512,128]{2,1,0:T(8,128)} %get-tuple-element.133.g_ref, ...), custom_call_target="tpu_custom_call" | custom-call | flops 49999998976 | bytes 60465152 | tf_op jit(solution)/shard_map/backward/pallas_call | solution.py:345
  163.3 2.4 convolution_convert_fusion.2
  166.4 0.9 concatenate.17.pg_ref
  167.3 11.8 %input_grads.2 = (bf16[16,128,256]{2,1,0:T(8,128)(2,1)}, bf16[16,128,256]{2,1,0:T(8,128)(2,1)}, bf16[512,1024]{1,0:T(8,128)(2,1)}, f32[16,1024]{1,0:T(8,128)}, f...) custom-call(s32[33]{0:T(128)} %pad_add_fusion.place_ref, f32[512,2048]{1,0:T(8,128)} %get-tuple-element.164.cp_ref, ...), custom_call_target="tpu_custom_call" | custom-call | flops 12884901888 | bytes 16777216 | tf_op jit(solution)/shard_map/input_grads/pallas_call | solution.py:769
  179.1 2.7 collective-permute-start.1
  181.8 5.5 %convert_add_fusion = bf16[512,1024]{1,0:T(8,128)(2,1)} fusion(bf16[512,1024]{1,0:T(8,128)(2,1)S(1)} %bitcast.122, bf16[512,2048]{1,0:T(8,128)(2,1)S(1)} %copy-done.32, bf16[2048,1024]{1,0:T(8,128)(2,1)} %ow_ref.1), kind=kOutput, calls=%fused_computation.4 | convolution fusion | flops 2149056512 | bytes 8388608 | tf_op jit(solution)/shard_map/dot_general | solution.py:1064
  187.4 1.2 add_convert_fusion.3
  188.5 3.7 %collective-permute-start.2 = (bf16[4,128,256]{2,1,0:T(8,128)(2,1)}, bf16[4,128,256]{2,1,0:T(8,128)(2,1)S(1)}, u32[]{:S(2)}, u32[]{:S(2)}) collective-permute-start(bf16[4,128,256]{2,1,0:T(8,128)(2,1)} %get-tuple-element.168), channel_id=1, source_target_pairs={{0,16},{4,20},{8,24},{12,28},{16,0},{20,4},{24,8},{28,12},{1,17},{... | collective-permute-start | bytes 786440 | tf_op jit(solution)/shard_map/ppermute | solution.py:936
  192.6 1.1 collective-permute-start.4
  193.7 11.5 %input_grads.3 = (bf16[16,192,256]{2,1,0:T(8,128)(2,1)}, bf16[16,192,256]{2,1,0:T(8,128)(2,1)}, bf16[512,1024]{1,0:T(8,128)(2,1)}, f32[16,1024]{1,0:T(8,128)}, f32[16,1024]{1,0:T(8,128)}) custom-call(s32[33]{0:T(128)} %pad_add_fusion.place_ref, f32[512,2048]{1,0:T(8,128)} %get-tuple-element.164.cp_ref, bf16[512,2048]{1,0:T(8,128)(2,1)} %get-tuple-element.149.inner_ref, ...), custom_call_target="tpu_custom_call" | custom-call | flops 12884901888 | bytes 16777216 | tf_op jit(solution)/shard_map/input_grads/pallas_call | solution.py:769
  205.2 1.0 pad_maximum_fusion
  206.6 6.3 %collective-permute-done.4 = bf16[4,128,256]{2,1,0:T(8,128)(2,1)S(1)} collective-permute-done((bf16[4,128,256]{2,1,0:T(8,128)(2,1)S(1)}, bf16[4,128,256]{2,1,0:T(8,128)(2,1)S(1)}, u32[]{:S(2)}, u32[]{:S(2)}) %collective-permute-start.4) | collective-permute-done | bytes 262176 | tf_op jit(solution)/shard_map/ppermute | solution.py:936
  213.2 1.5 collective-permute-start.9
  215.4 1.0 collective-permute-done.9
  216.7 1.9 add_convert_fusion
  218.6 2.3 collective-permute-start.6
  221.5 1.0 collective-permute-start.8
  222.5 4.6 %fusion = f32[512,1024]{1,0:T(8,128)S(1)} fusion(bf16[512,2048]{1,0:T(8,128)(2,1)S(1)} %copy-done.31, bf16[1024,4096]{1,0:T(8,128)(2,1)} %refs_9_.1), kind=kOutput, calls=%fused_computation | convolution fusion | flops 2147483648 | bytes 8388608 | tf_op jit(solution)/shard_map/dot_general | solution.py:40
  227.9 2.5 collective-permute-start.10
  230.4 1.5 collective-permute-start.11
  231.9 1.6 collective-permute-start.12
  233.5 6.6 %collective-permute-done.8 = bf16[4,192,256]{2,1,0:T(8,128)(2,1)S(1)} collective-permute-done((bf16[4,192,256]{2,1,0:T(8,128)(2,1)S(1)}, bf16[4,192,256]{2,1,0:T(8,128)(2,1)S(1)}, u32[]{:S(2)}, u32[]{:S(2)}) %collective-permute-start.8) | collective-permute-done | bytes 393248 | tf_op jit(solution)/shard_map/ppermute | solution.py:936
  240.1 0.9 add_convert_fusion.7
  241.0 2.4 collective-permute-start.13
  243.4 1.5 collective-permute-start.14
  245.5 1.4 scatter.6
  246.9 1.4 scatter.9
  248.3 3.3 %fusion.8 = f32[512,1024]{1,0:T(8,128)S(1)} fusion(bf16[512,1024]{1,0:T(8,128)(2,1)} %bitcast.162, bf16[1024,4096]{1,0:T(8,128)(2,1)} %refs_9_.1), kind=kOutput, calls=%fused_computation.12 | convolution fusion | flops 1073741824 | bytes 5242880 | tf_op jit(solution)/shard_map/dot_general | solution.py:40
  251.6 2.9 %fusion.6 = f32[512,1024]{1,0:T(8,128)S(1)} fusion(bf16[512,1024]{1,0:T(8,128)(2,1)S(1)} %bitcast.164, bf16[1024,4096]{1,0:T(8,128)(2,1)} %refs_9_.1), kind=kOutput, calls=%fused_computation.10 | convolution fusion | flops 1073741824 | bytes 5242880 | tf_op jit(solution)/shard_map/dot_general | solution.py:40
  255.8 1.6 fusion.4
  257.4 4.9 %collective-permute-done.15.refs_7_ = bf16[1,192,256]{2,1,0:T(8,128)(2,1)S(1)} collective-permute-done((bf16[1,192,256]{2,1,0:T(8,128)(2,1)S(1)}, bf16[1,192,256]{2,1,0:T(8,128)(2,1)S(1)}, u32[]{:S(2)}, u32[]{:S(2)}) %collective-permute-start.15) | collective-permute-done | bytes 98336 | tf_op jit(solution)/shard_map/ppermute | solution.py:936
  262.9 2.4 shares.1
  (129 shorter events, 9.7 us)
Async XLA Ops:
  7.2 74.2 %all-gather.5.cloned.1.call-start = ((), (), s32[]{:S(2)}) async-start(), calls=%async_computation.4 | async-start | bytes 1769472 | tf_op jit(solution)/shard_map/all_gather | solution.py:962
  8.0 3.3 %collective-permute-start = (bf16[2,8,1024]{2,1,0:T(8,128)(2,1)S(1)}, bf16[2,8,1024]{2,1,0:T(8,128)(2,1)S(1)}, u32[]{:S(2)}, u32[]{:S(2)}) collective-permute-start(bf16[2,8,1024]{2,1,0:T(8,128)(2,1)S(1)} %slice.404), channel_id=1, source_target_pairs={{0,4},{4,8},{8,12},{12,16},{16,20},{20,24},{24,28},{1,5},{5,9},{9,... | collective-permute-start | bytes 98312 | tf_op jit(solution)/shard_map/ppermute | solution.py:1005
  28.2 19.3 %copy-start.1 = (f32[512,128]{1,0:T(8,128)S(1)}, f32[512,128]{1,0:T(8,128)}, u32[]{:S(2)}) copy-start(f32[512,128]{1,0:T(8,128)} %get-tuple-element.127.proj_ref) | copy-start | bytes 786436
  28.2 19.3 %copy-start.4 = (bf16[512,1024]{1,0:T(8,128)(2,1)S(1)}, bf16[512,1024]{1,0:T(8,128)(2,1)}, u32[]{:S(2)}) copy-start(bf16[512,1024]{1,0:T(8,128)(2,1)} %constant.182.clone) | copy-start | bytes 3145732
  28.2 19.3 %copy-start.23 = (bf16[16,1024]{1,0:T(8,128)(2,1)S(1)}, bf16[16,1024]{1,0:T(8,128)(2,1)}, u32[]{:S(2)}) copy-start(bf16[16,1024]{1,0:T(8,128)(2,1)} %constant.181.clone) | copy-start | bytes 98308
  47.4 78.5 %all-gather.7.cloned.1.call-start = ((), (), s32[]{:S(2)}) async-start(), calls=%async_computation.5 | async-start | bytes 1179648 | tf_op jit(solution)/shard_map/all_gather | solution.py:962
  64.3 15.9 %copy-start.8 = (bf16[512,512]{1,0:T(8,128)(2,1)S(1)}, bf16[512,512]{1,0:T(8,128)(2,1)}, u32[]{:S(2)}) copy-start(bf16[512,512]{1,0:T(8,128)(2,1)} %constant.180.clone) | copy-start | bytes 1572868
  64.3 15.9 %copy-start.28 = (bf16[16,512]{1,0:T(8,128)(2,1)S(1)}, bf16[16,512]{1,0:T(8,128)(2,1)}, u32[]{:S(2)}) copy-start(bf16[16,512]{1,0:T(8,128)(2,1)} %constant.179.clone) | copy-start | bytes 49156
  81.3 131.6 %reduce-scatter.3.cloned.1.call-start = ((), (), s32[]{:S(2)}) async-start(), calls=%async_computation.2 | async-start | bytes 9437184 | tf_op jit(solution)/shard_map/reduce_scatter | solution.py:1033
  125.9 1.2 copy-start.7
  126.0 136.3 %reduce-scatter.5.cloned.1.call-start = ((), (), s32[]{:S(2)}) async-start(), calls=%async_computation.3 | async-start | bytes 1310720 | tf_op jit(solution)/shard_map/reduce_scatter | solution.py:1078
  128.4 34.9 %copy-start.9 = (bf16[64,2048]{1,0:T(8,128)(2,1)S(1)}, bf16[64,2048]{1,0:T(8,128)(2,1)}, u32[]{:S(2)}) copy-start(bf16[64,2048]{1,0:T(8,128)(2,1)} %rw_ref.1) | copy-start | bytes 786436
  163.3 2.6 copy-start.25
  163.3 2.7 copy-start.14
  167.3 14.5 %copy-start = (bf16[2,256,1024]{2,1,0:T(8,128)(2,1)S(1)}, bf16[2,256,1024]{2,1,0:T(8,128)(2,1)}, u32[]{:S(2)}) copy-start(bf16[2,256,1024]{2,1,0:T(8,128)(2,1)} %param.21) | copy-start | bytes 3145732
  167.3 14.5 %copy-start.32 = (bf16[512,2048]{1,0:T(8,128)(2,1)S(1)}, bf16[512,2048]{1,0:T(8,128)(2,1)}, u32[]{:S(2)}) copy-start(bf16[512,2048]{1,0:T(8,128)(2,1)} %get-tuple-element.162.gated_ref) | copy-start | bytes 6291460
  179.1 8.2 %copy-start.5 = (bf16[16,128,256]{2,1,0:T(8,128)(2,1)S(1)}, bf16[16,128,256]{2,1,0:T(8,128)(2,1)}, u32[]{:S(2)}) copy-start(bf16[16,128,256]{2,1,0:T(8,128)(2,1)} %get-tuple-element.159) | copy-start | bytes 3145732
  179.1 8.2 %collective-permute-start.1 = (bf16[16,128,256]{2,1,0:T(8,128)(2,1)}, bf16[16,128,256]{2,1,0:T(8,128)(2,1)S(1)}, u32[]{:S(2)}, u32[]{:S(2)}) collective-permute-start(bf16[16,128,256]{2,1,0:T(8,128)(2,1)} %get-tuple-element.161), channel_id=1, source_target_pairs={{0,4},{4,0},{8,12},{12,8},{16,20},{20,16},{24,28},{28,24},{1,5},{5... | collective-permute-start | bytes 3145736 | tf_op jit(solution)/shard_map/ppermute | solution.py:942
  188.5 17.6 %collective-permute-start.2 = (bf16[4,128,256]{2,1,0:T(8,128)(2,1)}, bf16[4,128,256]{2,1,0:T(8,128)(2,1)S(1)}, u32[]{:S(2)}, u32[]{:S(2)}) collective-permute-start(bf16[4,128,256]{2,1,0:T(8,128)(2,1)} %get-tuple-element.168), channel_id=1, source_target_pairs={{0,16},{4,20},{8,24},{12,28},{16,0},{20,4},{24,8},{28,12},{1,17},{... | collective-permute-start | bytes 786440 | tf_op jit(solution)/shard_map/ppermute | solution.py:936
  192.2 14.4 %collective-permute-start.3 = (bf16[4,128,256]{2,1,0:T(8,128)(2,1)S(1)}, bf16[4,128,256]{2,1,0:T(8,128)(2,1)S(1)}, u32[]{:S(2)}, u32[]{:S(2)}) collective-permute-start(bf16[4,128,256]{2,1,0:T(8,128)(2,1)S(1)} %get-tuple-element.169), channel_id=1, source_target_pairs={{0,8},{4,12},{8,0},{12,4},{16,24},{20,28},{24,16},{28,20},{1,9},{5... | collective-permute-start | bytes 786440 | tf_op jit(solution)/shard_map/ppermute | solution.py:936
  192.6 20.3 %collective-permute-start.4 = (bf16[4,128,256]{2,1,0:T(8,128)(2,1)S(1)}, bf16[4,128,256]{2,1,0:T(8,128)(2,1)S(1)}, u32[]{:S(2)}, u32[]{:S(2)}) collective-permute-start(bf16[4,128,256]{2,1,0:T(8,128)(2,1)S(1)} %get-tuple-element.170), channel_id=1, source_target_pairs={{0,24},{4,28},{8,16},{12,20},{16,8},{20,12},{24,0},{28,4},{1,25},{... | collective-permute-start | bytes 786440 | tf_op jit(solution)/shard_map/ppermute | solution.py:936
  193.7 11.5 %copy-start.18 = (f32[16,1024]{1,0:T(8,128)S(1)}, f32[16,1024]{1,0:T(8,128)}, u32[]{:S(2)}) copy-start(f32[16,1024]{1,0:T(8,128)} %get-tuple-element.172) | copy-start | bytes 196612
  205.2 11.5 %copy-start.3 = (bf16[16,192,256]{2,1,0:T(8,128)(2,1)S(1)}, bf16[16,192,256]{2,1,0:T(8,128)(2,1)}, u32[]{:S(2)}) copy-start(bf16[16,192,256]{2,1,0:T(8,128)(2,1)} %get-tuple-element.166) | copy-start | bytes 4718596
  206.6 11.9 %copy-start.10 = (bf16[4,128,256]{2,1,0:T(8,128)(2,1)}, bf16[4,128,256]{2,1,0:T(8,128)(2,1)S(1)}, u32[]{:S(2)}) copy-start(bf16[4,128,256]{2,1,0:T(8,128)(2,1)S(1)} %collective-permute-done.3) | copy-start | bytes 786436
  212.9 5.7 %copy-start.12 = (bf16[4,128,256]{2,1,0:T(8,128)(2,1)}, bf16[4,128,256]{2,1,0:T(8,128)(2,1)S(1)}, u32[]{:S(2)}) copy-start(bf16[4,128,256]{2,1,0:T(8,128)(2,1)S(1)} %collective-permute-done.4) | copy-start | bytes 786436
  212.9 3.8 %collective-permute-start.5 = (bf16[16,192,256]{2,1,0:T(8,128)(2,1)}, bf16[16,192,256]{2,1,0:T(8,128)(2,1)}, u32[]{:S(2)}, u32[]{:S(2)}) collective-permute-start(bf16[16,192,256]{2,1,0:T(8,128)(2,1)} %get-tuple-element.175), channel_id=1, source_target_pairs={{0,4},{4,0},{8,12},{12,8},{16,20},{20,16},{24,28},{28,24},{1,5},{5... | collective-permute-start | bytes 4718600 | tf_op jit(solution)/shard_map/ppermute | solution.py:942
  213.2 1.6 copy-start.26
  213.2 3.1 %collective-permute-start.9 = (bf16[2,3,2048]{2,1,0:T(4,128)(2,1)S(1)}, bf16[2,3,2048]{2,1,0:T(4,128)(2,1)S(1)}, u32[]{:S(2)}, u32[]{:S(2)}) collective-permute-start(bf16[2,3,2048]{2,1,0:T(4,128)(2,1)S(1)} %slice.559), channel_id=1, source_target_pairs={{4,0},{8,4},{12,8},{16,12},{20,16},{24,20},{28,24},{5,1},{9,5},{13... | collective-permute-start | bytes 73736 | tf_op jit(solution)/shard_map/ppermute | solution.py:1070
  216.7 5.8 %copy-start.31 = (bf16[512,2048]{1,0:T(8,128)(2,1)S(1)}, bf16[512,2048]{1,0:T(8,128)(2,1)}, u32[]{:S(2)}) copy-start(bf16[512,2048]{1,0:T(8,128)(2,1)} %get-tuple-element.190.gate_ref) | copy-start | bytes 6291460
  218.6 8.5 %copy-start.2 = (f32[4,128,256]{2,1,0:T(8,128)S(1)}, f32[4,128,256]{2,1,0:T(8,128)}, u32[]{:S(2)}) copy-start(f32[4,128,256]{2,1,0:T(8,128)} %get-tuple-element.199) | copy-start | bytes 1572868
  218.6 8.5 %copy-start.11 = (bf16[4,128,256]{2,1,0:T(8,128)(2,1)S(1)}, bf16[4,128,256]{2,1,0:T(8,128)(2,1)}, u32[]{:S(2)}) copy-start(bf16[4,128,256]{2,1,0:T(8,128)(2,1)} %copy-done.10) | copy-start | bytes 786436
  218.6 8.5 %copy-start.13 = (bf16[4,128,256]{2,1,0:T(8,128)(2,1)S(1)}, bf16[4,128,256]{2,1,0:T(8,128)(2,1)}, u32[]{:S(2)}) copy-start(bf16[4,128,256]{2,1,0:T(8,128)(2,1)} %copy-done.12) | copy-start | bytes 786436
  218.6 13.3 %collective-permute-start.6 = (bf16[4,192,256]{2,1,0:T(8,128)(2,1)S(1)}, bf16[4,192,256]{2,1,0:T(8,128)(2,1)S(1)}, u32[]{:S(2)}, u32[]{:S(2)}) collective-permute-start(bf16[4,192,256]{2,1,0:T(8,128)(2,1)S(1)} %get-tuple-element.181), channel_id=1, source_target_pairs={{0,16},{4,20},{8,24},{12,28},{16,0},{20,4},{24,8},{28,12},{1,17},{... | collective-permute-start | bytes 1179656 | tf_op jit(solution)/shard_map/ppermute | solution.py:936
  220.9 12.5 %collective-permute-start.7 = (bf16[4,192,256]{2,1,0:T(8,128)(2,1)S(1)}, bf16[4,192,256]{2,1,0:T(8,128)(2,1)S(1)}, u32[]{:S(2)}, u32[]{:S(2)}) collective-permute-start(bf16[4,192,256]{2,1,0:T(8,128)(2,1)S(1)} %get-tuple-element.182), channel_id=1, source_target_pairs={{0,8},{4,12},{8,0},{12,4},{16,24},{20,28},{24,16},{28,20},{1,9},{5... | collective-permute-start | bytes 1179656 | tf_op jit(solution)/shard_map/ppermute | solution.py:936
  221.5 18.6 %collective-permute-start.8 = (bf16[4,192,256]{2,1,0:T(8,128)(2,1)S(1)}, bf16[4,192,256]{2,1,0:T(8,128)(2,1)S(1)}, u32[]{:S(2)}, u32[]{:S(2)}) collective-permute-start(bf16[4,192,256]{2,1,0:T(8,128)(2,1)S(1)} %get-tuple-element.183), channel_id=1, source_target_pairs={{0,24},{4,28},{8,16},{12,20},{16,8},{20,12},{24,0},{28,4},{1,25},{... | collective-permute-start | bytes 1179656 | tf_op jit(solution)/shard_map/ppermute | solution.py:936
  227.1 17.7 %copy-start.19 = (f32[16,1024]{1,0:T(8,128)S(1)}, f32[16,1024]{1,0:T(8,128)}, u32[]{:S(2)}) copy-start(f32[16,1024]{1,0:T(8,128)} %get-tuple-element.195) | copy-start | bytes 196612
  227.1 17.7 %copy-start.20 = (f32[16,1024]{1,0:T(8,128)S(1)}, f32[16,1024]{1,0:T(8,128)}, u32[]{:S(2)}) copy-start(f32[16,1024]{1,0:T(8,128)} %get-tuple-element.196) | copy-start | bytes 196612
  227.9 27.3 %collective-permute-start.10 = (bf16[1,128,256]{2,1,0:T(8,128)(2,1)}, bf16[1,128,256]{2,1,0:T(8,128)(2,1)}, u32[]{:S(2)}, u32[]{:S(2)}) collective-permute-start(bf16[1,128,256]{2,1,0:T(8,128)(2,1)} %get-tuple-element.242), channel_id=1, source_target_pairs={{0,2},{1,3},{2,0},{3,1},{4,6},{5,7},{6,4},{7,5},{8,10},{9,11},{10,... | collective-permute-start | bytes 196616 | tf_op jit(solution)/shard_map/ppermute | solution.py:936
  230.4 27.0 %collective-permute-start.11 = (bf16[1,128,256]{2,1,0:T(8,128)(2,1)}, bf16[1,128,256]{2,1,0:T(8,128)(2,1)}, u32[]{:S(2)}, u32[]{:S(2)}) collective-permute-start(bf16[1,128,256]{2,1,0:T(8,128)(2,1)} %get-tuple-element.241), channel_id=1, source_target_pairs={{0,1},{1,0},{2,3},{3,2},{4,5},{5,4},{6,7},{7,6},{8,9},{9,8},{10,11... | collective-permute-start | bytes 196616 | tf_op jit(solution)/shard_map/ppermute | solution.py:936
  231.9 25.5 %collective-permute-start.12 = (bf16[1,128,256]{2,1,0:T(8,128)(2,1)}, bf16[1,128,256]{2,1,0:T(8,128)(2,1)}, u32[]{:S(2)}, u32[]{:S(2)}) collective-permute-start(bf16[1,128,256]{2,1,0:T(8,128)(2,1)} %get-tuple-element.240), channel_id=1, source_target_pairs={{0,3},{1,2},{2,1},{3,0},{4,7},{5,6},{6,5},{7,4},{8,11},{9,10},{10,... | collective-permute-start | bytes 196616 | tf_op jit(solution)/shard_map/ppermute | solution.py:936
  241.0 16.4 %collective-permute-start.13 = (bf16[1,192,256]{2,1,0:T(8,128)(2,1)}, bf16[1,192,256]{2,1,0:T(8,128)(2,1)S(1)}, u32[]{:S(2)}, u32[]{:S(2)}) collective-permute-start(bf16[1,192,256]{2,1,0:T(8,128)(2,1)} %get-tuple-element.204), channel_id=1, source_target_pairs={{0,2},{1,3},{2,0},{3,1},{4,6},{5,7},{6,4},{7,5},{8,10},{9,11},{10,... | collective-permute-start | bytes 294920 | tf_op jit(solution)/shard_map/ppermute | solution.py:936
  243.4 14.0 %collective-permute-start.14 = (bf16[1,192,256]{2,1,0:T(8,128)(2,1)S(1)}, bf16[1,192,256]{2,1,0:T(8,128)(2,1)S(1)}, u32[]{:S(2)}, u32[]{:S(2)}) collective-permute-start(bf16[1,192,256]{2,1,0:T(8,128)(2,1)S(1)} %get-tuple-element.205), channel_id=1, source_target_pairs={{0,1},{1,0},{2,3},{3,2},{4,5},{5,4},{6,7},{7,6},{8,9},{9,8},{10,11... | collective-permute-start | bytes 294920 | tf_op jit(solution)/shard_map/ppermute | solution.py:936
  248.3 3.3 %copy-start.30 = (bf16[2,256,1024]{2,1,0:T(8,128)(2,1)S(1)}, bf16[2,256,1024]{2,1,0:T(8,128)(2,1)}, u32[]{:S(2)}) copy-start(bf16[2,256,1024]{2,1,0:T(8,128)(2,1)} %scatter.9) | copy-start | bytes 3145732
  251.6 2.9 %copy-start.21 = (f32[1024]{0:T(1024)S(1)}, f32[1024]{0:T(1024)}, u32[]{:S(2)}) copy-start(f32[1024]{0:T(1024)} %param.23) | copy-start | bytes 12292
  254.5 1.2 copy-start.6
  255.2 7.1 %collective-permute-start.15 = (bf16[1,192,256]{2,1,0:T(8,128)(2,1)S(1)}, bf16[1,192,256]{2,1,0:T(8,128)(2,1)S(1)}, u32[]{:S(2)}, u32[]{:S(2)}) collective-permute-start(bf16[1,192,256]{2,1,0:T(8,128)(2,1)S(1)} %get-tuple-element.206), channel_id=1, source_target_pairs={{0,3},{1,2},{2,1},{3,0},{4,7},{5,6},{6,5},{7,4},{8,11},{9,10},{10,... | collective-permute-start | bytes 294920 | tf_op jit(solution)/shard_map/ppermute | solution.py:936
  257.4 4.9 %copy-start.15 = (bf16[1,192,256]{2,1,0:T(8,128)(2,1)}, bf16[1,192,256]{2,1,0:T(8,128)(2,1)S(1)}, u32[]{:S(2)}) copy-start(bf16[1,192,256]{2,1,0:T(8,128)(2,1)S(1)} %collective-permute-done.13.refs_5_) | copy-start | bytes 294916
  257.4 4.9 %copy-start.16 = (bf16[1,192,256]{2,1,0:T(8,128)(2,1)}, bf16[1,192,256]{2,1,0:T(8,128)(2,1)S(1)}, u32[]{:S(2)}) copy-start(bf16[1,192,256]{2,1,0:T(8,128)(2,1)S(1)} %collective-permute-done.14.refs_6_) | copy-start | bytes 294916
  (5 other events, 4.6 us)
Sparse Core Ops, SparseCore 0:
  47.5 30.2 all-gather.4
  81.4 28.3 all-gather.6
  126.1 82.0 reduce-scatter.2
  215.5 33.3 reduce-scatter.4

commit v5 on v4

--- a/solution.py
+++ b/solution.py
@@ -189,8 +189,8 @@
             mo = sc_all[s * T : (s + 1) * T] + (d * bc + skip) * x
             gu = gx * d
             gu_ref[at, :] += sum(gu[:, lane(l)] for l in range(NL))
-            gated_ref[at, :] = (mo * joined(ga_ref, at)).astype(bf16)
-            ggr_ref[at, :] = (mo * joined(gs_ref, at)).astype(bf16)
+            gated_ref[at, :] = (mo * joined(ga_ref, at).astype(f32)).astype(bf16)
+            ggr_ref[at, :] = (mo * joined(gs_ref, at).astype(f32)).astype(bf16)
             acc = acc + gx
         return acc
 
@@ -472,8 +472,8 @@
         g = gg * ga
         for l in range(NL):
             g_ref[l, at, :] = g[:, lane(l)]
-            ga_ref[l, at, :] = ga[:, lane(l)]
-            gs_ref[l, at, :] = gs[:, lane(l)]
+            ga_ref[l, at, :] = ga[:, lane(l)].astype(bf16)
+            gs_ref[l, at, :] = gs[:, lane(l)].astype(bf16)
         return 0
 
     lax.fori_loop(0, rows // ROWS, mix, 0)
@@ -484,6 +484,7 @@
     inner = out_weight.shape[0]
     first = inner // WIDTH
     tiles = jax.ShapeDtypeStruct((inner // 128, rows, 128), f32)
+    narrow = jax.ShapeDtypeStruct(tiles.shape, bf16)
     return kernel_call(
         gate_kernel, "gate_side", inner,
         (normed, cotangent, in_weight, out_weight),
@@ -492,7 +493,7 @@
             pl.BlockSpec((WIDTH, model), lambda j: (j, 0)),
         ],
         [pl.BlockSpec((model, rows), lambda j: (0, 0))] + [tiles_of(rows)] * 3,
-        (jax.ShapeDtypeStruct((model, rows), bf16), tiles, tiles, tiles),
+        (jax.ShapeDtypeStruct((model, rows), bf16), tiles, narrow, narrow),
         4 * rows * model * inner, scratch=[pltpu.VMEM((rows, WIDTH), f32)] * 2,
     )
 
@@ -543,7 +544,7 @@
                     pre = pre + cw_ref[k : k + 1, lane(l)] * ext_ref[s, l, pl.ds(r + PAD - taps + 1 + k, ROWS), :]
                 sg = sigmoid(pre)
                 x = (pre * sg).astype(bf16)
-                slope_ref[at, lane(l)] = sg * (1.0 + pre * (1.0 - sg))
+                slope_ref[at, lane(l)] = (sg * (1.0 + pre * (1.0 - sg))).astype(bf16)
                 x_ref[l, at, :] = x
                 flat_ref[at, lane(l)] = x
             return 0
@@ -581,7 +582,7 @@
         ],
         out_shape=(
             o((rows, model), bf16), o((rows, inner), bf16), o((halo.shape[0], inner), bf16), o((inner // 128, rows, 128), bf16),
-            o((rows, inner), f32), o((rows, 128), f32), o((rows, 128), f32),
+            o((rows, inner), bf16), o((rows, 128), f32), o((rows, 128), f32),
         ),
         scratch_shapes=[pltpu.VMEM((nseq, NL, PAD + length, 128), f32), pltpu.VMEM((rows, WIDTH), bf16)],
         compiler_params=pltpu.CompilerParams(vmem_limit_bytes=VMEM, dimension_semantics=("arbitrary",)),
@@ -613,7 +614,7 @@
         def first(i, total):
             r = pl.multiple_of(i * small_step, small_step)
             at = pl.ds(pl.multiple_of(s * length + r, small_step), small_step)
-            back = back_ref[at, :] * slope_ref[at, :]
+            back = back_ref[at, :] * slope_ref[at, :].astype(f32)
             for l in range(NL):
                 pre_ref[s, l, pl.ds(pl.multiple_of(r + PAD, PAD), small_step), :] = back[:, lane(l)]
             return total + sum(back[q * 8 : (q + 1) * 8] for q in range(small_step // 8))

time: 273 us -> 272 us (level)
  no operation moved by 1% of the time
where the time goes in v5:
time: 272 us; the launch traced here: 271 us
  Pallas kernels  161 us (59%)
  starting transfers between devices  25.8 us (9%)
  matrix products  21.2 us (8%)
  waiting for transfers between devices  20.1 us (7%)
  other arithmetic  14.9 us (5%)
  between operations  14.5 us (5%)
  local copies, waits for them, and re-layouts  13.9 us (5%)
    pallas_call x5, Pallas kernels, kernel_call(): pl.pallas_call(functools.partial(body, **options), grid=(channels // WIDT...  113 us
    pallas_call x2, Pallas kernels, input_grads(): pl.pallas_call(functools.partial(input_grad_kernel, nseq=nseq, length=len...  22.8 us
    ppermute x12, starting transfers between devices, round_trade(): held.append(lax.ppermute(parts[i], bits[0][0], flip_bit(bits[0][0], flip)))  18.8 us
    ppermute x12, waiting for transfers between devices, round_trade(): held.append(lax.ppermute(parts[i], bits[0][0], flip_bit(bits[0][0], flip)))  18.7 us
    dot_general x4, matrix products, rows_dot(): lax.dot_general(left, right, (((1,), (1,)), ((), ())), preferred_element_...  13.1 us
    pallas_call x1, Pallas kernels, inner_side(): pl.pallas_call(functools.partial(inner_kernel, nseq=nseq, length=length,...  12.2 us
    pallas_call x1, Pallas kernels, weight_grads(): pl.pallas_call(functools.partial(weight_grad_kernel, part=part), grid=(wi...  10.4 us
    dot_general x1, matrix products, shards(): jnp.dot(gated, out_weight, preferred_element_type=f32)  5.52 us
  transfers between devices with their start and end apart: 20, of which 6 were waited for; matrix products, arithmetic and copies ran while one was open for 16% of the time, Pallas kernels for 47%

profile of v5, /device:TPU:0, one launch (start us, length us, event | category | flops | bytes accessed | tf_op | source)
XLA Modules:
  0.0 271.0 jit_solution(1648623724512550579)
XLA Ops:
  8.0 2.3 collective-permute-start
  10.3 0.9 exponential_negate_fusion
  11.9 12.2 %inner_side.1 = (bf16[512,1024]{1,0:T(8,128)(2,1)}, bf16[512,2048]{1,0:T(8,128)(2,1)}, bf16[16,2048]{1,0:T(8,128)(2,1)}, bf16[16,512,128]{2,1,0:T(8,128)(2,1)}, ...) custom-call(bf16[512,1024]{1,0:T(8,128)(2,1)} %bitcast.121, bf16[16,1024]{1,0:T(8,128)(2,1)} %bitcast.155, ...), custom_call_target="tpu_custom_call" | custom-call | flops 2147483648 | bytes 14680064 | tf_op jit(solution)/shard_map/inner_side/pallas_call | solution.py:575
  24.1 1.2 fusion.51
  25.4 2.7 broadcast_in_dim.24.bb_ref
  28.1 19.3 %state_end.1 = (bf16[48,2048]{1,0:T(8,128)(2,1)}, f32[16,512,128]{2,1,0:T(8,128)}, f32[16,512,128]{2,1,0:T(8,128)}) custom-call(f32[512,128]{1,0:T(8,128)} %get-tuple-element.127.proj_ref, bf16[64,2048]{1,0:T(8,128)(2,1)} %rw_ref.1, f32[1,2048]{1,0:T(1,128)} %bitcast.165, bf16[16,512,128]{2,1,0:T(8,128)(2,1)} %get-tuple-element.128.x_ref, ...), custom_call_target="tpu_custom_call" | custom-call | flops 20000000000 | bytes 15540224 | tf_op jit(solution)/shard_map/state_end/pallas_call | solution.py:345
  47.5 1.5 fusion.10.lb_ref
  48.9 12.2 %gate_side.1 = (bf16[1024,512]{1,0:T(8,128)(2,1)}, f32[16,512,128]{2,1,0:T(8,128)}, bf16[16,512,128]{2,1,0:T(8,128)(2,1)}, bf16[16,512,128]{2,1,0:T(8,128)(2,1)}) custom-call(bf16[512,1024]{1,0:T(8,128)(2,1)} %get-tuple-element.130.normed_ref, bf16[512,1024]{1,0:T(8,128)(2,1)} %bitcast.123, bf16[1024,4096]{1,0:T(8,128)(2,1)} %refs_9_.1, ...), custom_call_target="tpu_custom_call" | custom-call | flops 4294967296 | bytes 24117248 | tf_op jit(solution)/shard_map/gate_side/pallas_call | solution.py:345
  61.1 2.7 broadcast_in_dim.25.cb_ref
  63.8 15.9 %adjoint_end.1 = bf16[32,2048]{1,0:T(8,128)(2,1)} custom-call(f32[16,512,128]{2,1,0:T(8,128)} %get-tuple-element.129.dl_ref, f32[16,512,128]{2,1,0:T(8,128)} %get-tuple-element.133.g_ref, f32[16,2048]{1,0:T(8,128)} %bitcast.148, f32[512,16,128]{2,1,0:T(8,128)} %broadcast_in_dim.25.cb_ref), custom_call_target="tpu_custom_call" | custom-call | flops 20000000000 | bytes 12845056 | tf_op jit(solution)/shard_map/adjoint_end/pallas_call | solution.py:345
  79.7 1.1 fusion.11.lc_ref
  80.9 1.8 fusion.20
  83.0 1.1 add_select_fusion.hin_ref
  84.1 30.6 %forward.1 = (bf16[8192,2048]{1,0:T(8,128)(2,1)}, bf16[512,2048]{1,0:T(8,128)(2,1)}, bf16[512,2048]{1,0:T(8,128)(2,1)}, f32[32,256]{1,0:T(8,128)}, f32[512,128]{1,0:T(8,128)}, /*index=5*/f32[8,2048]{1,0:T(8,128)}) custom-call(f32[16,512,128]{2,1,0:T(8,128)} %get-tuple-element.129.dl_ref, f32[16,512,128]{2,1,0:T(8,128)} %get-tuple-element.135.u_ref, ...), custom_call_target="tpu_custom_call" | custom-call | flops 30000001024 | bytes 62365696 | tf_op jit(solution)/shard_map/forward/pallas_call | solution.py:345
  114.7 10.4 %weight_grads.1 = bf16[32,128,1024]{2,1,0:T(8,128)(2,1)} custom-call(bf16[512,2048]{1,0:T(8,128)(2,1)} %get-tuple-element.162.gated_ref, bf16[512,2048]{1,0:T(8,128)(2,1)} %get-tuple-element.190.gate_ref, bf16[512,1024]{1,0:T(8,128)(2,1)} %bitcast.124, bf16[1024,512]{1,0:T(8,128)(2,1)} %get-tuple-element.145.turned_ref), custom_call_target="tpu_custom_call" | custom-call | flops 4294967296 | bytes 14680064 | tf_op jit(solution)/shard_map/weight_grads/pallas_call | solution.py:822
  126.4 1.1 fusion.12.lin_ref
  127.5 34.9 %backward.1 = (bf16[512,2048]{1,0:T(8,128)(2,1)}, f32[512,2048]{1,0:T(8,128)}, f32[32,256]{1,0:T(8,128)}, f32[16,2048]{1,0:T(8,128)}, f32[8,2048]{1,0:T(8,128)}) custom-call(f32[16,512,128]{2,1,0:T(8,128)} %get-tuple-element.129.dl_ref, f32[16,512,128]{2,1,0:T(8,128)} %get-tuple-element.135.u_ref, f32[16,512,128]{2,1,0:T(8,128)} %get-tuple-element.133.g_ref, ...), custom_call_target="tpu_custom_call" | custom-call | flops 49999998976 | bytes 60465152 | tf_op jit(solution)/shard_map/backward/pallas_call | solution.py:345
  162.4 2.4 convolution_convert_fusion.2
  165.5 1.0 concatenate.17.pg_ref
  166.5 11.5 %input_grads.2 = (bf16[16,128,256]{2,1,0:T(8,128)(2,1)}, bf16[16,128,256]{2,1,0:T(8,128)(2,1)}, bf16[512,1024]{1,0:T(8,128)(2,1)}, f32[16,1024]{1,0:T(8,128)}, f...) custom-call(s32[33]{0:T(128)} %pad_add_fusion.place_ref, f32[512,2048]{1,0:T(8,128)} %get-tuple-element.164.cp_ref, ...), custom_call_target="tpu_custom_call" | custom-call | flops 12884901888 | bytes 16777216 | tf_op jit(solution)/shard_map/input_grads/pallas_call | solution.py:770
  178.0 2.8 %collective-permute-start.1 = (bf16[16,128,256]{2,1,0:T(8,128)(2,1)}, bf16[16,128,256]{2,1,0:T(8,128)(2,1)S(1)}, u32[]{:S(2)}, u32[]{:S(2)}) collective-permute-start(bf16[16,128,256]{2,1,0:T(8,128)(2,1)} %get-tuple-element.161), channel_id=1, source_target_pairs={{0,4},{4,0},{8,12},{12,8},{16,20},{20,16},{24,28},{28,24},{1,5},{5... | collective-permute-start | bytes 3145736 | tf_op jit(solution)/shard_map/ppermute | solution.py:943
  180.8 5.5 %convert_add_fusion = bf16[512,1024]{1,0:T(8,128)(2,1)} fusion(bf16[512,1024]{1,0:T(8,128)(2,1)S(1)} %bitcast.122, bf16[512,2048]{1,0:T(8,128)(2,1)S(1)} %copy-done.32, bf16[2048,1024]{1,0:T(8,128)(2,1)} %ow_ref.1), kind=kOutput, calls=%fused_computation.4 | convolution fusion | flops 2149056512 | bytes 8388608 | tf_op jit(solution)/shard_map/dot_general | solution.py:1065
  186.4 1.2 add_convert_fusion.3
  187.6 3.5 %collective-permute-start.2 = (bf16[4,128,256]{2,1,0:T(8,128)(2,1)}, bf16[4,128,256]{2,1,0:T(8,128)(2,1)S(1)}, u32[]{:S(2)}, u32[]{:S(2)}) collective-permute-start(bf16[4,128,256]{2,1,0:T(8,128)(2,1)} %get-tuple-element.168), channel_id=1, source_target_pairs={{0,16},{4,20},{8,24},{12,28},{16,0},{20,4},{24,8},{28,12},{1,17},{... | collective-permute-start | bytes 786440 | tf_op jit(solution)/shard_map/ppermute | solution.py:937
  191.6 1.0 collective-permute-start.4
  192.5 11.3 %input_grads.3 = (bf16[16,192,256]{2,1,0:T(8,128)(2,1)}, bf16[16,192,256]{2,1,0:T(8,128)(2,1)}, bf16[512,1024]{1,0:T(8,128)(2,1)}, f32[16,1024]{1,0:T(8,128)}, f32[16,1024]{1,0:T(8,128)}) custom-call(s32[33]{0:T(128)} %pad_add_fusion.place_ref, f32[512,2048]{1,0:T(8,128)} %get-tuple-element.164.cp_ref, bf16[512,2048]{1,0:T(8,128)(2,1)} %get-tuple-element.149.inner_ref, ...), custom_call_target="tpu_custom_call" | custom-call | flops 12884901888 | bytes 16777216 | tf_op jit(solution)/shard_map/input_grads/pallas_call | solution.py:770
  203.8 1.0 pad_maximum_fusion
  204.8 0.9 collective-permute-done.3
  205.7 6.4 %collective-permute-done.4 = bf16[4,128,256]{2,1,0:T(8,128)(2,1)S(1)} collective-permute-done((bf16[4,128,256]{2,1,0:T(8,128)(2,1)S(1)}, bf16[4,128,256]{2,1,0:T(8,128)(2,1)S(1)}, u32[]{:S(2)}, u32[]{:S(2)}) %collective-permute-start.4) | collective-permute-done | bytes 262176 | tf_op jit(solution)/shard_map/ppermute | solution.py:937
  212.4 1.5 collective-permute-start.9
  214.5 1.0 collective-permute-done.9
  215.8 1.9 add_convert_fusion
  217.8 2.3 collective-permute-start.6
  220.7 1.0 collective-permute-start.8
  221.6 4.6 %fusion = f32[512,1024]{1,0:T(8,128)S(1)} fusion(bf16[512,2048]{1,0:T(8,128)(2,1)S(1)} %copy-done.31, bf16[1024,4096]{1,0:T(8,128)(2,1)} %refs_9_.1), kind=kOutput, calls=%fused_computation | convolution fusion | flops 2147483648 | bytes 8388608 | tf_op jit(solution)/shard_map/dot_general | solution.py:40
  227.1 2.5 collective-permute-start.10
  229.6 1.5 collective-permute-start.11
  231.1 1.6 collective-permute-start.12
  232.6 6.6 %collective-permute-done.8 = bf16[4,192,256]{2,1,0:T(8,128)(2,1)S(1)} collective-permute-done((bf16[4,192,256]{2,1,0:T(8,128)(2,1)S(1)}, bf16[4,192,256]{2,1,0:T(8,128)(2,1)S(1)}, u32[]{:S(2)}, u32[]{:S(2)}) %collective-permute-start.8) | collective-permute-done | bytes 393248 | tf_op jit(solution)/shard_map/ppermute | solution.py:937
  240.1 2.4 collective-permute-start.13
  242.5 1.5 collective-permute-start.14
  244.7 1.4 scatter.6
  246.1 1.4 scatter.9
  247.5 3.3 %fusion.8 = f32[512,1024]{1,0:T(8,128)S(1)} fusion(bf16[512,1024]{1,0:T(8,128)(2,1)} %bitcast.162, bf16[1024,4096]{1,0:T(8,128)(2,1)} %refs_9_.1), kind=kOutput, calls=%fused_computation.12 | convolution fusion | flops 1073741824 | bytes 5242880 | tf_op jit(solution)/shard_map/dot_general | solution.py:40
  250.8 2.9 %fusion.6 = f32[512,1024]{1,0:T(8,128)S(1)} fusion(bf16[512,1024]{1,0:T(8,128)(2,1)S(1)} %bitcast.164, bf16[1024,4096]{1,0:T(8,128)(2,1)} %refs_9_.1), kind=kOutput, calls=%fused_computation.10 | convolution fusion | flops 1073741824 | bytes 5242880 | tf_op jit(solution)/shard_map/dot_general | solution.py:40
  255.0 1.6 fusion.4
  256.6 4.8 %collective-permute-done.15.refs_7_ = bf16[1,192,256]{2,1,0:T(8,128)(2,1)S(1)} collective-permute-done((bf16[1,192,256]{2,1,0:T(8,128)(2,1)S(1)}, bf16[1,192,256]{2,1,0:T(8,128)(2,1)S(1)}, u32[]{:S(2)}, u32[]{:S(2)}) %collective-permute-start.15) | collective-permute-done | bytes 98336 | tf_op jit(solution)/shard_map/ppermute | solution.py:937
  262.1 2.4 shares.1
  (129 shorter events, 10.2 us)
Async XLA Ops:
  7.2 73.7 %all-gather.5.cloned.1.call-start = ((), (), s32[]{:S(2)}) async-start(), calls=%async_computation.4 | async-start | bytes 1769472 | tf_op jit(solution)/shard_map/all_gather | solution.py:963
  8.0 3.3 %collective-permute-start = (bf16[2,8,1024]{2,1,0:T(8,128)(2,1)S(1)}, bf16[2,8,1024]{2,1,0:T(8,128)(2,1)S(1)}, u32[]{:S(2)}, u32[]{:S(2)}) collective-permute-start(bf16[2,8,1024]{2,1,0:T(8,128)(2,1)S(1)} %slice.404), channel_id=1, source_target_pairs={{0,4},{4,8},{8,12},{12,16},{16,20},{20,24},{24,28},{1,5},{5,9},{9,... | collective-permute-start | bytes 98312 | tf_op jit(solution)/shard_map/ppermute | solution.py:1006
  28.1 19.4 %copy-start.1 = (f32[512,128]{1,0:T(8,128)S(1)}, f32[512,128]{1,0:T(8,128)}, u32[]{:S(2)}) copy-start(f32[512,128]{1,0:T(8,128)} %get-tuple-element.127.proj_ref) | copy-start | bytes 786436
  28.1 19.4 %copy-start.4 = (bf16[512,1024]{1,0:T(8,128)(2,1)S(1)}, bf16[512,1024]{1,0:T(8,128)(2,1)}, u32[]{:S(2)}) copy-start(bf16[512,1024]{1,0:T(8,128)(2,1)} %constant.182.clone) | copy-start | bytes 3145732
  28.1 19.4 %copy-start.23 = (bf16[16,1024]{1,0:T(8,128)(2,1)S(1)}, bf16[16,1024]{1,0:T(8,128)(2,1)}, u32[]{:S(2)}) copy-start(bf16[16,1024]{1,0:T(8,128)(2,1)} %constant.181.clone) | copy-start | bytes 98308
  47.4 77.7 %all-gather.7.cloned.1.call-start = ((), (), s32[]{:S(2)}) async-start(), calls=%async_computation.5 | async-start | bytes 1179648 | tf_op jit(solution)/shard_map/all_gather | solution.py:963
  63.8 15.9 %copy-start.8 = (bf16[512,512]{1,0:T(8,128)(2,1)S(1)}, bf16[512,512]{1,0:T(8,128)(2,1)}, u32[]{:S(2)}) copy-start(bf16[512,512]{1,0:T(8,128)(2,1)} %constant.180.clone) | copy-start | bytes 1572868
  63.8 15.9 %copy-start.28 = (bf16[16,512]{1,0:T(8,128)(2,1)S(1)}, bf16[16,512]{1,0:T(8,128)(2,1)}, u32[]{:S(2)}) copy-start(bf16[16,512]{1,0:T(8,128)(2,1)} %constant.179.clone) | copy-start | bytes 49156
  80.8 131.2 %reduce-scatter.3.cloned.1.call-start = ((), (), s32[]{:S(2)}) async-start(), calls=%async_computation.2 | async-start | bytes 9437184 | tf_op jit(solution)/shard_map/reduce_scatter | solution.py:1034
  125.1 1.2 copy-start.7
  125.1 136.3 %reduce-scatter.5.cloned.1.call-start = ((), (), s32[]{:S(2)}) async-start(), calls=%async_computation.3 | async-start | bytes 1310720 | tf_op jit(solution)/shard_map/reduce_scatter | solution.py:1079
  127.5 34.9 %copy-start.9 = (bf16[64,2048]{1,0:T(8,128)(2,1)S(1)}, bf16[64,2048]{1,0:T(8,128)(2,1)}, u32[]{:S(2)}) copy-start(bf16[64,2048]{1,0:T(8,128)(2,1)} %rw_ref.1) | copy-start | bytes 786436
  162.4 2.6 copy-start.25
  162.4 2.7 copy-start.14
  166.5 14.4 %copy-start = (bf16[2,256,1024]{2,1,0:T(8,128)(2,1)S(1)}, bf16[2,256,1024]{2,1,0:T(8,128)(2,1)}, u32[]{:S(2)}) copy-start(bf16[2,256,1024]{2,1,0:T(8,128)(2,1)} %param.21) | copy-start | bytes 3145732
  166.5 14.4 %copy-start.32 = (bf16[512,2048]{1,0:T(8,128)(2,1)S(1)}, bf16[512,2048]{1,0:T(8,128)(2,1)}, u32[]{:S(2)}) copy-start(bf16[512,2048]{1,0:T(8,128)(2,1)} %get-tuple-element.162.gated_ref) | copy-start | bytes 6291460
  178.0 8.3 %copy-start.5 = (bf16[16,128,256]{2,1,0:T(8,128)(2,1)S(1)}, bf16[16,128,256]{2,1,0:T(8,128)(2,1)}, u32[]{:S(2)}) copy-start(bf16[16,128,256]{2,1,0:T(8,128)(2,1)} %get-tuple-element.159) | copy-start | bytes 3145732
  178.0 8.3 %collective-permute-start.1 = (bf16[16,128,256]{2,1,0:T(8,128)(2,1)}, bf16[16,128,256]{2,1,0:T(8,128)(2,1)S(1)}, u32[]{:S(2)}, u32[]{:S(2)}) collective-permute-start(bf16[16,128,256]{2,1,0:T(8,128)(2,1)} %get-tuple-element.161), channel_id=1, source_target_pairs={{0,4},{4,0},{8,12},{12,8},{16,20},{20,16},{24,28},{28,24},{1,5},{5... | collective-permute-start | bytes 3145736 | tf_op jit(solution)/shard_map/ppermute | solution.py:943
  187.6 17.2 %collective-permute-start.2 = (bf16[4,128,256]{2,1,0:T(8,128)(2,1)}, bf16[4,128,256]{2,1,0:T(8,128)(2,1)S(1)}, u32[]{:S(2)}, u32[]{:S(2)}) collective-permute-start(bf16[4,128,256]{2,1,0:T(8,128)(2,1)} %get-tuple-element.168), channel_id=1, source_target_pairs={{0,16},{4,20},{8,24},{12,28},{16,0},{20,4},{24,8},{28,12},{1,17},{... | collective-permute-start | bytes 786440 | tf_op jit(solution)/shard_map/ppermute | solution.py:937
  191.1 14.6 %collective-permute-start.3 = (bf16[4,128,256]{2,1,0:T(8,128)(2,1)S(1)}, bf16[4,128,256]{2,1,0:T(8,128)(2,1)S(1)}, u32[]{:S(2)}, u32[]{:S(2)}) collective-permute-start(bf16[4,128,256]{2,1,0:T(8,128)(2,1)S(1)} %get-tuple-element.169), channel_id=1, source_target_pairs={{0,8},{4,12},{8,0},{12,4},{16,24},{20,28},{24,16},{28,20},{1,9},{5... | collective-permute-start | bytes 786440 | tf_op jit(solution)/shard_map/ppermute | solution.py:937
  191.6 20.5 %collective-permute-start.4 = (bf16[4,128,256]{2,1,0:T(8,128)(2,1)S(1)}, bf16[4,128,256]{2,1,0:T(8,128)(2,1)S(1)}, u32[]{:S(2)}, u32[]{:S(2)}) collective-permute-start(bf16[4,128,256]{2,1,0:T(8,128)(2,1)S(1)} %get-tuple-element.170), channel_id=1, source_target_pairs={{0,24},{4,28},{8,16},{12,20},{16,8},{20,12},{24,0},{28,4},{1,25},{... | collective-permute-start | bytes 786440 | tf_op jit(solution)/shard_map/ppermute | solution.py:937
  192.5 11.3 %copy-start.18 = (f32[16,1024]{1,0:T(8,128)S(1)}, f32[16,1024]{1,0:T(8,128)}, u32[]{:S(2)}) copy-start(f32[16,1024]{1,0:T(8,128)} %get-tuple-element.172) | copy-start | bytes 196612
  203.8 12.0 %copy-start.3 = (bf16[16,192,256]{2,1,0:T(8,128)(2,1)S(1)}, bf16[16,192,256]{2,1,0:T(8,128)(2,1)}, u32[]{:S(2)}) copy-start(bf16[16,192,256]{2,1,0:T(8,128)(2,1)} %get-tuple-element.166) | copy-start | bytes 4718596
  205.7 12.0 %copy-start.10 = (bf16[4,128,256]{2,1,0:T(8,128)(2,1)}, bf16[4,128,256]{2,1,0:T(8,128)(2,1)S(1)}, u32[]{:S(2)}) copy-start(bf16[4,128,256]{2,1,0:T(8,128)(2,1)S(1)} %collective-permute-done.3) | copy-start | bytes 786436
  212.1 5.7 %copy-start.12 = (bf16[4,128,256]{2,1,0:T(8,128)(2,1)}, bf16[4,128,256]{2,1,0:T(8,128)(2,1)S(1)}, u32[]{:S(2)}) copy-start(bf16[4,128,256]{2,1,0:T(8,128)(2,1)S(1)} %collective-permute-done.4) | copy-start | bytes 786436
  212.1 3.8 %collective-permute-start.5 = (bf16[16,192,256]{2,1,0:T(8,128)(2,1)}, bf16[16,192,256]{2,1,0:T(8,128)(2,1)}, u32[]{:S(2)}, u32[]{:S(2)}) collective-permute-start(bf16[16,192,256]{2,1,0:T(8,128)(2,1)} %get-tuple-element.175), channel_id=1, source_target_pairs={{0,4},{4,0},{8,12},{12,8},{16,20},{20,16},{24,28},{28,24},{1,5},{5... | collective-permute-start | bytes 4718600 | tf_op jit(solution)/shard_map/ppermute | solution.py:943
  212.4 1.6 copy-start.26
  212.4 3.1 %collective-permute-start.9 = (bf16[2,3,2048]{2,1,0:T(4,128)(2,1)S(1)}, bf16[2,3,2048]{2,1,0:T(4,128)(2,1)S(1)}, u32[]{:S(2)}, u32[]{:S(2)}) collective-permute-start(bf16[2,3,2048]{2,1,0:T(4,128)(2,1)S(1)} %slice.559), channel_id=1, source_target_pairs={{4,0},{8,4},{12,8},{16,12},{20,16},{24,20},{28,24},{5,1},{9,5},{13... | collective-permute-start | bytes 73736 | tf_op jit(solution)/shard_map/ppermute | solution.py:1071
  215.8 5.8 %copy-start.31 = (bf16[512,2048]{1,0:T(8,128)(2,1)S(1)}, bf16[512,2048]{1,0:T(8,128)(2,1)}, u32[]{:S(2)}) copy-start(bf16[512,2048]{1,0:T(8,128)(2,1)} %get-tuple-element.190.gate_ref) | copy-start | bytes 6291460
  217.8 8.5 %copy-start.2 = (f32[4,128,256]{2,1,0:T(8,128)S(1)}, f32[4,128,256]{2,1,0:T(8,128)}, u32[]{:S(2)}) copy-start(f32[4,128,256]{2,1,0:T(8,128)} %get-tuple-element.199) | copy-start | bytes 1572868
  217.8 8.5 %copy-start.11 = (bf16[4,128,256]{2,1,0:T(8,128)(2,1)S(1)}, bf16[4,128,256]{2,1,0:T(8,128)(2,1)}, u32[]{:S(2)}) copy-start(bf16[4,128,256]{2,1,0:T(8,128)(2,1)} %copy-done.10) | copy-start | bytes 786436
  217.8 8.5 %copy-start.13 = (bf16[4,128,256]{2,1,0:T(8,128)(2,1)S(1)}, bf16[4,128,256]{2,1,0:T(8,128)(2,1)}, u32[]{:S(2)}) copy-start(bf16[4,128,256]{2,1,0:T(8,128)(2,1)} %copy-done.12) | copy-start | bytes 786436
  217.8 13.3 %collective-permute-start.6 = (bf16[4,192,256]{2,1,0:T(8,128)(2,1)S(1)}, bf16[4,192,256]{2,1,0:T(8,128)(2,1)S(1)}, u32[]{:S(2)}, u32[]{:S(2)}) collective-permute-start(bf16[4,192,256]{2,1,0:T(8,128)(2,1)S(1)} %get-tuple-element.181), channel_id=1, source_target_pairs={{0,16},{4,20},{8,24},{12,28},{16,0},{20,4},{24,8},{28,12},{1,17},{... | collective-permute-start | bytes 1179656 | tf_op jit(solution)/shard_map/ppermute | solution.py:937
  220.1 12.5 %collective-permute-start.7 = (bf16[4,192,256]{2,1,0:T(8,128)(2,1)S(1)}, bf16[4,192,256]{2,1,0:T(8,128)(2,1)S(1)}, u32[]{:S(2)}, u32[]{:S(2)}) collective-permute-start(bf16[4,192,256]{2,1,0:T(8,128)(2,1)S(1)} %get-tuple-element.182), channel_id=1, source_target_pairs={{0,8},{4,12},{8,0},{12,4},{16,24},{20,28},{24,16},{28,20},{1,9},{5... | collective-permute-start | bytes 1179656 | tf_op jit(solution)/shard_map/ppermute | solution.py:937
  220.7 18.6 %collective-permute-start.8 = (bf16[4,192,256]{2,1,0:T(8,128)(2,1)S(1)}, bf16[4,192,256]{2,1,0:T(8,128)(2,1)S(1)}, u32[]{:S(2)}, u32[]{:S(2)}) collective-permute-start(bf16[4,192,256]{2,1,0:T(8,128)(2,1)S(1)} %get-tuple-element.183), channel_id=1, source_target_pairs={{0,24},{4,28},{8,16},{12,20},{16,8},{20,12},{24,0},{28,4},{1,25},{... | collective-permute-start | bytes 1179656 | tf_op jit(solution)/shard_map/ppermute | solution.py:937
  226.3 17.7 %copy-start.19 = (f32[16,1024]{1,0:T(8,128)S(1)}, f32[16,1024]{1,0:T(8,128)}, u32[]{:S(2)}) copy-start(f32[16,1024]{1,0:T(8,128)} %get-tuple-element.195) | copy-start | bytes 196612
  226.3 17.7 %copy-start.20 = (f32[16,1024]{1,0:T(8,128)S(1)}, f32[16,1024]{1,0:T(8,128)}, u32[]{:S(2)}) copy-start(f32[16,1024]{1,0:T(8,128)} %get-tuple-element.196) | copy-start | bytes 196612
  227.1 27.3 %collective-permute-start.10 = (bf16[1,128,256]{2,1,0:T(8,128)(2,1)}, bf16[1,128,256]{2,1,0:T(8,128)(2,1)}, u32[]{:S(2)}, u32[]{:S(2)}) collective-permute-start(bf16[1,128,256]{2,1,0:T(8,128)(2,1)} %get-tuple-element.242), channel_id=1, source_target_pairs={{0,2},{1,3},{2,0},{3,1},{4,6},{5,7},{6,4},{7,5},{8,10},{9,11},{10,... | collective-permute-start | bytes 196616 | tf_op jit(solution)/shard_map/ppermute | solution.py:937
  229.6 27.0 %collective-permute-start.11 = (bf16[1,128,256]{2,1,0:T(8,128)(2,1)}, bf16[1,128,256]{2,1,0:T(8,128)(2,1)}, u32[]{:S(2)}, u32[]{:S(2)}) collective-permute-start(bf16[1,128,256]{2,1,0:T(8,128)(2,1)} %get-tuple-element.241), channel_id=1, source_target_pairs={{0,1},{1,0},{2,3},{3,2},{4,5},{5,4},{6,7},{7,6},{8,9},{9,8},{10,11... | collective-permute-start | bytes 196616 | tf_op jit(solution)/shard_map/ppermute | solution.py:937
  231.1 25.5 %collective-permute-start.12 = (bf16[1,128,256]{2,1,0:T(8,128)(2,1)}, bf16[1,128,256]{2,1,0:T(8,128)(2,1)}, u32[]{:S(2)}, u32[]{:S(2)}) collective-permute-start(bf16[1,128,256]{2,1,0:T(8,128)(2,1)} %get-tuple-element.240), channel_id=1, source_target_pairs={{0,3},{1,2},{2,1},{3,0},{4,7},{5,6},{6,5},{7,4},{8,11},{9,10},{10,... | collective-permute-start | bytes 196616 | tf_op jit(solution)/shard_map/ppermute | solution.py:937
  240.1 16.4 %collective-permute-start.13 = (bf16[1,192,256]{2,1,0:T(8,128)(2,1)}, bf16[1,192,256]{2,1,0:T(8,128)(2,1)S(1)}, u32[]{:S(2)}, u32[]{:S(2)}) collective-permute-start(bf16[1,192,256]{2,1,0:T(8,128)(2,1)} %get-tuple-element.204), channel_id=1, source_target_pairs={{0,2},{1,3},{2,0},{3,1},{4,6},{5,7},{6,4},{7,5},{8,10},{9,11},{10,... | collective-permute-start | bytes 294920 | tf_op jit(solution)/shard_map/ppermute | solution.py:937
  242.5 14.1 %collective-permute-start.14 = (bf16[1,192,256]{2,1,0:T(8,128)(2,1)S(1)}, bf16[1,192,256]{2,1,0:T(8,128)(2,1)S(1)}, u32[]{:S(2)}, u32[]{:S(2)}) collective-permute-start(bf16[1,192,256]{2,1,0:T(8,128)(2,1)S(1)} %get-tuple-element.205), channel_id=1, source_target_pairs={{0,1},{1,0},{2,3},{3,2},{4,5},{5,4},{6,7},{7,6},{8,9},{9,8},{10,11... | collective-permute-start | bytes 294920 | tf_op jit(solution)/shard_map/ppermute | solution.py:937
  247.5 3.3 %copy-start.30 = (bf16[2,256,1024]{2,1,0:T(8,128)(2,1)S(1)}, bf16[2,256,1024]{2,1,0:T(8,128)(2,1)}, u32[]{:S(2)}) copy-start(bf16[2,256,1024]{2,1,0:T(8,128)(2,1)} %scatter.9) | copy-start | bytes 3145732
  250.8 2.9 %copy-start.21 = (f32[1024]{0:T(1024)S(1)}, f32[1024]{0:T(1024)}, u32[]{:S(2)}) copy-start(f32[1024]{0:T(1024)} %param.23) | copy-start | bytes 12292
  253.7 1.2 copy-start.6
  254.4 7.1 %collective-permute-start.15 = (bf16[1,192,256]{2,1,0:T(8,128)(2,1)S(1)}, bf16[1,192,256]{2,1,0:T(8,128)(2,1)S(1)}, u32[]{:S(2)}, u32[]{:S(2)}) collective-permute-start(bf16[1,192,256]{2,1,0:T(8,128)(2,1)S(1)} %get-tuple-element.206), channel_id=1, source_target_pairs={{0,3},{1,2},{2,1},{3,0},{4,7},{5,6},{6,5},{7,4},{8,11},{9,10},{10,... | collective-permute-start | bytes 294920 | tf_op jit(solution)/shard_map/ppermute | solution.py:937
  256.6 4.9 %copy-start.15 = (bf16[1,192,256]{2,1,0:T(8,128)(2,1)}, bf16[1,192,256]{2,1,0:T(8,128)(2,1)S(1)}, u32[]{:S(2)}) copy-start(bf16[1,192,256]{2,1,0:T(8,128)(2,1)S(1)} %collective-permute-done.13.refs_5_) | copy-start | bytes 294916
  256.6 4.9 %copy-start.16 = (bf16[1,192,256]{2,1,0:T(8,128)(2,1)}, bf16[1,192,256]{2,1,0:T(8,128)(2,1)S(1)}, u32[]{:S(2)}) copy-start(bf16[1,192,256]{2,1,0:T(8,128)(2,1)S(1)} %collective-permute-done.14.refs_6_) | copy-start | bytes 294916
  (5 other events, 4.6 us)
Sparse Core Ops, SparseCore 0:
  47.5 30.2 all-gather.4
  80.9 28.4 all-gather.6
  125.2 82.3 reduce-scatter.2
  214.7 33.3 reduce-scatter.4
